TPU v7x, 32 devices: a whole 2x2x4 slice. The times are simulated.
32 devices in a mesh: dp: 8 (over z, core), ctx: 4 (over y, x).
Axes of the slice: x: 2, y: 2, z: 4, core: 2. Of those that a mesh axis runs over, the one named last changes fastest.
Arguments:
- tokens: bfloat16 [8192, 2048], P(('dp', 'ctx')), may hold values from -6 to 6
- w_query: bfloat16 [2048, 2048], P(('dp', 'ctx')), may hold values from -0.125 to 0.125
- w_key: bfloat16 [2048, 2048], P(('dp', 'ctx')), may hold values from -0.125 to 0.125
- w_value: bfloat16 [2048, 2048], P(('dp', 'ctx')), may hold values from -0.125 to 0.125
- w_out: bfloat16 [2048, 2048], P(('dp', 'ctx')), may hold values from -0.125 to 0.125
- gain_query: bfloat16 [2048], P(('dp', 'ctx')), may hold values from 0.099609375 to 1.8984375
- gain_key: bfloat16 [2048], P(('dp', 'ctx')), may hold values from 0.099609375 to 1.8984375
- gain_attn: bfloat16 [2048], P(('dp', 'ctx')), may hold values from 0.099609375 to 1.8984375
- w_gate: bfloat16 [2048, 8192], P(('dp', 'ctx')), may hold values from -0.125 to 0.125
- w_up: bfloat16 [2048, 8192], P(('dp', 'ctx')), may hold values from -0.125 to 0.125
- w_down: bfloat16 [8192, 2048], P(('dp', 'ctx')), may hold values from -0.0625 to 0.0625
- gain_ffn: bfloat16 [2048], P(('dp', 'ctx')), may hold values from 0.099609375 to 1.8984375
- positions: int32 [8192], replicated, may hold values from 0 to 1023, as said below
- image_starts: int32 [8, 2], replicated, may hold values from 0 to 768, as said below
- cotangent: bfloat16 [8192, 2048], P(('dp', 'ctx')), may hold values from -6 to 6
Outputs:
- output: bfloat16 [8192, 2048], P(('dp', 'ctx'))
- grad_input: float32 [8192, 2048], P(('dp', 'ctx'))
- grad_w_query: float32 [2048, 2048], P(('dp', 'ctx'))
- grad_w_key: float32 [2048, 2048], P(('dp', 'ctx'))
- grad_w_value: float32 [2048, 2048], P(('dp', 'ctx'))
- grad_w_out: float32 [2048, 2048], P(('dp', 'ctx'))
- grad_gain_query: float32 [2048], P(('dp', 'ctx'))
- grad_gain_key: float32 [2048], P(('dp', 'ctx'))
- grad_gain_attn: float32 [2048], P(('dp', 'ctx'))
- grad_w_gate: float32 [2048, 8192], P(('dp', 'ctx'))
- grad_w_up: float32 [2048, 8192], P(('dp', 'ctx'))
- grad_w_down: float32 [8192, 2048], P(('dp', 'ctx'))
- grad_gain_ffn: float32 [2048], P(('dp', 'ctx'))
Inputs may be any that keep to these rules, and one draw needn't show every extreme that they name: Each sequence's 1024 rows hold every position once; consecutive groups of 256 rows hold two aligned blocks of 128 positions, block b and block 7 - b, in that order, each block within it in rising order; which b lands where is drawn per sequence. `image_starts`: piece j of a sequence lies inside the j-th of 2 equal parts of the sequence.
All inputs are finite; a program needn't handle non-finite values.
Results may differ from a plain program's by a relative error of at most 0.018.
Values may be sent and summed in bfloat16 or wider, within the bound.
A program may use at most 640 MiB of HBM per device.

v0:
```python
import math

import jax
import jax.numpy as jnp
from jax import lax
from jax.sharding import PartitionSpec as P

HD = 128
IMG = 256


EPS = 1e-06
THETA = 500000.0
NEG = -1e30


def norm_forward(tensor, gain_row):
    factor = lax.rsqrt(jnp.mean(tensor * tensor, axis=-1, keepdims=True) + EPS)
    normed = tensor * factor
    return (normed * gain_row, normed, factor)


def norm_backward(normed, factor, gain_row, incoming):
    weighted = incoming * gain_row
    inner_mean = jnp.mean(weighted * normed, axis=-1, keepdims=True)
    return (factor * (weighted - normed * inner_mean), jnp.sum(incoming * normed, axis=0))


def turning(token_places):
    half_width = HD // 2
    frequency = THETA ** (-(jnp.arange(half_width, dtype=jnp.float32) * 2.0) / HD)
    angles = token_places.astype(jnp.float32)[:, None] * frequency[None, :]
    return (jnp.cos(angles)[:, None, :], jnp.sin(angles)[:, None, :])


def rotate(tensor, cosine_table, sine_table, direction_sign):
    row_count = tensor.shape[0]
    grouped = tensor.reshape(row_count, -1, HD)
    leading = grouped[..., : HD // 2]
    trailing = grouped[..., HD // 2 :]
    turned = jnp.concatenate(
        [
            leading * cosine_table - direction_sign * trailing * sine_table,
            trailing * cosine_table + direction_sign * leading * sine_table,
        ],
        axis=-1,
    )
    return turned.reshape(row_count, -1)


def piece_label(token_places, starts_row):
    inside = (token_places[:, None] >= starts_row[None, :]) & (
        token_places[:, None] < starts_row[None, :] + IMG
    )
    labels = jnp.arange(1, starts_row.shape[0] + 1, dtype=jnp.int32)
    return jnp.sum(jnp.where(inside, labels[None, :], 0), axis=1) - 1


def visible(query_places, key_places, starts_row):
    query_label = piece_label(query_places, starts_row)
    key_label = piece_label(key_places, starts_row)
    causal = key_places[None, :] <= query_places[:, None]
    same_piece = (query_label[:, None] == key_label[None, :]) & (query_label[:, None] >= 0)
    return causal | same_piece


def contract_rows(left, right):
    return lax.dot_general(
        left, right, (((0,), (0,)), ((), ())), preferred_element_type=jnp.float32
    )


def contract_cols(left, right):
    return lax.dot_general(
        left, right, (((1,), (1,)), ((), ())), preferred_element_type=jnp.float32
    )


def group_scores(query_part, key_part, allowed, factor_scale):
    scores = (
        jnp.einsum("qhd,khd->hqk", query_part, key_part, preferred_element_type=jnp.float32)
        * factor_scale
    )
    return jnp.where(allowed[None], scores, NEG)


def attend(query_turned, keys_all, values_all, allowed, head_count, factor_scale):
    query_rows = query_turned.shape[0]
    seq_rows = keys_all.shape[0]
    group_heads = 2
    group_span = group_heads * HD

    def one_group(number, state_pair):
        out_acc, total_acc = state_pair
        offset = number * group_span
        query_part = lax.dynamic_slice_in_dim(query_turned, offset, group_span, 1).reshape(
            query_rows, group_heads, HD
        )
        key_part = lax.dynamic_slice_in_dim(keys_all, offset, group_span, 1).reshape(
            seq_rows, group_heads, HD
        )
        value_part = lax.dynamic_slice_in_dim(values_all, offset, group_span, 1).reshape(
            seq_rows, group_heads, HD
        )
        scores = group_scores(query_part, key_part, allowed, factor_scale)
        row_peak = jnp.max(scores, axis=-1, keepdims=True)
        exponent = jnp.exp(scores - row_peak)
        row_total = jnp.sum(exponent, axis=-1, keepdims=True)
        softmax_weights = exponent / row_total
        head_mix = jnp.einsum(
            "hqk,khd->qhd",
            softmax_weights.astype(jnp.bfloat16),
            value_part,
            preferred_element_type=jnp.float32,
        ).reshape(query_rows, group_span)
        out_acc = lax.dynamic_update_slice_in_dim(out_acc, head_mix, offset, 1)
        log_total = (row_peak + jnp.log(row_total))[..., 0]
        total_acc = lax.dynamic_update_slice_in_dim(total_acc, log_total, number * group_heads, 0)
        return (out_acc, total_acc)

    start_pair = (
        jnp.zeros((query_rows, head_count * HD), jnp.float32),
        jnp.zeros((head_count, query_rows), jnp.float32),
    )
    return lax.fori_loop(0, head_count // group_heads, one_group, start_pair)


def attend_back(
    query_turned, keys_all, values_all, grad_attended, log_totals, allowed, head_count, factor_scale
):
    query_rows = query_turned.shape[0]
    seq_rows = keys_all.shape[0]
    width = head_count * HD
    group_heads = 2
    group_span = group_heads * HD

    def one_group(number, state_triple):
        grad_query, grad_keys, grad_values = state_triple
        offset = number * group_span
        query_part = lax.dynamic_slice_in_dim(query_turned, offset, group_span, 1).reshape(
            query_rows, group_heads, HD
        )
        key_part = lax.dynamic_slice_in_dim(keys_all, offset, group_span, 1).reshape(
            seq_rows, group_heads, HD
        )
        value_part = lax.dynamic_slice_in_dim(values_all, offset, group_span, 1).reshape(
            seq_rows, group_heads, HD
        )
        grad_part = lax.dynamic_slice_in_dim(grad_attended, offset, group_span, 1).reshape(
            query_rows, group_heads, HD
        )
        log_part = lax.dynamic_slice_in_dim(log_totals, number * group_heads, group_heads, 0)
        scores = group_scores(query_part, key_part, allowed, factor_scale)
        softmax_weights = jnp.exp(scores - log_part[..., None])
        grad_weights = jnp.einsum(
            "qhd,khd->hqk", grad_part, value_part, preferred_element_type=jnp.float32
        )
        inner_sum = jnp.sum(softmax_weights * grad_weights, axis=-1, keepdims=True)
        grad_scores = (softmax_weights * (grad_weights - inner_sum)).astype(jnp.bfloat16)
        query_term = (
            jnp.einsum("hqk,khd->qhd", grad_scores, key_part, preferred_element_type=jnp.float32)
            * factor_scale
        )
        key_term = (
            jnp.einsum("hqk,qhd->khd", grad_scores, query_part, preferred_element_type=jnp.float32)
            * factor_scale
        )
        value_term = jnp.einsum(
            "hqk,qhd->khd",
            softmax_weights.astype(jnp.bfloat16),
            grad_part,
            preferred_element_type=jnp.float32,
        )
        grad_query = lax.dynamic_update_slice_in_dim(
            grad_query, query_term.reshape(query_rows, group_span), offset, 1
        )
        grad_keys = lax.dynamic_update_slice_in_dim(
            grad_keys, key_term.reshape(seq_rows, group_span), offset, 1
        )
        grad_values = lax.dynamic_update_slice_in_dim(
            grad_values, value_term.reshape(seq_rows, group_span), offset, 1
        )
        return (grad_query, grad_keys, grad_values)

    start_triple = (
        jnp.zeros((query_rows, width), jnp.float32),
        jnp.zeros((seq_rows, width), jnp.float32),
        jnp.zeros((seq_rows, width), jnp.float32),
    )
    return lax.fori_loop(0, head_count // group_heads, one_group, start_triple)


def local(
    tokens,
    w_query,
    w_key,
    w_value,
    w_out,
    gain_query,
    gain_key,
    gain_attn,
    w_gate,
    w_up,
    w_down,
    gain_ffn,
    positions,
    image_starts,
    cotangent,
):
    ctx_place = lax.axis_index("ctx")
    seq_number = lax.axis_index("dp")
    tok_rows = tokens.shape[0]
    width = tokens.shape[1]
    seq_len = tok_rows * lax.axis_size("ctx")
    head_count = width // HD
    factor_scale = 1.0 / math.sqrt(HD)
    seq_places = lax.dynamic_slice_in_dim(positions, seq_number * seq_len, seq_len)
    starts_row = lax.dynamic_slice_in_dim(image_starts, seq_number, 1, 0)[0]
    own_places = lax.dynamic_slice_in_dim(seq_places, ctx_place * tok_rows, tok_rows)
    cosine_own, sine_own = turning(own_places)
    allowed = visible(own_places, seq_places, starts_row)
    attn_set = (
        lax.all_gather(w_query, ("dp", "ctx"), axis=0, tiled=True),
        lax.all_gather(w_key, ("dp", "ctx"), axis=0, tiled=True),
        lax.all_gather(w_value, ("dp", "ctx"), axis=0, tiled=True),
        lax.all_gather(w_out, ("dp", "ctx"), axis=0, tiled=True),
        lax.all_gather(gain_query, ("dp", "ctx"), axis=0, tiled=True),
        lax.all_gather(gain_key, ("dp", "ctx"), axis=0, tiled=True),
        lax.all_gather(gain_attn, ("dp", "ctx"), axis=0, tiled=True),
    )
    full_query, full_key, full_value, full_out, full_gain_query, full_gain_key, full_gain_attn = (
        attn_set
    )
    query_raw = jnp.dot(tokens, full_query, preferred_element_type=jnp.float32)
    key_raw = jnp.dot(tokens, full_key, preferred_element_type=jnp.float32)
    value_raw = jnp.dot(tokens, full_value, preferred_element_type=jnp.float32)
    query_normed, query_unit, query_factor = norm_forward(
        query_raw, full_gain_query.astype(jnp.float32)
    )
    key_normed, key_unit, key_factor = norm_forward(key_raw, full_gain_key.astype(jnp.float32))
    query_turned = rotate(query_normed, cosine_own, sine_own, 1.0).astype(jnp.bfloat16)
    key_turned = rotate(key_normed, cosine_own, sine_own, 1.0).astype(jnp.bfloat16)
    value_low = value_raw.astype(jnp.bfloat16)
    key_value_stack = jnp.stack([key_turned, value_low])
    whole_stack = lax.all_gather(key_value_stack, "ctx", axis=1, tiled=True)
    keys_all = whole_stack[0]
    values_all = whole_stack[1]
    attended, log_totals = attend(
        query_turned, keys_all, values_all, allowed, head_count, factor_scale
    )
    attended_low = attended.astype(jnp.bfloat16)
    attn_proj = jnp.dot(attended_low, full_out, preferred_element_type=jnp.float32)
    attn_normed, attn_unit, attn_factor = norm_forward(
        attn_proj, full_gain_attn.astype(jnp.float32)
    )
    hidden = tokens.astype(jnp.float32) + attn_normed
    hidden_low = hidden.astype(jnp.bfloat16)
    ffn_set = (
        lax.all_gather(w_gate, ("dp", "ctx"), axis=0, tiled=True),
        lax.all_gather(w_up, ("dp", "ctx"), axis=0, tiled=True),
        lax.all_gather(w_down, ("dp", "ctx"), axis=0, tiled=True),
        lax.all_gather(gain_ffn, ("dp", "ctx"), axis=0, tiled=True),
    )
    full_gate, full_up, full_down, full_gain_ffn = ffn_set
    gate_pre = jnp.dot(hidden_low, full_gate, preferred_element_type=jnp.float32)
    up_pre = jnp.dot(hidden_low, full_up, preferred_element_type=jnp.float32)
    sigmoid_gate = jax.nn.sigmoid(gate_pre)
    silu_gate = gate_pre * sigmoid_gate
    mixed_low = (silu_gate * up_pre).astype(jnp.bfloat16)
    ffn_proj = jnp.dot(mixed_low, full_down, preferred_element_type=jnp.float32)
    ffn_normed, ffn_unit, ffn_factor = norm_forward(ffn_proj, full_gain_ffn.astype(jnp.float32))
    output = (hidden + ffn_normed).astype(jnp.bfloat16)
    grad_out = cotangent.astype(jnp.float32)
    back_gate, back_up, back_down, back_gain_ffn = (
        lax.all_gather(w_gate, ("dp", "ctx"), axis=0, tiled=True),
        lax.all_gather(w_up, ("dp", "ctx"), axis=0, tiled=True),
        lax.all_gather(w_down, ("dp", "ctx"), axis=0, tiled=True),
        lax.all_gather(gain_ffn, ("dp", "ctx"), axis=0, tiled=True),
    )
    grad_ffn_proj, grad_gain_ffn_term = norm_backward(
        ffn_unit, ffn_factor, back_gain_ffn.astype(jnp.float32), grad_out
    )
    ffn_grad_low = grad_ffn_proj.astype(jnp.bfloat16)
    columns = mixed_low
    grad_w_down = lax.psum_scatter(
        contract_rows(columns, ffn_grad_low), ("dp", "ctx"), scatter_dimension=0, tiled=True
    )
    grad_mixed = contract_cols(ffn_grad_low, back_down)
    grad_gate_low = (
        grad_mixed * up_pre * sigmoid_gate * (1.0 + gate_pre * (1.0 - sigmoid_gate))
    ).astype(jnp.bfloat16)
    grad_up_low = (grad_mixed * silu_gate).astype(jnp.bfloat16)
    both_low = jnp.concatenate([grad_gate_low, grad_up_low], axis=1)
    columns = hidden_low
    gate_up = lax.psum_scatter(
        contract_rows(columns, both_low), ("dp", "ctx"), scatter_dimension=0, tiled=True
    )
    ffn_width = w_gate.shape[1]
    grad_w_gate = gate_up[:, :ffn_width]
    grad_w_up = gate_up[:, ffn_width:]
    grad_hidden = (
        grad_out + contract_cols(grad_gate_low, back_gate) + contract_cols(grad_up_low, back_up)
    )
    attn_back = (
        lax.all_gather(w_query, ("dp", "ctx"), axis=0, tiled=True),
        lax.all_gather(w_key, ("dp", "ctx"), axis=0, tiled=True),
        lax.all_gather(w_value, ("dp", "ctx"), axis=0, tiled=True),
        lax.all_gather(w_out, ("dp", "ctx"), axis=0, tiled=True),
        lax.all_gather(gain_query, ("dp", "ctx"), axis=0, tiled=True),
        lax.all_gather(gain_key, ("dp", "ctx"), axis=0, tiled=True),
        lax.all_gather(gain_attn, ("dp", "ctx"), axis=0, tiled=True),
    )
    back_query, back_key, back_value, back_out, back_gain_query, back_gain_key, back_gain_attn = (
        attn_back
    )
    grad_attn_proj, grad_gain_attn_term = norm_backward(
        attn_unit, attn_factor, back_gain_attn.astype(jnp.float32), grad_hidden
    )
    attn_grad_low = grad_attn_proj.astype(jnp.bfloat16)
    term_out = contract_rows(attended_low, attn_grad_low)
    grad_attended_low = contract_cols(attn_grad_low, back_out).astype(jnp.bfloat16)
    again_stack = lax.all_gather(key_value_stack, "ctx", axis=1, tiled=True)
    keys_back = again_stack[0]
    values_back = again_stack[1]
    grad_query_turned, grad_keys_part, grad_values_part = attend_back(
        query_turned,
        keys_back,
        values_back,
        grad_attended_low,
        log_totals,
        allowed,
        head_count,
        factor_scale,
    )
    grad_key_turned, grad_value_sum = (
        lax.psum_scatter(
            grad_keys_part.astype(jnp.bfloat16), "ctx", scatter_dimension=0, tiled=True
        ).astype(jnp.float32),
        lax.psum_scatter(
            grad_values_part.astype(jnp.bfloat16), "ctx", scatter_dimension=0, tiled=True
        ).astype(jnp.float32),
    )
    grad_query_normed = rotate(grad_query_turned, cosine_own, sine_own, -1.0)
    grad_key_normed = rotate(grad_key_turned, cosine_own, sine_own, -1.0)
    grad_query_raw, grad_gain_query_term = norm_backward(
        query_unit, query_factor, back_gain_query.astype(jnp.float32), grad_query_normed
    )
    grad_key_raw, grad_gain_key_term = norm_backward(
        key_unit, key_factor, back_gain_key.astype(jnp.float32), grad_key_normed
    )
    query_grad_low = grad_query_raw.astype(jnp.bfloat16)
    key_grad_low = grad_key_raw.astype(jnp.bfloat16)
    value_grad_low = grad_value_sum.astype(jnp.bfloat16)
    term_query = contract_rows(tokens, query_grad_low)
    term_key = contract_rows(tokens, key_grad_low)
    term_value = contract_rows(tokens, value_grad_low)
    grad_input = (
        grad_hidden
        + contract_cols(query_grad_low, back_query)
        + contract_cols(key_grad_low, back_key)
        + contract_cols(value_grad_low, back_value)
    )
    summed = (
        lax.psum_scatter(term_query, ("dp", "ctx"), scatter_dimension=0, tiled=True),
        lax.psum_scatter(term_key, ("dp", "ctx"), scatter_dimension=0, tiled=True),
        lax.psum_scatter(term_value, ("dp", "ctx"), scatter_dimension=0, tiled=True),
        lax.psum_scatter(term_out, ("dp", "ctx"), scatter_dimension=0, tiled=True),
        lax.psum_scatter(grad_gain_query_term, ("dp", "ctx"), scatter_dimension=0, tiled=True),
        lax.psum_scatter(grad_gain_key_term, ("dp", "ctx"), scatter_dimension=0, tiled=True),
        lax.psum_scatter(grad_gain_attn_term, ("dp", "ctx"), scatter_dimension=0, tiled=True),
        lax.psum_scatter(grad_gain_ffn_term, ("dp", "ctx"), scatter_dimension=0, tiled=True),
    )
    return (
        output,
        grad_input,
        summed[0],
        summed[1],
        summed[2],
        summed[3],
        summed[4],
        summed[5],
        summed[6],
        grad_w_gate,
        grad_w_up,
        grad_w_down,
        summed[7],
    )


def solution(mesh):
    return jax.shard_map(
        local,
        mesh=mesh,
        in_specs=(
            P(("dp", "ctx"), None),
            P(("dp", "ctx"), None),
            P(("dp", "ctx"), None),
            P(("dp", "ctx"), None),
            P(("dp", "ctx"), None),
            P(("dp", "ctx")),
            P(("dp", "ctx")),
            P(("dp", "ctx")),
            P(("dp", "ctx"), None),
            P(("dp", "ctx"), None),
            P(("dp", "ctx"), None),
            P(("dp", "ctx")),
            P(),
            P(),
            P(("dp", "ctx"), None),
        ),
        out_specs=(
            P(("dp", "ctx"), None),
            P(("dp", "ctx"), None),
            P(("dp", "ctx"), None),
            P(("dp", "ctx"), None),
            P(("dp", "ctx"), None),
            P(("dp", "ctx"), None),
            P(("dp", "ctx")),
            P(("dp", "ctx")),
            P(("dp", "ctx")),
            P(("dp", "ctx"), None),
            P(("dp", "ctx"), None),
            P(("dp", "ctx"), None),
            P(("dp", "ctx")),
        ),
        check_vma=False,
    )
```

profile of v0, /device:TPU:0, one launch (start us, length us, event | category | flops | bytes accessed | tf_op | source)
XLA Modules:
  0.0 6025.4 jit_solution(14290329911106608899)
XLA Ops:
  12.9 42.6 all-reduce.10
  57.5 33.8 all-gather.9.cloned.1.call-done
  91.3 6.1 multiply_reduce_fusion.8
  99.2 71.2 %all-gather.15.cloned.1.call-done = bf16[2048,2048]{1,0:T(8,128)(2,1)} async-done(((bf16[64,2048]{1,0:T(8,128)(2,1)}), bf16[2048,2048]{1,0:T(8,128)(2,1)}) %all-gather.15.cloned.1.call-update) | async-done | bytes 8388624 | tf_op jit(solution)/shard_map/all_gather | solution.py:223
  170.4 5.8 multiply_reduce_fusion.7
  181.8 67.7 %all-gather.11.cloned.1.call-done = bf16[2048,2048]{1,0:T(8,128)(2,1)} async-done(((bf16[64,2048]{1,0:T(8,128)(2,1)}), bf16[2048,2048]{1,0:T(8,128)(2,1)}) %all-gather.11.cloned.1.call-update) | async-done | bytes 8388624 | tf_op jit(solution)/shard_map/all_gather | solution.py:225
  249.4 5.7 fusion.18
  265.5 77.6 %all-gather.13.cloned.1.call-done = bf16[2,1024,2048]{2,1,0:T(8,128)(2,1)} async-done(((bf16[2,256,2048]{2,1,0:T(8,128)(2,1)}), bf16[2,1024,2048]{2,1,0:T(8,128)(2,1)}) %all-gather.13.cloned.1.call-update) | async-done | bytes 8388624 | tf_op jit(solution)/shard_map/all_gather | solution.py:245
  343.1 6.1 slice_bitcast_fusion
  349.1 6.4 copy.85
  355.6 6.4 copy.84
  362.0 31.2 while.34
  393.2 30.2 all-gather.17.cloned.1.call-done
  423.4 5.8 multiply_reduce_fusion.6
  430.9 188.6 %all-gather.19.cloned.1.call-done = bf16[2048,8192]{1,0:T(8,128)(2,1)} async-done(((bf16[64,8192]{1,0:T(8,128)(2,1)}), bf16[2048,8192]{1,0:T(8,128)(2,1)}) %all-gather.19.cloned.1.call-update) | async-done | bytes 33554448 | tf_op jit(solution)/shard_map/all_gather | solution.py:259
  619.5 17.8 fusion.41
  637.4 178.0 %all-gather.21.cloned.1.call-done = bf16[2048,8192]{1,0:T(8,128)(2,1)} async-done(((bf16[64,8192]{1,0:T(8,128)(2,1)}), bf16[2048,8192]{1,0:T(8,128)(2,1)}) %all-gather.21.cloned.1.call-update) | async-done | bytes 33554448 | tf_op jit(solution)/shard_map/all_gather | solution.py:260
  815.4 24.2 multiply_convert_fusion.3
  839.6 171.7 %all-gather.23.cloned.1.call-done = bf16[8192,2048]{1,0:T(8,128)(2,1)} async-done(((bf16[256,2048]{1,0:T(8,128)(2,1)}), bf16[8192,2048]{1,0:T(8,128)(2,1)}) %all-gather.23.cloned.1.call-update) | async-done | bytes 33554448 | tf_op jit(solution)/shard_map/all_gather | solution.py:261
  1011.3 16.4 multiply_reduce_fusion.5
  1029.1 22.5 multiply_convert_fusion.1
  1051.5 17.5 convert_add_fusion
  1069.1 19.3 multiply_reduce_fusion.1
  1088.4 4.1 multiply_convert_fusion.6
  1092.5 7.1 convolution_convert_fusion
  1104.7 68.0 %while.35 = (s32[]{:T(128)}, f32[256,2048]{0,1:T(8,128)S(1)}, bf16[1024,2048]{0,1:T(8,128)(2,1)}, bf16[1024,2048]{0,1:T(8,128)(2,1)}, bf16[1024,2048]{0,1:T(8,12...) while((s32[]{:T(128)}, f32[256,2048]{0,1:T(8,128)S(1)}, ...), condition=%wide.region_14.15_spmd.clone, body=%wide.region_12.14_spmd.clone.sunk | while | flops 677445120 | bytes 25186868 | solution.py:190
  1175.3 49.9 fusion.11
  1226.8 8.6 fusion.42
  1235.5 9.8 convolution_bitcast_fusion
  1245.3 17.9 copy.106
  1272.5 7.1 reduce-scatter.14.cloned.1.call-done
  1286.0 3.7 copy.111
  1289.8 4.9 multiply_subtract_fusion
  1300.0 8.1 convolution_bitcast_fusion.1
  1308.2 17.8 copy.104
  1332.3 8.8 convolution_bitcast_fusion.2
  1341.2 18.0 copy.102
  1361.1 26.9 fusion.37
  1388.8 41.4 all-reduce.9
  1432.5 6.7 convolution_add_fusion.3
  1439.2 6.8 convolution_add_fusion.2
  1449.7 1715.1 %all-reduce.13.cloned.1.call-done = f32[2048,16384]{1,0:T(8,128)} async-done(((f32[2048,16384]{1,0:T(8,128)}), f32[2048,16384]{1,0:T(8,128)}) %all-reduce.13.cloned.1.call-update) | async-done | bytes 134217744
  3164.8 4.9 fusion.34
  3169.7 354.8 %reduce-scatter.18.cloned.1.call-done = f32[64,2048]{1,0:T(8,128)} async-done(((f32[2048,2048]{1,0:T(8,128)}), f32[64,2048]{1,0:T(8,128)}) %reduce-scatter.18.cloned.1.call-update) | async-done | bytes 524304 | tf_op jit(solution)/shard_map/reduce_scatter | solution.py:367
  3524.5 361.9 %reduce-scatter.26.cloned.1.call-done = f32[64,2048]{1,0:T(8,128)} async-done(((f32[2048,2048]{1,0:T(8,128)}), f32[64,2048]{1,0:T(8,128)}) %reduce-scatter.26.cloned.1.call-update) | async-done | bytes 524304
  3886.5 361.8 %reduce-scatter.24.cloned.1.call-done = f32[64,2048]{1,0:T(8,128)} async-done(((f32[2048,2048]{1,0:T(8,128)}), f32[64,2048]{1,0:T(8,128)}) %reduce-scatter.24.cloned.1.call-update) | async-done | bytes 524304
  4248.2 361.8 %reduce-scatter.22.cloned.1.call-done = f32[64,2048]{1,0:T(8,128)} async-done(((f32[2048,2048]{1,0:T(8,128)}), f32[64,2048]{1,0:T(8,128)}) %reduce-scatter.22.cloned.1.call-update) | async-done | bytes 524304
  4610.0 1408.6 %reduce-scatter.20.cloned.1.call-done = f32[256,2048]{1,0:T(8,128)} async-done(((f32[8192,2048]{1,0:T(8,128)}), f32[256,2048]{1,0:T(8,128)}) %reduce-scatter.20.cloned.1.call-update) | async-done | bytes 2097168 | tf_op jit(solution)/shard_map/reduce_scatter | solution.py:285
  (377 shorter events, 171.2 us)
Async XLA Ops:
  7.2 84.2 %all-gather.9.cloned.1.call-start = ((), (), s32[]{:S(2)}) async-start(), calls=%async_computation.7 | async-start | bytes 8650752 | tf_op jit(solution)/shard_map/all_gather | solution.py:224
  7.9 162.5 %all-gather.15.cloned.1.call-start = ((), (), s32[]{:S(2)}) async-start(), calls=%async_computation.10 | async-start | bytes 8650752 | tf_op jit(solution)/shard_map/all_gather | solution.py:223
  8.7 240.8 %all-gather.11.cloned.1.call-start = ((), (), s32[]{:S(2)}) async-start(), calls=%async_computation.8 | async-start | bytes 8650752 | tf_op jit(solution)/shard_map/all_gather | solution.py:225
  9.4 333.7 %all-gather.13.cloned.1.call-start = ((), (), s32[]{:S(2)}) async-start(), calls=%async_computation.9 | async-start | bytes 10485760 | tf_op jit(solution)/shard_map/all_gather | solution.py:245
  55.5 42.0 copy-start.31
  55.5 120.7 %copy-start.29 = (f32[2048]{0:T(1024)}, f32[2048]{0:T(1024)S(1)}, u32[]{:S(2)}) copy-start(f32[2048]{0:T(1024)S(1)} %convert_element_type.111) | copy-start | bytes 24580
  57.5 120.7 %copy-start.25 = (f32[256,64]{1,0:T(8,128)}, f32[256,64]{1,0:T(8,128)S(1)}, u32[]{:S(2)}) copy-start(f32[256,64]{1,0:T(8,128)S(1)} %get-tuple-element.620) | copy-start | bytes 196612
  98.8 71.6 %copy-start = (bf16[256,2048]{1,0:T(8,128)(2,1)S(1)}, bf16[256,2048]{1,0:T(8,128)(2,1)}, u32[]{:S(2)}) copy-start(bf16[256,2048]{1,0:T(8,128)(2,1)} %param.19) | copy-start | bytes 3145732
  256.7 3.7 copy-start.45
  256.7 166.7 %all-gather.17.cloned.1.call-start = ((), (), s32[]{:S(2)}) async-start(), calls=%async_computation.11 | async-start | bytes 8650752 | tf_op jit(solution)/shard_map/all_gather | solution.py:226
  257.3 3.5 copy-start.20
  257.3 362.2 %all-gather.19.cloned.1.call-start = ((), (), s32[]{:S(2)}) async-start(), calls=%async_computation.12 | async-start | bytes 34603008 | tf_op jit(solution)/shard_map/all_gather | solution.py:259
  257.9 557.5 %all-gather.21.cloned.1.call-start = ((), (), s32[]{:S(2)}) async-start(), calls=%async_computation.13 | async-start | bytes 34603008 | tf_op jit(solution)/shard_map/all_gather | solution.py:260
  258.6 752.7 %all-gather.23.cloned.1.call-start = ((), (), s32[]{:S(2)}) async-start(), calls=%async_computation.14 | async-start | bytes 34603008 | tf_op jit(solution)/shard_map/all_gather | solution.py:261
  259.4 976.1 %reduce-scatter.16.cloned.1.call-start = ((), (), s32[]{:S(2)}) async-start(), calls=%async_computation.16 | async-start | bytes 5242880 | tf_op jit(solution)/shard_map/reduce_scatter | solution.py:339
  260.3 828.0 %copy-start.33 = (f32[2048]{0:T(1024)}, f32[2048]{0:T(1024)S(1)}, u32[]{:S(2)}) copy-start(f32[2048]{0:T(1024)S(1)} %convert_element_type.117) | copy-start | bytes 24580
  393.1 36.0 copy-start.9
  393.2 36.0 copy-start.13
  430.9 384.5 %copy-start.14 = (bf16[256,2048]{1,0:T(8,128)(2,1)}, bf16[256,2048]{1,0:T(8,128)(2,1)S(1)}, u32[]{:S(2)}) copy-start(bf16[256,2048]{1,0:T(8,128)(2,1)S(1)} %fusion.25) | copy-start | bytes 3145732
  1011.3 16.4 copy-start.16
  1027.7 60.7 %copy-start.5 = (f32[256,2048]{1,0:T(8,128)}, f32[256,2048]{1,0:T(8,128)S(1)}, u32[]{:S(2)}) copy-start(f32[256,2048]{1,0:T(8,128)S(1)} %get-tuple-element.630) | copy-start | bytes 6291460
  1027.7 60.7 %copy-start.36 = (f32[256]{0:T(256)}, f32[256]{0:T(256)S(1)}, u32[]{:S(2)}) copy-start(f32[256]{0:T(256)S(1)} %add_rsqrt_fusion) | copy-start | bytes 3076
  1029.1 22.5 copy-start.43
  1092.5 7.1 copy-start.23
  1174.1 105.5 %reduce-scatter.14.cloned.1.call-start = ((), (), s32[]{:S(2)}) async-start(), calls=%async_computation.15 | async-start | bytes 5242880 | tf_op jit(solution)/shard_map/reduce_scatter | solution.py:336
  1174.6 1990.1 %all-reduce.13.cloned.1.call-start = ((), (), s32[]{:S(2)}) async-start(), calls=%async_computation.22 | async-start | bytes 268435456
  1225.3 2299.2 %reduce-scatter.18.cloned.1.call-start = ((), (), s32[]{:S(2)}) async-start(), calls=%async_computation.17 | async-start | bytes 17301504 | tf_op jit(solution)/shard_map/reduce_scatter | solution.py:367
  1235.4 2651.1 %reduce-scatter.26.cloned.1.call-start = ((), (), s32[]{:S(2)}) async-start(), calls=%async_computation.21 | async-start | bytes 17301504
  1263.2 2985.1 %reduce-scatter.24.cloned.1.call-start = ((), (), s32[]{:S(2)}) async-start(), calls=%async_computation.20 | async-start | bytes 17301504
  1286.0 3.7 copy-start.26
  1286.0 3.7 copy-start.28
  1294.7 2.5 copy-start.4
  1294.7 2.5 copy-start.32
  1294.7 2.5 copy-start.41
  1326.0 1.6 copy-start.39
  1326.0 3284.0 %reduce-scatter.22.cloned.1.call-start = ((), (), s32[]{:S(2)}) async-start(), calls=%async_computation.19 | async-start | bytes 17301504
  1327.7 2.8 copy-start.7
  1359.1 1.7 copy-start.6
  1359.1 2.0 copy-start.17
  1359.1 2.0 copy-start.34
  1359.1 2.0 copy-start.37
  1359.1 2.0 copy-start.44
  1359.2 4659.5 %reduce-scatter.20.cloned.1.call-start = ((), (), s32[]{:S(2)}) async-start(), calls=%async_computation.18 | async-start | bytes 69206016 | tf_op jit(solution)/shard_map/reduce_scatter | solution.py:285
  1388.1 44.4 copy-start.22
  1432.5 6.7 copy-start.19
  1432.5 13.5 slice-start
  1439.2 6.8 copy-start.27
  1439.2 6.8 slice-start.1
  (16 other events, 20.4 us)
Sparse Core Ops, SparseCore 0:
  10.9 80.3 all-gather.8
  94.2 76.1 all-gather.14
  173.3 76.1 all-gather.10
  256.8 86.1 all-gather.12
  345.8 77.5 all-gather.16
  426.1 193.3 all-gather.18
  622.4 192.9 all-gather.20
  818.3 192.9 all-gather.22
  1172.9 50.8 reduce-scatter.15
  1226.9 52.6 reduce-scatter.13
  1286.0 1878.7 all-reduce.12
  3167.5 356.9 reduce-scatter.17
  3527.4 359.0 reduce-scatter.25
  3889.2 359.0 reduce-scatter.23
  4251.0 359.0 reduce-scatter.21
  4612.8 1405.8 reduce-scatter.19
where the time goes:
time: 6040 us; the launch traced here: 6030 us
  waiting for transfers between devices  5400 us (89%)
  matrix products  311 us (5%)
  local copies, waits for them, and re-layouts  176 us (3%)
  blocking collectives  84 us (1%)
    unnamed x20, waiting for transfers between devices  2810 us
    reduce_scatter x1, waiting for transfers between devices, local(): lax.psum_scatter(contract_rows(columns, ffn_grad_low), ('dp', 'ctx'), sca...  1410 us
    reduce_scatter x1, waiting for transfers between devices, local(): lax.psum_scatter(term_out, ('dp', 'ctx'), scatter_dimension=0, tiled=True)  355 us
    all_gather x1, waiting for transfers between devices, local(): lax.all_gather(w_gate, ('dp', 'ctx'), axis=0, tiled=True)  189 us
    all_gather x1, waiting for transfers between devices, local(): lax.all_gather(w_up, ('dp', 'ctx'), axis=0, tiled=True)  178 us
    all_gather x1, waiting for transfers between devices, local(): lax.all_gather(w_down, ('dp', 'ctx'), axis=0, tiled=True)  172 us
  transfers between devices with their start and end apart: 16, of which 15 were waited for; matrix products, arithmetic and copies ran while one was open for 6% of the time, Pallas kernels for 0%

commit v1 on v0

v1 whole, which is shorter than its diff:
```python
import functools
import math

import jax
import jax.numpy as jnp
from jax import lax
from jax.experimental import pallas as pl
from jax.experimental.pallas import tpu as pltpu
from jax.sharding import PartitionSpec as P

HD = 128
IMG = 256
EPS = 1e-06
THETA = 500000.0
NEG = -1e30
AXES = ("dp", "ctx")
F32 = jnp.float32
BF16 = jnp.bfloat16
SCALE = 1.0 / math.sqrt(HD)
LOG2E = math.log2(math.e)


def dot(left, right, left_dim, right_dim, kind=F32):
    return lax.dot_general(
        left, right, (((left_dim,), (right_dim,)), ((), ())), preferred_element_type=kind
    )


def probs_of(q, k, limit, places):
    scores = dot(q, k, 1, 1)
    scores = jnp.where(places <= limit, scores, NEG)
    peak = jnp.max(scores, axis=-1, keepdims=True)
    weights = jnp.exp2((scores - peak) * (SCALE * LOG2E))
    return weights * (1.0 / jnp.sum(weights, axis=-1, keepdims=True))


def attend_kernel(q_ref, k_ref, v_ref, limit_ref, place_ref, out_ref):
    probs = probs_of(q_ref[...], k_ref[...], limit_ref[...], place_ref[0])
    out_ref[...] = dot(probs.astype(BF16), v_ref[...], 1, 0).astype(BF16)


def attend_back_kernel(
    q_ref, k_ref, v_ref, g_ref, limit_ref, place_ref, dq_ref, dk_ref, dv_ref
):
    step = pl.program_id(2)

    @pl.when(step == 0)
    def _():
        dk_ref[...] = jnp.zeros_like(dk_ref)
        dv_ref[...] = jnp.zeros_like(dv_ref)

    q, k, v, g = q_ref[...], k_ref[...], v_ref[...], g_ref[...]
    probs = probs_of(q, k, limit_ref[...], place_ref[0])
    grad_probs = dot(g, v, 1, 1)
    inner = jnp.sum(probs * grad_probs, axis=-1, keepdims=True)
    grad_scores = (probs * (grad_probs - inner)).astype(BF16)
    dq_ref[...] = dot(grad_scores, k, 1, 0) * SCALE
    dk_ref[...] += dot(grad_scores, q, 0, 0) * SCALE
    dv_ref[...] += dot(probs.astype(BF16), g, 0, 0)


def attention_specs(seq_len, rows):
    steps = seq_len // rows
    query = pl.BlockSpec((rows, HD), lambda s, h, i: (s * steps + i, h))
    keys = pl.BlockSpec((seq_len, HD), lambda s, h, i: (s, h))
    limit = pl.BlockSpec((rows, 1), lambda s, h, i: (s * steps + i, 0))
    places = pl.BlockSpec((1, 1, seq_len), lambda s, h, i: (s, 0, 0))
    return query, keys, limit, places


def attend(q, k, v, limits, places, seq_len):
    rows = min(256, seq_len)
    total, width = q.shape
    query, keys, limit, place = attention_specs(seq_len, rows)
    return pl.pallas_call(
        attend_kernel,
        out_shape=jax.ShapeDtypeStruct((total, width), BF16),
        grid=(total // seq_len, width // HD, seq_len // rows),
        in_specs=[query, keys, keys, limit, place],
        out_specs=query,
        compiler_params=pltpu.CompilerParams(vmem_limit_bytes=48 * 2**20),
        cost_estimate=pl.CostEstimate(
            flops=4 * total * seq_len * width,
            bytes_accessed=8 * total * width,
            transcendentals=total * seq_len * (width // HD),
        ),
        name="attend",
    )(q, k, v, limits, places)


def attend_back(q, k, v, g, limits, places, seq_len):
    rows = min(256, seq_len)
    total, width = q.shape
    query, keys, limit, place = attention_specs(seq_len, rows)
    shape = jax.ShapeDtypeStruct((total, width), F32)
    return pl.pallas_call(
        attend_back_kernel,
        out_shape=(shape, shape, shape),
        grid=(total // seq_len, width // HD, seq_len // rows),
        in_specs=[query, keys, keys, query, limit, place],
        out_specs=(query, keys, keys),
        compiler_params=pltpu.CompilerParams(vmem_limit_bytes=48 * 2**20),
        cost_estimate=pl.CostEstimate(
            flops=10 * total * seq_len * width,
            bytes_accessed=20 * total * width,
            transcendentals=total * seq_len * (width // HD),
        ),
        name="attend_back",
    )(q, k, v, g, limits, places)


def rope_tables(places):
    half = HD // 2
    frequency = THETA ** (-(jnp.arange(half, dtype=F32) * 2.0) / HD)
    angles = places.astype(F32)[:, None] * frequency[None, :]
    return jnp.cos(angles)[:, None, :], jnp.sin(angles)[:, None, :]


def rotate(tensor, cosine, sine, sign):
    rows = tensor.shape[0]
    grouped = tensor.reshape(rows, -1, HD)
    low, high = grouped[..., : HD // 2], grouped[..., HD // 2 :]
    turned = jnp.concatenate(
        [low * cosine - sign * high * sine, high * cosine + sign * low * sine], axis=-1
    )
    return turned.reshape(rows, -1)


def row_norm(tensor):
    factor = lax.rsqrt(jnp.mean(tensor * tensor, axis=-1, keepdims=True) + EPS)
    return tensor * factor, factor


def row_norm_back(unit, factor, gain, incoming):
    weighted = incoming * gain
    inner = jnp.mean(weighted * unit, axis=-1, keepdims=True)
    return factor * (weighted - unit * inner), jnp.sum(incoming * unit, axis=0)


def layer(
    ctx_size,
    dp_size,
    tokens,
    w_query,
    w_key,
    w_value,
    w_out,
    gain_query,
    gain_key,
    gain_attn,
    w_gate,
    w_up,
    w_down,
    gain_ffn,
    positions,
    image_starts,
    cotangent,
):
    C, Z = ctx_size, dp_size // 2
    A = 2 * C
    N = Z * A
    ctx, dp = lax.axis_index("ctx"), lax.axis_index("dp")
    core, z = lax.rem(dp, 2), lax.div(dp, 2)
    plane_at = core * C + ctx
    own_at = dp * C + ctx
    rows, width = tokens.shape
    ffn_width = w_gate.shape[1]
    shard = w_query.shape[0]
    down_shard = w_down.shape[0]
    seq_len = rows * C
    slice_width = width // A
    ffn_slice = ffn_width // A
    bits = [1 << b for b in range(C.bit_length() - 1)]
    planes = [[zz * A + p for p in range(A)] for zz in range(Z)]

    def swap(x, bit):
        return lax.ppermute(x, AXES, [(i, i ^ bit) for i in range(N)])

    def swap_core(x):
        return swap(x, C)

    def ring(x):
        return lax.ppermute(x, AXES, [(i, (i + A) % N) for i in range(N)])

    def rows_of(x, at, count):
        return lax.dynamic_slice_in_dim(x, at, count, 0)

    def put(x, part, at):
        return lax.dynamic_update_slice_in_dim(x, part, at, 0)

    def gather_ctx(x):
        count = x.shape[0]
        half = count // 2
        whole = jnp.zeros((C * count,) + x.shape[1:], x.dtype)
        for number, order in enumerate((bits, bits[::-1])):
            pieces = [(0, x[number * half : (number + 1) * half])]
            for bit in order:
                pieces = pieces + [(mask ^ bit, swap(part, bit)) for mask, part in pieces]
            for mask, part in pieces:
                whole = put(whole, part, (ctx ^ mask) * count + number * half)
        return whole

    def gather_plane(x):
        own = gather_ctx(x)
        return own, swap_core(own)

    def scatter_ctx(x):
        count = x.shape[0] // C
        half = count // 2
        halves = []
        for number, order in enumerate((bits, bits[::-1])):
            held = {
                mask: rows_of(x, (ctx ^ mask) * count + number * half, half) for mask in range(C)
            }
            for bit in order[::-1]:
                arrived = {m ^ bit: swap(held[m].astype(BF16), bit) for m in held if m & bit}
                held = {m: held[m].astype(F32) + arrived[m].astype(F32) for m in arrived}
            halves.append(held[0])
        return jnp.concatenate(halves, axis=0)

    def scatter_plane(own, other):
        arrived = swap_core(other)
        return scatter_ctx((own.astype(F32) + arrived.astype(F32)).astype(BF16))

    def gather_z(x):
        count = x.shape[0]
        whole = jnp.zeros((Z * count,) + x.shape[1:], x.dtype)
        whole = put(whole, x, z * count)
        for step in range(1, Z):
            x = ring(x)
            whole = put(whole, x, lax.rem(z + Z - step, Z) * count)
        return whole

    def scatter_z(x):
        count = x.shape[0] // Z
        moving = rows_of(x, lax.rem(z + Z - 1, Z) * count, count)
        for step in range(1, Z):
            arrived = ring(moving.astype(BF16)).astype(F32)
            moving = arrived + rows_of(x, lax.rem(z + 2 * Z - 1 - step, Z) * count, count).astype(F32)
        return moving

    def exchange(x):
        return lax.all_to_all(x, AXES, 0, 0, tiled=True, axis_index_groups=planes)

    def sum_everywhere(x):
        for power in range(N.bit_length() - 1):
            x = x + swap(x, 1 << power)
        return x

    def sum_plane(own, other):
        stats = jnp.stack([own, other])
        for bit in bits:
            stats = stats + swap(stats, bit)
        stats = stats + swap_core(stats)[::-1]
        return stats[0], stats[1]

    def sorted_cores(own, other):
        return jnp.where(core == 0, jnp.stack([own, other]), jnp.stack([other, own]))

    qkv = jnp.stack(
        [w.reshape(shard, A, slice_width) for w in (w_query, w_key, w_value)], axis=1
    ).transpose(2, 0, 1, 3)
    qkv = exchange(qkv.reshape(A * shard, 3 * slice_width))
    full_qkv = gather_z(qkv)
    part = down_shard
    gate_up = jnp.stack([w.reshape(shard, Z, A, part) for w in (w_gate, w_up)], axis=1)
    gate_up = exchange(gate_up.transpose(3, 0, 1, 2, 4).reshape(A * shard, 2 * ffn_slice))

    gains = jnp.stack([gain_query, gain_key, gain_attn, gain_ffn]).astype(F32)
    all_gains = sum_everywhere(
        lax.dynamic_update_slice(jnp.zeros((4, width), F32), gains, (0, own_at * shard))
    )
    head_gains = lax.dynamic_slice(all_gains, (0, plane_at * slice_width), (2, slice_width))
    gain_q, gain_k = head_gains[0:1], head_gains[1:2]
    gain_a, gain_f = all_gains[2:3], all_gains[3:4]

    out_own, out_other = gather_plane(gather_z(w_out))
    full_out = (
        sorted_cores(out_own, out_other)
        .reshape(2, C, Z, shard, width)
        .transpose(2, 0, 1, 3, 4)
        .reshape(width, width)
    )
    full_gate_up = gather_z(gate_up)
    full_down = gather_z(w_down)

    x_own, x_other = gather_plane(tokens)
    x_all = jnp.concatenate([x_own, x_other], axis=0)
    other_dp = dp + 1 - 2 * core
    places = jnp.concatenate(
        [rows_of(positions, dp * seq_len, seq_len), rows_of(positions, other_dp * seq_len, seq_len)]
    )
    starts = jnp.concatenate([rows_of(image_starts, dp, 1), rows_of(image_starts, other_dp, 1)])
    start_rows = jnp.repeat(starts, seq_len, axis=0)
    inside = (places[:, None] >= start_rows) & (places[:, None] < start_rows + IMG)
    limits = jnp.max(jnp.where(inside, start_rows + (IMG - 1), places[:, None]), axis=1)
    limit_column = limits[:, None]
    place_rows = places.reshape(2, 1, seq_len)
    cosine, sine = rope_tables(places)

    def project(x):
        raw = dot(x, full_qkv, 1, 0)
        return raw, jnp.stack(
            [
                jnp.sum(jnp.square(raw[:, i * slice_width : (i + 1) * slice_width]), axis=1)
                for i in range(2)
            ]
        )

    raw_own, squares_own = project(x_own)
    raw_other, squares_other = project(x_other)
    squares_own, squares_other = sum_plane(squares_own, squares_other)
    raw = jnp.concatenate([raw_own, raw_other], axis=0)
    factors = lax.rsqrt(jnp.concatenate([squares_own, squares_other], axis=1) / width + EPS)
    factor_q, factor_k = factors[0][:, None], factors[1][:, None]
    unit_q = raw[:, :slice_width] * factor_q
    unit_k = raw[:, slice_width : 2 * slice_width] * factor_k
    value = raw[:, 2 * slice_width :].astype(BF16)
    query_turned = rotate(unit_q * gain_q, cosine, sine, 1.0).astype(BF16)
    key_turned = rotate(unit_k * gain_k, cosine, sine, 1.0).astype(BF16)
    attended = attend(query_turned, key_turned, value, limit_column, place_rows, seq_len)
    by_core = sorted_cores(attended[:seq_len], attended[seq_len:])
    attended_own = (
        exchange(by_core.reshape(A * rows, slice_width))
        .reshape(A, rows, slice_width)
        .transpose(1, 0, 2)
        .reshape(rows, width)
    )
    attn_proj = dot(attended_own, full_out, 1, 0)
    attn_unit, attn_factor = row_norm(attn_proj)
    hidden = tokens.astype(F32) + attn_unit * gain_a

    h_own, h_other = gather_plane(hidden.astype(BF16))
    h_all = jnp.concatenate([h_own, h_other], axis=0)

    def mix(h):
        pre = dot(h, full_gate_up, 1, 0)
        gate, up = pre[:, :ffn_slice], pre[:, ffn_slice:]
        return gate, up, (gate * jax.nn.sigmoid(gate) * up).astype(BF16)

    gate_other, up_other, mixed_other = mix(h_other)
    gate_own, up_own, mixed_own = mix(h_own)
    ffn_other = dot(mixed_other, full_down, 1, 0, BF16)
    ffn_own = dot(mixed_own, full_down, 1, 0, BF16)
    ffn_proj = scatter_plane(ffn_own, ffn_other)
    ffn_unit, ffn_factor = row_norm(ffn_proj)
    output = (hidden + ffn_unit * gain_f).astype(BF16)

    grad_out = cotangent.astype(F32)
    grad_ffn, term_gain_ffn = row_norm_back(ffn_unit, ffn_factor, gain_f, grad_out)
    f_own, f_other = gather_plane(grad_ffn.astype(BF16))
    f_all = jnp.concatenate([f_own, f_other], axis=0)
    mixed_all = jnp.concatenate([mixed_own, mixed_other], axis=0)
    grad_w_down = scatter_z(dot(mixed_all, f_all, 0, 0, BF16))

    def mix_back(f, gate, up):
        grad_mixed = dot(f, full_down, 1, 1)
        sig = jax.nn.sigmoid(gate)
        grad_gate = grad_mixed * up * sig * (1.0 + gate * (1.0 - sig))
        return jnp.concatenate([grad_gate.astype(BF16), (grad_mixed * (gate * sig)).astype(BF16)], axis=1)

    b_other = mix_back(f_other, gate_other, up_other)
    b_own = mix_back(f_own, gate_own, up_own)
    back_other = dot(b_other, full_gate_up, 1, 1, BF16)
    back_own = dot(b_own, full_gate_up, 1, 1, BF16)
    b_all = jnp.concatenate([b_own, b_other], axis=0)
    grad_gate_up = scatter_z(dot(h_all, b_all, 0, 0, BF16)).astype(BF16)
    grad_gate_up = (
        exchange(grad_gate_up)
        .reshape(A, shard, 2, Z, part)
        .transpose(2, 1, 3, 0, 4)
        .reshape(2, shard, ffn_width)
        .astype(F32)
    )
    grad_hidden = grad_out + scatter_plane(back_own, back_other)

    grad_attn, term_gain_attn = row_norm_back(attn_unit, attn_factor, gain_a, grad_hidden)
    grad_attn = grad_attn.astype(BF16)
    grad_attended = dot(grad_attn, full_out, 1, 1, BF16)
    grad_attended = exchange(
        grad_attended.reshape(rows, A, slice_width).transpose(1, 0, 2).reshape(A * rows, slice_width)
    ).reshape(2, seq_len, slice_width)
    grad_attended = jnp.where(core == 0, grad_attended, grad_attended[::-1]).reshape(
        2 * seq_len, slice_width
    )
    term_out = dot(attended_own, grad_attn, 0, 0, BF16)
    term_out = (
        term_out.reshape(Z, 2, C, shard, width)
        .transpose(1, 2, 0, 3, 4)
        .reshape(2, C * Z * shard, width)
    )
    term_out = jnp.where(core == 0, term_out, term_out[::-1])
    grad_w_out = scatter_z(scatter_plane(term_out[0], term_out[1]).astype(BF16))

    grad_q, grad_k, grad_v = attend_back(
        query_turned, key_turned, value, grad_attended, limit_column, place_rows, seq_len
    )
    grad_q = rotate(grad_q, cosine, sine, -1.0)
    grad_k = rotate(grad_k, cosine, sine, -1.0)
    term_gain_q = jnp.sum(grad_q * unit_q, axis=0)
    term_gain_k = jnp.sum(grad_k * unit_k, axis=0)
    weighted_q, weighted_k = grad_q * gain_q, grad_k * gain_k
    inner = jnp.stack([jnp.sum(weighted_q * unit_q, axis=1), jnp.sum(weighted_k * unit_k, axis=1)])
    inner_own, inner_other = sum_plane(inner[:, :seq_len], inner[:, seq_len:])
    inner = jnp.concatenate([inner_own, inner_other], axis=1) / width
    grad_raw = jnp.concatenate(
        [
            (factor_q * (weighted_q - unit_q * inner[0][:, None])).astype(BF16),
            (factor_k * (weighted_k - unit_k * inner[1][:, None])).astype(BF16),
            grad_v.astype(BF16),
        ],
        axis=1,
    )
    input_other = dot(grad_raw[seq_len:], full_qkv, 1, 1, BF16)
    input_own = dot(grad_raw[:seq_len], full_qkv, 1, 1, BF16)
    grad_input = grad_hidden + scatter_plane(input_own, input_other)
    grad_qkv = scatter_z(dot(x_all, grad_raw, 0, 0, BF16)).astype(BF16)
    grad_qkv = (
        exchange(grad_qkv)
        .reshape(A, shard, 3, slice_width)
        .transpose(2, 1, 0, 3)
        .reshape(3, shard, width)
        .astype(F32)
    )

    head_terms = lax.dynamic_update_slice(
        jnp.zeros((2, width), F32), jnp.stack([term_gain_q, term_gain_k]), (0, plane_at * slice_width)
    )
    gain_terms = jnp.concatenate([head_terms, term_gain_attn[None], term_gain_ffn[None]], axis=0)
    gain_sums = lax.dynamic_slice(sum_everywhere(gain_terms), (0, own_at * shard), (4, shard))

    return (
        output,
        grad_input,
        grad_qkv[0],
        grad_qkv[1],
        grad_qkv[2],
        grad_w_out,
        gain_sums[0],
        gain_sums[1],
        gain_sums[2],
        grad_gate_up[0],
        grad_gate_up[1],
        grad_w_down,
        gain_sums[3],
    )


def solution(mesh):
    split, line, copied = P(AXES, None), P(AXES), P()
    return jax.shard_map(
        functools.partial(layer, mesh.shape["ctx"], mesh.shape["dp"]),
        mesh=mesh,
        in_specs=(split,) * 5 + (line,) * 3 + (split,) * 3 + (line, copied, copied, split),
        out_specs=(split,) * 6 + (line,) * 3 + (split,) * 3 + (line,),
        check_vma=False,
    )
```

time: 6040 us -> 1090 us (0.18)
  waiting for transfers between devices: 5400 us -> 449 us
  matrix products: 311 us -> 170 us
  starting transfers between devices: 1.38 us -> 119 us
  other arithmetic: 42.2 us -> 146 us
  blocking collectives: 84 us -> 0 us
    unnamed x20 -> x0, waiting for transfers between devices: 2810 us -> none
    reduce_scatter x4 -> x0, waiting for transfers between devices: 1770 us -> none  [the longest x1 1410 us: local(): lax.psum_scatter(contract_rows(columns, ffn_grad_low), ('dp', 'ctx'), sca...]
    all_gather x8 -> x0, waiting for transfers between devices: 819 us -> none  [the longest x1 189 us: local(): lax.all_gather(w_gate, ('dp', 'ctx'), axis=0, tiled=True)]
    ppermute x0 -> x96, waiting for transfers between devices: none -> 446 us  [the longest x24 237 us: ring(): return lax.ppermute(x, AXES, [(i, (i + A) % N) for i in range(N)])]
    dot_general x76 -> x18, matrix products: 311 us -> 170 us  [dot(): lax.dot_general(left, right, (((left_dim,), (right_dim,)), ((), ())), pre...]
    ppermute x0 -> x96, starting transfers between devices: none -> 93.9 us  [the longest x72 74.4 us: swap(): return lax.ppermute(x, AXES, [(i, i ^ bit) for i in range(N)])]
    unnamed x2 -> x0, blocking collectives: 84 us -> none
    unnamed x119 -> x206, local copies, waits for them, and re-layouts: 101 us -> 25.1 us
  transfers between devices with their start and end apart: 16 -> 102, of which waited for: 15 -> 44; matrix products, arithmetic and copies ran while one was open for 6% -> 37% of each run, Pallas kernels for 0% -> 3%
where the time goes in v1:
time: 1090 us; the launch traced here: 1080 us
  waiting for transfers between devices  449 us (41%)
  matrix products  170 us (16%)
  local copies, waits for them, and re-layouts  162 us (15%)
  other arithmetic  146 us (13%)
  starting transfers between devices  119 us (11%)
  Pallas kernels  36.4 us (3%)
    ppermute x24, waiting for transfers between devices, ring(): return lax.ppermute(x, AXES, [(i, (i + A) % N) for i in range(N)])  237 us
    ppermute x72, waiting for transfers between devices, swap(): return lax.ppermute(x, AXES, [(i, i ^ bit) for i in range(N)])  209 us
    dot_general x18, matrix products, dot(): lax.dot_general(left, right, (((left_dim,), (right_dim,)), ((), ())), pre...  170 us
    ppermute x72, starting transfers between devices, swap(): return lax.ppermute(x, AXES, [(i, i ^ bit) for i in range(N)])  74.4 us
    dynamic_update_slice x44, local copies, waits for them, and re-layouts, put(): return lax.dynamic_update_slice_in_dim(x, part, at, 0)  46.3 us
    unnamed x206, local copies, waits for them, and re-layouts  25.1 us
    all_to_all x6, starting transfers between devices, exchange(): return lax.all_to_all(x, AXES, 0, 0, tiled=True, axis_index_groups=planes)  24.8 us
    pallas_call x1, Pallas kernels, attend_back(): pl.pallas_call(attend_back_kernel, out_shape=(shape, shape, shape), grid=...  22.7 us
  transfers between devices with their start and end apart: 102, of which 44 were waited for; matrix products, arithmetic and copies ran while one was open for 37% of the time, Pallas kernels for 3%

profile of v1, /device:TPU:0, one launch (start us, length us, event | category | flops | bytes accessed | tf_op | source)
XLA Modules:
  0.0 1084.4 jit_solution(18290077723688885990)
XLA Ops:
  23.0 5.5 broadcast_multiply_fusion.2
  34.9 6.9 collective-permute-done.14
  94.4 20.2 %collective-permute-done.21 = bf16[128,2048]{1,0:T(8,128)(2,1)S(1)} collective-permute-done((bf16[128,2048]{1,0:T(8,128)(2,1)S(1)}, bf16[128,2048]{1,0:T(8,128)(2,1)S(1)}, u32[]{:S(2)}, u32[]{:S(2)}) %collective-permute-start.21) | collective-permute-done | bytes 524320 | tf_op jit(solution)/shard_map/ppermute | solution.py:177
  117.7 8.1 collective-permute-done.24
  126.8 10.0 collective-permute-done.23
  140.0 18.6 %collective-permute-done.8 = bf16[512,768]{1,0:T(8,128)(2,1)S(1)} collective-permute-done((bf16[512,768]{1,0:T(8,128)(2,1)S(1)}, bf16[512,768]{1,0:T(8,128)(2,1)S(1)}, u32[]{:S(2)}, u32[]{:S(2)}) %collective-permute-start.8) | collective-permute-done | bytes 786464 | tf_op jit(solution)/shard_map/ppermute | solution.py:183
  194.5 10.9 %subtract_convert_fusion = (bf16[2048,2,64]{2,1,0:T(2,128)(2,1)S(1)}, bf16[2048,2,64]{2,1,0:T(2,128)(2,1)S(1)}, bf16[2048,2,64]{2,1,0:T(2,128)(2,1)S(1)}, bf16[2048,2,64]{2,1,0:T(2,128)(2,1)S(1)}) fusion(f32[2048,2,128]{2,1,0:T(2,128)} %reshape.247, f32[2048,64]{1,0:T(8,128)} %get-tuple-element.119, f32[2048,64]{1,0:T(8,128)S(1)} %get-tuple-element.120, ...), kind=kLoop, calls=%fused_computation.106 | loop fusion | flops 4194304 | bytes 7340032 | tf_op jit(solution)/shard_map/convert.8
  211.6 13.7 %attend.1 = bf16[2048,256]{1,0:T(8,128)(2,1)S(1)} custom-call(bf16[2048,256]{1,0:T(8,128)(2,1)S(1)} %bitcast.195, bf16[2048,256]{1,0:T(8,128)(2,1)S(1)} %bitcast.193, bf16[2048,256]{1,0:T(8,128)(2,1)S(1)} %fusion.45.v_ref, s32[2048,1]{1,0:T(8,128)S(1)} %bitcast.191, s32[2,1,1024]{2,1,0:T(1,128)S(1)} %pad_add_fusion.1.place_ref), custom_call_target="tpu_custom_call" | custom-call | flops 2147483648 | bytes 4194304 | tf_op jit(solution)/shard_map/attend/pallas_call | solution.py:75
  230.9 7.9 pad_maximum_fusion
  245.7 6.2 multiply_reduce_fusion.5
  260.1 11.1 %collective-permute-done.28 = bf16[128,2048]{1,0:T(8,128)(2,1)S(1)} collective-permute-done((bf16[128,2048]{1,0:T(8,128)(2,1)S(1)}, bf16[128,2048]{1,0:T(8,128)(2,1)S(1)}, u32[]{:S(2)}, u32[]{:S(2)}) %collective-permute-start.28) | collective-permute-done | bytes 524320 | tf_op jit(solution)/shard_map/ppermute | solution.py:177
  276.0 8.1 collective-permute-done.31
  286.0 8.2 collective-permute-done.30
  302.8 41.8 %collective-permute-done.35 = bf16[512,2048]{1,0:T(8,128)(2,1)} collective-permute-done((bf16[512,2048]{1,0:T(8,128)(2,1)}, bf16[512,2048]{1,0:T(8,128)(2,1)}, u32[]{:S(2)}, u32[]{:S(2)}) %collective-permute-start.35) | collective-permute-done | bytes 2097184 | tf_op jit(solution)/shard_map/ppermute | solution.py:183
  344.6 22.5 %collective-permute-done.38 = bf16[256,2048]{1,0:T(8,128)(2,1)} collective-permute-done((bf16[256,2048]{1,0:T(8,128)(2,1)S(1)}, bf16[256,2048]{1,0:T(8,128)(2,1)}, u32[]{:S(2)}, u32[]{:S(2)}) %collective-permute-start.38) | collective-permute-done | bytes 1048608 | tf_op jit(solution)/shard_map/ppermute | solution.py:183
  372.6 60.1 %collective-permute-done.39 = bf16[256,2048]{1,0:T(8,128)(2,1)} collective-permute-done((bf16[256,2048]{1,0:T(8,128)(2,1)}, bf16[256,2048]{1,0:T(8,128)(2,1)}, u32[]{:S(2)}, u32[]{:S(2)}) %collective-permute-start.39) | collective-permute-done | bytes 1048608 | tf_op jit(solution)/shard_map/ppermute | solution.py:183
  441.2 12.6 %fusion.96 = f32[1024,2048]{1,0:T(8,128)S(1)} fusion(bf16[1024,2048]{1,0:T(8,128)(2,1)} %collective-permute-done.40, bf16[2048,2048]{1,0:T(8,128)(2,1)S(1)} %constant_dynamic-update-slice_fusion.13), kind=kOutput, calls=%fused_computation.312 | convolution fusion | flops 8589934592 | bytes 20971520 | tf_op jit(solution)/shard_map/dot_general | solution.py:24
  457.1 6.0 fusion.97
  463.1 10.8 fusion.94
  477.2 5.1 fusion.95
  487.6 12.1 %collective-permute-done.43 = bf16[128,2048]{1,0:T(8,128)(2,1)S(1)} collective-permute-done((bf16[128,2048]{1,0:T(8,128)(2,1)S(1)}, bf16[128,2048]{1,0:T(8,128)(2,1)S(1)}, u32[]{:S(2)}, u32[]{:S(2)}) %collective-permute-start.43) | collective-permute-done | bytes 524320 | tf_op jit(solution)/shard_map/ppermute | solution.py:177
  501.9 8.6 collective-permute-done.42
  517.0 7.3 collective-permute-done.45
  534.3 8.1 collective-permute-done.48
  549.4 9.0 collective-permute-done.49
  559.2 5.9 collective-permute-done.50
  569.4 14.0 %multiply_convert_fusion.3 = (bf16[1024,1024]{1,0:T(8,128)(2,1)}, bf16[1024,1024]{1,0:T(8,128)(2,1)}) fusion(f32[1024,2048]{1,0:T(8,128)} %copy-done.36, bf16[1024,2048]{1,0:T(8,128)(2,1)} %constant_dynamic-update-slice_fusion.1, bf16[1024,2048]{1,0:T(8,128)(2,1)} %copy-done.48), kind=kOutput, calls=%fused_computation.53 | convolution fusion | flops 4308598784 | bytes 20971520 | tf_op jit(solution)/shard_map/dot_general | solution.py:24
  583.4 11.9 %fusion.15 = bf16[1024,2048]{1,0:T(8,128)(2,1)S(1)} fusion(bf16[1024,2048]{1,0:T(8,128)(2,1)} %collective-permute-done.54, bf16[1024,2048]{1,0:T(8,128)(2,1)} %constant_dynamic-update-slice_fusion.1, bf16[1024,1024]{1,0:T(8,128)(2,1)S(1)} %copy-done.55, bf16[1024,1024]{1,0:T(8,128)(2,1)S(1)} %copy-done.57), kind=kOutput, calls=%fused_computation.18 | convolution fusion | flops 8615100416 | bytes 16777216 | tf_op jit(solution)/shard_map/dot_general | solution.py:24
  596.4 14.8 %multiply_convert_fusion.1 = (bf16[1024,1024]{1,0:T(8,128)(2,1)S(1)}, bf16[1024,1024]{1,0:T(8,128)(2,1)}) fusion(f32[1024,2048]{1,0:T(8,128)} %copy-done.35, bf16[1024,2048]{1,0:T(8,128)(2,1)} %collective-permute-done.54, bf16[1024,2048]{1,0:T(8,128)(2,1)} %copy-done.48), kind=kOutput, calls=%fused_computation.51 | convolution fusion | flops 4308598784 | bytes 20971520 | tf_op jit(solution)/shard_map/dot_general | solution.py:24
  611.3 12.3 %fusion.24 = bf16[1024,2048]{1,0:T(8,128)(2,1)} fusion(bf16[2048,2048]{1,0:T(8,128)(2,1)S(1)} %bitcast.213, bf16[1024,1024]{1,0:T(8,128)(2,1)} %get-tuple-element.40, bf16[1024,1024]{1,0:T(8,128)(2,1)S(1)} %get-tuple-element.39), kind=kOutput, calls=%fused_computation.39 | convolution fusion | flops 8598323200 | bytes 16777216 | tf_op jit(solution)/shard_map/dot_general | solution.py:24
  624.2 25.0 %fusion.4 = bf16[2048,2048]{1,0:T(8,128)(2,1)} fusion(bf16[1024,2048]{1,0:T(8,128)(2,1)} %collective-permute-done.40, bf16[1024,2048]{1,0:T(8,128)(2,1)} %constant_dynamic-update-slice_fusion.17, bf16[1024,1024]{1,0:T(8,128)(2,1)} %get-tuple-element.40, bf16[1024,1024]{1,0:T(8,128)(2,1)} %copy-done.90, bf16[1024,1024]{1,0:T(8,128)(2,1)} %get-tuple-element.38, ...), kind=kOutput, calls=%fused_computation.7 | convolution fusion | flops 17230200832 | bytes 25165824 | tf_op jit(solution)/shard_map/dot_general | solution.py:24
  656.5 13.0 %fusion.20 = bf16[1024,2048]{1,0:T(8,128)(2,1)S(1)} fusion(bf16[2048,2048]{1,0:T(8,128)(2,1)} %copy-done.37, bf16[1024,1024]{1,0:T(8,128)(2,1)} %get-tuple-element.38, bf16[1024,1024]{1,0:T(8,128)(2,1)} %get-tuple-element.37), kind=kOutput, calls=%fused_computation.35 | convolution fusion | flops 8598323200 | bytes 16777216 | tf_op jit(solution)/shard_map/dot_general | solution.py:24
  669.5 33.5 %collective-permute-done.90 = bf16[512,2048]{1,0:T(8,128)(2,1)S(1)} collective-permute-done((bf16[512,2048]{1,0:T(8,128)(2,1)}, bf16[512,2048]{1,0:T(8,128)(2,1)S(1)}, u32[]{:S(2)}, u32[]{:S(2)}) %collective-permute-start.90) | collective-permute-done | bytes 2097184 | tf_op jit(solution)/shard_map/ppermute | solution.py:183
  706.6 18.9 %collective-permute-done.94 = bf16[256,2048]{1,0:T(8,128)(2,1)} collective-permute-done((bf16[256,2048]{1,0:T(8,128)(2,1)}, bf16[256,2048]{1,0:T(8,128)(2,1)}, u32[]{:S(2)}, u32[]{:S(2)}) %collective-permute-start.94) | collective-permute-done | bytes 1048608 | tf_op jit(solution)/shard_map/ppermute | solution.py:183
  738.9 11.7 %collective-permute-done.57 = bf16[128,2048]{1,0:T(8,128)(2,1)} collective-permute-done((bf16[128,2048]{1,0:T(8,128)(2,1)}, bf16[128,2048]{1,0:T(8,128)(2,1)}, u32[]{:S(2)}, u32[]{:S(2)}) %collective-permute-start.57) | collective-permute-done | bytes 524320 | tf_op jit(solution)/shard_map/ppermute | solution.py:177
  753.5 38.5 %collective-permute-done.95 = bf16[256,2048]{1,0:T(8,128)(2,1)} collective-permute-done((bf16[256,2048]{1,0:T(8,128)(2,1)}, bf16[256,2048]{1,0:T(8,128)(2,1)}, u32[]{:S(2)}, u32[]{:S(2)}) %collective-permute-start.95) | collective-permute-done | bytes 1048608 | tf_op jit(solution)/shard_map/ppermute | solution.py:183
  824.2 6.9 convolution_bitcast_fusion
  831.1 8.4 copy.116
  839.5 14.6 %reverse_select_fusion = bf16[2,1024,2048]{2,1,0:T(8,128)(2,1)} fusion(bf16[2,1024,2048]{2,1,0:T(8,128)(2,1)} %bitcast.203, pred[]{:T(512)S(6)} %eq.2), kind=kLoop, calls=%fused_computation | loop fusion | flops 4194304 | bytes 16777216 | tf_op jit(solution)/shard_map/jit(_where)/select_n | solution.py:392
  862.6 22.7 %attend_back.1 = (f32[2048,256]{1,0:T(8,128)}, f32[2048,256]{1,0:T(8,128)}, f32[2048,256]{1,0:T(8,128)}) custom-call(bf16[2048,256]{1,0:T(8,128)(2,1)S(1)} %bitcast.196, bf16[2048,256]{1,0:T(8,128)(2,1)S(1)} %bitcast.194, bf16[2048,256]{1,0:T(8,128)(2,1)S(1)} %fusion.45.v_ref, bf16[2048,256]{1,0:T(8,128)(2,1)S(1)} %bitcast.190, s32[2048,1]{1,0:T(8,128)S(1)} %bitcast.192, ...), custom_call_target="tpu_custom_call" | custom-call | flops 5368709120 | bytes 10485760 | tf_op jit(solution)/shard_map/attend_back/pallas_call | solution.py:96
  890.9 10.1 multiply_subtract_fusion.1
  920.3 5.4 fusion.47
  926.4 7.2 fusion
  945.0 8.0 fusion.49
  953.0 5.3 collective-permute-done.88
  975.6 6.8 copy.148
  1001.9 21.0 %collective-permute-done.81 = bf16[128,2048]{1,0:T(8,128)(2,1)S(1)} collective-permute-done((bf16[128,2048]{1,0:T(8,128)(2,1)S(1)}, bf16[128,2048]{1,0:T(8,128)(2,1)S(1)}, u32[]{:S(2)}, u32[]{:S(2)}) %collective-permute-start.81) | collective-permute-done | bytes 524320 | tf_op jit(solution)/shard_map/ppermute | solution.py:177
  1056.3 11.2 %collective-permute-done.68 = bf16[128,2048]{1,0:T(8,128)(2,1)} collective-permute-done((bf16[128,2048]{1,0:T(8,128)(2,1)}, bf16[128,2048]{1,0:T(8,128)(2,1)}, u32[]{:S(2)}, u32[]{:S(2)}) %collective-permute-start.68) | collective-permute-done | bytes 524320 | tf_op jit(solution)/shard_map/ppermute | solution.py:177
  (589 shorter events, 414.8 us)
Async XLA Ops:
  3.0 57.8 %collective-permute-start = (bf16[128,2048]{1,0:T(8,128)(2,1)}, bf16[128,2048]{1,0:T(8,128)(2,1)}, u32[]{:S(2)}, u32[]{:S(2)}) collective-permute-start(bf16[128,2048]{1,0:T(8,128)(2,1)} %get-tuple-element.101), channel_id=1, source_target_pairs={{0,1},{1,0},{2,3},{3,2},{4,5},{5,4},{6,7},{7,6},{8,9},{9,8},{10,11... | collective-permute-start | bytes 1572872 | tf_op jit(solution)/shard_map/ppermute | solution.py:177
  5.9 59.3 %collective-permute-start.1 = (bf16[128,2048]{1,0:T(8,128)(2,1)}, bf16[128,2048]{1,0:T(8,128)(2,1)}, u32[]{:S(2)}, u32[]{:S(2)}) collective-permute-start(bf16[128,2048]{1,0:T(8,128)(2,1)} %get-tuple-element.101), channel_id=1, source_target_pairs={{0,2},{1,3},{2,0},{3,1},{4,6},{5,7},{6,4},{7,5},{8,10},{9,11},{10,... | collective-permute-start | bytes 1572872 | tf_op jit(solution)/shard_map/ppermute | solution.py:177
  7.4 44.0 %collective-permute-start.18 = (bf16[64,2048]{1,0:T(8,128)(2,1)S(1)}, bf16[64,2048]{1,0:T(8,128)(2,1)}, u32[]{:S(2)}, u32[]{:S(2)}) collective-permute-start(bf16[64,2048]{1,0:T(8,128)(2,1)S(1)} %copy-done.66), channel_id=1, source_target_pairs={{0,8},{1,9},{2,10},{3,11},{4,12},{5,13},{6,14},{7,15},{8,16},{9,17... | collective-permute-start | bytes 786440 | tf_op jit(solution)/shard_map/ppermute | solution.py:183
  14.0 53.1 %all-to-all-start = ((bf16[8,64,768]{2,1,0:T(8,128)(2,1)}), bf16[8,64,768]{2,1,0:T(8,128)(2,1)}, u32[]{:S(2)}, u32[]{:S(2)}) async-start(bf16[8,64,768]{2,1,0:T(8,128)(2,1)} %all_to_all.36), calls=%async_computation | async-start | bytes 1572864 | tf_op jit(solution)/shard_map/all_to_all | solution.py:243
  18.3 42.9 %collective-permute-start.3 = (bf16[128,2048]{1,0:T(8,128)(2,1)}, bf16[128,2048]{1,0:T(8,128)(2,1)}, u32[]{:S(2)}, u32[]{:S(2)}) collective-permute-start(bf16[128,2048]{1,0:T(8,128)(2,1)} %get-tuple-element.99), channel_id=1, source_target_pairs={{0,2},{1,3},{2,0},{3,1},{4,6},{5,7},{6,4},{7,5},{8,10},{9,11},{10,... | collective-permute-start | bytes 1572872 | tf_op jit(solution)/shard_map/ppermute | solution.py:177
  60.7 24.1 %collective-permute-start.20 = (bf16[64,2048]{1,0:T(8,128)(2,1)S(1)}, bf16[64,2048]{1,0:T(8,128)(2,1)}, u32[]{:S(2)}, u32[]{:S(2)}) collective-permute-start(bf16[64,2048]{1,0:T(8,128)(2,1)S(1)} %collective-permute-done.19), channel_id=1, source_target_pairs={{0,8},{1,9},{2,10},{3,11},{4,12},{5,13},{6,14},{7,15},{8,16},{9,17... | collective-permute-start | bytes 786440 | tf_op jit(solution)/shard_map/ppermute | solution.py:183
  67.1 106.4 %all-to-all-start.2 = ((bf16[8,64,2048]{2,1,0:T(8,128)(2,1)}), bf16[8,64,2048]{2,1,0:T(8,128)(2,1)}, u32[]{:S(2)}, u32[]{:S(2)}) async-start(bf16[8,64,2048]{2,1,0:T(8,128)(2,1)} %all_to_all.40), calls=%async_computation.2 | async-start | bytes 4194304 | tf_op jit(solution)/shard_map/all_to_all | solution.py:243
  71.5 43.9 %collective-permute-start.6 = (bf16[512,768]{1,0:T(8,128)(2,1)}, bf16[512,768]{1,0:T(8,128)(2,1)S(1)}, u32[]{:S(2)}, u32[]{:S(2)}) collective-permute-start(bf16[512,768]{1,0:T(8,128)(2,1)} %bitcast.1), channel_id=1, source_target_pairs={{0,8},{1,9},{2,10},{3,11},{4,12},{5,13},{6,14},{7,15},{8,16},{9,17... | collective-permute-start | bytes 2359304 | tf_op jit(solution)/shard_map/ppermute | solution.py:183
  84.8 77.7 %collective-permute-start.9 = (bf16[1024,2048]{1,0:T(8,128)(2,1)}, bf16[1024,2048]{1,0:T(8,128)(2,1)S(1)}, u32[]{:S(2)}, u32[]{:S(2)}) collective-permute-start(bf16[1024,2048]{1,0:T(8,128)(2,1)} %constant_dynamic-update-slice_fusion.41), channel_id=1, source_target_pairs={{0,4},{1,5},{2,6},{3,7},{4,0},{5,1},{6,2},{7,3},{8,12},{9,13},{10,... | collective-permute-start | bytes 12582920 | tf_op jit(solution)/shard_map/ppermute | solution.py:177
  89.3 25.2 %collective-permute-start.21 = (bf16[128,2048]{1,0:T(8,128)(2,1)S(1)}, bf16[128,2048]{1,0:T(8,128)(2,1)S(1)}, u32[]{:S(2)}, u32[]{:S(2)}) collective-permute-start(bf16[128,2048]{1,0:T(8,128)(2,1)S(1)} %get-tuple-element.96), channel_id=1, source_target_pairs={{0,1},{1,0},{2,3},{3,2},{4,5},{5,4},{6,7},{7,6},{8,9},{9,8},{10,11... | collective-permute-start | bytes 1572872 | tf_op jit(solution)/shard_map/ppermute | solution.py:177
  90.8 25.8 %collective-permute-start.22 = (bf16[128,2048]{1,0:T(8,128)(2,1)S(1)}, bf16[128,2048]{1,0:T(8,128)(2,1)S(1)}, u32[]{:S(2)}, u32[]{:S(2)}) collective-permute-start(bf16[128,2048]{1,0:T(8,128)(2,1)S(1)} %get-tuple-element.96), channel_id=1, source_target_pairs={{0,2},{1,3},{2,0},{3,1},{4,6},{5,7},{6,4},{7,5},{8,10},{9,11},{10,... | collective-permute-start | bytes 1572872 | tf_op jit(solution)/shard_map/ppermute | solution.py:177
  91.2 34.7 %collective-permute-start.24 = (bf16[128,2048]{1,0:T(8,128)(2,1)S(1)}, bf16[128,2048]{1,0:T(8,128)(2,1)S(1)}, u32[]{:S(2)}, u32[]{:S(2)}) collective-permute-start(bf16[128,2048]{1,0:T(8,128)(2,1)S(1)} %get-tuple-element.94), channel_id=1, source_target_pairs={{0,2},{1,3},{2,0},{3,1},{4,6},{5,7},{6,4},{7,5},{8,10},{9,11},{10,... | collective-permute-start | bytes 1572872 | tf_op jit(solution)/shard_map/ppermute | solution.py:177
  116.6 51.3 %collective-permute-start.25 = (bf16[128,2048]{1,0:T(8,128)(2,1)S(1)}, bf16[128,2048]{1,0:T(8,128)(2,1)S(1)}, u32[]{:S(2)}, u32[]{:S(2)}) collective-permute-start(bf16[128,2048]{1,0:T(8,128)(2,1)S(1)} %get-tuple-element.94), channel_id=1, source_target_pairs={{0,1},{1,0},{2,3},{3,2},{4,5},{5,4},{6,7},{7,6},{8,9},{9,8},{10,11... | collective-permute-start | bytes 1572872 | tf_op jit(solution)/shard_map/ppermute | solution.py:177
  125.9 46.8 %collective-permute-start.26 = (bf16[128,2048]{1,0:T(8,128)(2,1)S(1)}, bf16[128,2048]{1,0:T(8,128)(2,1)S(1)}, u32[]{:S(2)}, u32[]{:S(2)}) collective-permute-start(bf16[128,2048]{1,0:T(8,128)(2,1)S(1)} %collective-permute-done.24), channel_id=1, source_target_pairs={{0,1},{1,0},{2,3},{3,2},{4,5},{5,4},{6,7},{7,6},{8,9},{9,8},{10,11... | collective-permute-start | bytes 1572872 | tf_op jit(solution)/shard_map/ppermute | solution.py:177
  173.5 57.4 %collective-permute-start.27 = (bf16[1024,2048]{1,0:T(8,128)(2,1)}, bf16[1024,2048]{1,0:T(8,128)(2,1)}, u32[]{:S(2)}, u32[]{:S(2)}) collective-permute-start(bf16[1024,2048]{1,0:T(8,128)(2,1)} %constant_dynamic-update-slice_fusion.25), channel_id=1, source_target_pairs={{0,4},{1,5},{2,6},{3,7},{4,0},{5,1},{6,2},{7,3},{8,12},{9,13},{10,... | collective-permute-start | bytes 12582920 | tf_op jit(solution)/shard_map/ppermute | solution.py:177
  173.5 98.4 %collective-permute-start.34 = (bf16[512,2048]{1,0:T(8,128)(2,1)}, bf16[512,2048]{1,0:T(8,128)(2,1)}, u32[]{:S(2)}, u32[]{:S(2)}) collective-permute-start(bf16[512,2048]{1,0:T(8,128)(2,1)} %bitcast.31), channel_id=1, source_target_pairs={{0,8},{1,9},{2,10},{3,11},{4,12},{5,13},{6,14},{7,15},{8,16},{9,17... | collective-permute-start | bytes 6291464 | tf_op jit(solution)/shard_map/ppermute | solution.py:183
  258.7 25.4 %collective-permute-start.31 = (bf16[128,2048]{1,0:T(8,128)(2,1)S(1)}, bf16[128,2048]{1,0:T(8,128)(2,1)S(1)}, u32[]{:S(2)}, u32[]{:S(2)}) collective-permute-start(bf16[128,2048]{1,0:T(8,128)(2,1)S(1)} %get-tuple-element.91), channel_id=1, source_target_pairs={{0,2},{1,3},{2,0},{3,1},{4,6},{5,7},{6,4},{7,5},{8,10},{9,11},{10,... | collective-permute-start | bytes 1572872 | tf_op jit(solution)/shard_map/ppermute | solution.py:177
  271.6 28.0 %collective-permute-start.37 = (bf16[256,2048]{1,0:T(8,128)(2,1)S(1)}, bf16[256,2048]{1,0:T(8,128)(2,1)S(1)}, u32[]{:S(2)}, u32[]{:S(2)}) collective-permute-start(bf16[256,2048]{1,0:T(8,128)(2,1)S(1)} %copy-done.59), channel_id=1, source_target_pairs={{0,8},{1,9},{2,10},{3,11},{4,12},{5,13},{6,14},{7,15},{8,16},{9,17... | collective-permute-start | bytes 3145736 | tf_op jit(solution)/shard_map/ppermute | solution.py:183
  271.9 72.7 %collective-permute-start.35 = (bf16[512,2048]{1,0:T(8,128)(2,1)}, bf16[512,2048]{1,0:T(8,128)(2,1)}, u32[]{:S(2)}, u32[]{:S(2)}) collective-permute-start(bf16[512,2048]{1,0:T(8,128)(2,1)} %collective-permute-done.34), channel_id=1, source_target_pairs={{0,8},{1,9},{2,10},{3,11},{4,12},{5,13},{6,14},{7,15},{8,16},{9,17... | collective-permute-start | bytes 6291464 | tf_op jit(solution)/shard_map/ppermute | solution.py:183
  299.6 141.6 %collective-permute-start.40 = (bf16[1024,2048]{1,0:T(8,128)(2,1)}, bf16[1024,2048]{1,0:T(8,128)(2,1)}, u32[]{:S(2)}, u32[]{:S(2)}) collective-permute-start(bf16[1024,2048]{1,0:T(8,128)(2,1)} %constant_dynamic-update-slice_fusion.17), channel_id=1, source_target_pairs={{0,4},{1,5},{2,6},{3,7},{4,0},{5,1},{6,2},{7,3},{8,12},{9,13},{10,... | collective-permute-start | bytes 12582920 | tf_op jit(solution)/shard_map/ppermute | solution.py:177
  300.6 66.4 %collective-permute-start.38 = (bf16[256,2048]{1,0:T(8,128)(2,1)S(1)}, bf16[256,2048]{1,0:T(8,128)(2,1)}, u32[]{:S(2)}, u32[]{:S(2)}) collective-permute-start(bf16[256,2048]{1,0:T(8,128)(2,1)S(1)} %collective-permute-done.37), channel_id=1, source_target_pairs={{0,8},{1,9},{2,10},{3,11},{4,12},{5,13},{6,14},{7,15},{8,16},{9,17... | collective-permute-start | bytes 3145736 | tf_op jit(solution)/shard_map/ppermute | solution.py:183
  344.6 94.8 %collective-permute-start.36 = (bf16[512,2048]{1,0:T(8,128)(2,1)}, bf16[512,2048]{1,0:T(8,128)(2,1)}, u32[]{:S(2)}, u32[]{:S(2)}) collective-permute-start(bf16[512,2048]{1,0:T(8,128)(2,1)} %collective-permute-done.35), channel_id=1, source_target_pairs={{0,8},{1,9},{2,10},{3,11},{4,12},{5,13},{6,14},{7,15},{8,16},{9,17... | collective-permute-start | bytes 6291464 | tf_op jit(solution)/shard_map/ppermute | solution.py:183
  367.0 65.7 %collective-permute-start.39 = (bf16[256,2048]{1,0:T(8,128)(2,1)}, bf16[256,2048]{1,0:T(8,128)(2,1)}, u32[]{:S(2)}, u32[]{:S(2)}) collective-permute-start(bf16[256,2048]{1,0:T(8,128)(2,1)} %collective-permute-done.38), channel_id=1, source_target_pairs={{0,8},{1,9},{2,10},{3,11},{4,12},{5,13},{6,14},{7,15},{8,16},{9,17... | collective-permute-start | bytes 3145736 | tf_op jit(solution)/shard_map/ppermute | solution.py:183
  486.7 23.8 %collective-permute-start.42 = (bf16[128,2048]{1,0:T(8,128)(2,1)S(1)}, bf16[128,2048]{1,0:T(8,128)(2,1)S(1)}, u32[]{:S(2)}, u32[]{:S(2)}) collective-permute-start(bf16[128,2048]{1,0:T(8,128)(2,1)S(1)} %get-tuple-element.71), channel_id=1, source_target_pairs={{0,2},{1,3},{2,0},{3,1},{4,6},{5,7},{6,4},{7,5},{8,10},{9,11},{10,... | collective-permute-start | bytes 1572872 | tf_op jit(solution)/shard_map/ppermute | solution.py:177
  500.5 23.8 %collective-permute-start.45 = (bf16[128,2048]{1,0:T(8,128)(2,1)S(1)}, bf16[128,2048]{1,0:T(8,128)(2,1)S(1)}, u32[]{:S(2)}, u32[]{:S(2)}) collective-permute-start(bf16[128,2048]{1,0:T(8,128)(2,1)S(1)} %get-tuple-element.73), channel_id=1, source_target_pairs={{0,1},{1,0},{2,3},{3,2},{4,5},{5,4},{6,7},{7,6},{8,9},{9,8},{10,11... | collective-permute-start | bytes 1572872 | tf_op jit(solution)/shard_map/ppermute | solution.py:177
  534.0 24.4 %collective-permute-start.49 = (bf16[128,2048]{1,0:T(8,128)(2,1)S(1)}, bf16[128,2048]{1,0:T(8,128)(2,1)S(1)}, u32[]{:S(2)}, u32[]{:S(2)}) collective-permute-start(bf16[128,2048]{1,0:T(8,128)(2,1)S(1)} %get-tuple-element.90), channel_id=1, source_target_pairs={{0,2},{1,3},{2,0},{3,1},{4,6},{5,7},{6,4},{7,5},{8,10},{9,11},{10,... | collective-permute-start | bytes 1572872 | tf_op jit(solution)/shard_map/ppermute | solution.py:177
  596.4 56.0 %collective-permute-start.93 = (bf16[256,2048]{1,0:T(8,128)(2,1)}, bf16[256,2048]{1,0:T(8,128)(2,1)}, u32[]{:S(2)}, u32[]{:S(2)}) collective-permute-start(bf16[256,2048]{1,0:T(8,128)(2,1)} %constant_dynamic-slice_fusion.1), channel_id=1, source_target_pairs={{0,8},{1,9},{2,10},{3,11},{4,12},{5,13},{6,14},{7,15},{8,16},{9,17... | collective-permute-start | bytes 3145736 | tf_op jit(solution)/shard_map/ppermute | solution.py:183
  623.7 104.4 %collective-permute-start.55 = (bf16[1024,2048]{1,0:T(8,128)(2,1)}, bf16[1024,2048]{1,0:T(8,128)(2,1)}, u32[]{:S(2)}, u32[]{:S(2)}) collective-permute-start(bf16[1024,2048]{1,0:T(8,128)(2,1)} %fusion.24), channel_id=1, source_target_pairs={{0,4},{1,5},{2,6},{3,7},{4,0},{5,1},{6,2},{7,3},{8,12},{9,13},{10,... | collective-permute-start | bytes 12582920 | tf_op jit(solution)/shard_map/ppermute | solution.py:177
  652.4 50.5 %collective-permute-start.90 = (bf16[512,2048]{1,0:T(8,128)(2,1)}, bf16[512,2048]{1,0:T(8,128)(2,1)S(1)}, u32[]{:S(2)}, u32[]{:S(2)}) collective-permute-start(bf16[512,2048]{1,0:T(8,128)(2,1)} %constant_dynamic-slice_fusion.2), channel_id=1, source_target_pairs={{0,8},{1,9},{2,10},{3,11},{4,12},{5,13},{6,14},{7,15},{8,16},{9,17... | collective-permute-start | bytes 6291464 | tf_op jit(solution)/shard_map/ppermute | solution.py:183
  655.1 70.5 %collective-permute-start.94 = (bf16[256,2048]{1,0:T(8,128)(2,1)}, bf16[256,2048]{1,0:T(8,128)(2,1)}, u32[]{:S(2)}, u32[]{:S(2)}) collective-permute-start(bf16[256,2048]{1,0:T(8,128)(2,1)} %add_convert_fusion.7), channel_id=1, source_target_pairs={{0,8},{1,9},{2,10},{3,11},{4,12},{5,13},{6,14},{7,15},{8,16},{9,17... | collective-permute-start | bytes 3145736 | tf_op jit(solution)/shard_map/ppermute | solution.py:183
  706.6 93.5 %collective-permute-start.91 = (bf16[512,2048]{1,0:T(8,128)(2,1)}, bf16[512,2048]{1,0:T(8,128)(2,1)}, u32[]{:S(2)}, u32[]{:S(2)}) collective-permute-start(bf16[512,2048]{1,0:T(8,128)(2,1)} %add_convert_fusion.5), channel_id=1, source_target_pairs={{0,8},{1,9},{2,10},{3,11},{4,12},{5,13},{6,14},{7,15},{8,16},{9,17... | collective-permute-start | bytes 6291464 | tf_op jit(solution)/shard_map/ppermute | solution.py:183
  728.1 63.9 %collective-permute-start.95 = (bf16[256,2048]{1,0:T(8,128)(2,1)}, bf16[256,2048]{1,0:T(8,128)(2,1)}, u32[]{:S(2)}, u32[]{:S(2)}) collective-permute-start(bf16[256,2048]{1,0:T(8,128)(2,1)} %add_convert_fusion.6), channel_id=1, source_target_pairs={{0,8},{1,9},{2,10},{3,11},{4,12},{5,13},{6,14},{7,15},{8,16},{9,17... | collective-permute-start | bytes 3145736 | tf_op jit(solution)/shard_map/ppermute | solution.py:183
  737.2 59.5 %collective-permute-start.56 = (bf16[128,2048]{1,0:T(8,128)(2,1)}, bf16[128,2048]{1,0:T(8,128)(2,1)S(1)}, u32[]{:S(2)}, u32[]{:S(2)}) collective-permute-start(bf16[128,2048]{1,0:T(8,128)(2,1)} %get-tuple-element.65), channel_id=1, source_target_pairs={{0,2},{1,3},{2,0},{3,1},{4,6},{5,7},{6,4},{7,5},{8,10},{9,11},{10,... | collective-permute-start | bytes 1572872 | tf_op jit(solution)/shard_map/ppermute | solution.py:177
  737.5 59.2 %collective-permute-start.60 = (bf16[128,2048]{1,0:T(8,128)(2,1)}, bf16[128,2048]{1,0:T(8,128)(2,1)S(1)}, u32[]{:S(2)}, u32[]{:S(2)}) collective-permute-start(bf16[128,2048]{1,0:T(8,128)(2,1)} %get-tuple-element.66), channel_id=1, source_target_pairs={{0,1},{1,0},{2,3},{3,2},{4,5},{5,4},{6,7},{7,6},{8,9},{9,8},{10,11... | collective-permute-start | bytes 1572872 | tf_op jit(solution)/shard_map/ppermute | solution.py:177
  752.0 44.7 %collective-permute-start.58 = (bf16[128,2048]{1,0:T(8,128)(2,1)S(1)}, bf16[128,2048]{1,0:T(8,128)(2,1)S(1)}, u32[]{:S(2)}, u32[]{:S(2)}) collective-permute-start(bf16[128,2048]{1,0:T(8,128)(2,1)S(1)} %add_convert_fusion.21), channel_id=1, source_target_pairs={{0,1},{1,0},{2,3},{3,2},{4,5},{5,4},{6,7},{7,6},{8,9},{9,8},{10,11... | collective-permute-start | bytes 1572872 | tf_op jit(solution)/shard_map/ppermute | solution.py:177
  804.6 131.7 %collective-permute-start.92 = (bf16[512,2048]{1,0:T(8,128)(2,1)}, bf16[512,2048]{1,0:T(8,128)(2,1)}, u32[]{:S(2)}, u32[]{:S(2)}) collective-permute-start(bf16[512,2048]{1,0:T(8,128)(2,1)} %add_convert_fusion.4), channel_id=1, source_target_pairs={{0,8},{1,9},{2,10},{3,11},{4,12},{5,13},{6,14},{7,15},{8,16},{9,17... | collective-permute-start | bytes 6291464 | tf_op jit(solution)/shard_map/ppermute | solution.py:183
  819.8 39.7 %all-to-all-start.3 = ((bf16[8,256,256]{2,1,0:T(8,128)(2,1)}), bf16[8,256,256]{2,1,0:T(8,128)(2,1)}, u32[]{:S(2)}, u32[]{:S(2)}) async-start(bf16[8,256,256]{2,1,0:T(8,128)(2,1)} %convolution_bitcast_fusion.1), calls=%async_computation.3 | async-start | bytes 2097152 | tf_op jit(solution)/shard_map/all_to_all | solution.py:243
  859.0 102.3 %collective-permute-start.75 = (bf16[1024,2048]{1,0:T(8,128)(2,1)}, bf16[1024,2048]{1,0:T(8,128)(2,1)}, u32[]{:S(2)}, u32[]{:S(2)}) collective-permute-start(bf16[1024,2048]{1,0:T(8,128)(2,1)} %slice_bitcast_fusion), channel_id=1, source_target_pairs={{0,4},{1,5},{2,6},{3,7},{4,0},{5,1},{6,2},{7,3},{8,12},{9,13},{10,... | collective-permute-start | bytes 12582920 | tf_op jit(solution)/shard_map/ppermute | solution.py:177
  925.8 63.5 %collective-permute-start.65 = (bf16[1024,2048]{1,0:T(8,128)(2,1)}, bf16[1024,2048]{1,0:T(8,128)(2,1)}, u32[]{:S(2)}, u32[]{:S(2)}) collective-permute-start(bf16[1024,2048]{1,0:T(8,128)(2,1)} %fusion.47), channel_id=1, source_target_pairs={{0,4},{1,5},{2,6},{3,7},{4,0},{5,1},{6,2},{7,3},{8,12},{9,13},{10,... | collective-permute-start | bytes 12582920 | tf_op jit(solution)/shard_map/ppermute | solution.py:177
  940.8 30.3 %all-to-all-start.5 = ((bf16[8,64,2048]{2,1,0:T(8,128)(2,1)}), bf16[8,64,2048]{2,1,0:T(8,128)(2,1)S(1)}, u32[]{:S(2)}, u32[]{:S(2)}) async-start(bf16[8,64,2048]{2,1,0:T(8,128)(2,1)} %bitcast.211), calls=%async_computation.5 | async-start | bytes 4194304 | tf_op jit(solution)/shard_map/all_to_all | solution.py:243
  982.6 43.1 %collective-permute-start.74 = (bf16[512,768]{1,0:T(8,128)(2,1)S(1)}, bf16[512,768]{1,0:T(8,128)(2,1)S(1)}, u32[]{:S(2)}, u32[]{:S(2)}) collective-permute-start(bf16[512,768]{1,0:T(8,128)(2,1)S(1)} %add_convert_fusion.12), channel_id=1, source_target_pairs={{0,8},{1,9},{2,10},{3,11},{4,12},{5,13},{6,14},{7,15},{8,16},{9,17... | collective-permute-start | bytes 2359304 | tf_op jit(solution)/shard_map/ppermute | solution.py:183
  987.6 49.1 %collective-permute-start.76 = (bf16[128,2048]{1,0:T(8,128)(2,1)}, bf16[128,2048]{1,0:T(8,128)(2,1)S(1)}, u32[]{:S(2)}, u32[]{:S(2)}) collective-permute-start(bf16[128,2048]{1,0:T(8,128)(2,1)} %get-tuple-element.52), channel_id=1, source_target_pairs={{0,2},{1,3},{2,0},{3,1},{4,6},{5,7},{6,4},{7,5},{8,10},{9,11},{10,... | collective-permute-start | bytes 1572872 | tf_op jit(solution)/shard_map/ppermute | solution.py:177
  989.3 33.6 %collective-permute-start.81 = (bf16[128,2048]{1,0:T(8,128)(2,1)S(1)}, bf16[128,2048]{1,0:T(8,128)(2,1)S(1)}, u32[]{:S(2)}, u32[]{:S(2)}) collective-permute-start(bf16[128,2048]{1,0:T(8,128)(2,1)S(1)} %add_convert_fusion.15), channel_id=1, source_target_pairs={{0,2},{1,3},{2,0},{3,1},{4,6},{5,7},{6,4},{7,5},{8,10},{9,11},{10,... | collective-permute-start | bytes 1572872 | tf_op jit(solution)/shard_map/ppermute | solution.py:177
  1000.5 33.7 %collective-permute-start.67 = (bf16[128,2048]{1,0:T(8,128)(2,1)}, bf16[128,2048]{1,0:T(8,128)(2,1)S(1)}, u32[]{:S(2)}, u32[]{:S(2)}) collective-permute-start(bf16[128,2048]{1,0:T(8,128)(2,1)} %get-tuple-element.58), channel_id=1, source_target_pairs={{0,2},{1,3},{2,0},{3,1},{4,6},{5,7},{6,4},{7,5},{8,10},{9,11},{10,... | collective-permute-start | bytes 1572872 | tf_op jit(solution)/shard_map/ppermute | solution.py:177
  1030.7 24.3 %collective-permute-start.66 = (bf16[128,2048]{1,0:T(8,128)(2,1)}, bf16[128,2048]{1,0:T(8,128)(2,1)S(1)}, u32[]{:S(2)}, u32[]{:S(2)}) collective-permute-start(bf16[128,2048]{1,0:T(8,128)(2,1)} %get-tuple-element.55), channel_id=1, source_target_pairs={{0,2},{1,3},{2,0},{3,1},{4,6},{5,7},{6,4},{7,5},{8,10},{9,11},{10,... | collective-permute-start | bytes 1572872 | tf_op jit(solution)/shard_map/ppermute | solution.py:177
  1032.7 23.7 %collective-permute-start.70 = (bf16[128,2048]{1,0:T(8,128)(2,1)}, bf16[128,2048]{1,0:T(8,128)(2,1)}, u32[]{:S(2)}, u32[]{:S(2)}) collective-permute-start(bf16[128,2048]{1,0:T(8,128)(2,1)} %get-tuple-element.56), channel_id=1, source_target_pairs={{0,1},{1,0},{2,3},{3,2},{4,5},{5,4},{6,7},{7,6},{8,9},{9,8},{10,11... | collective-permute-start | bytes 1572872 | tf_op jit(solution)/shard_map/ppermute | solution.py:177
  1036.1 31.5 %collective-permute-start.68 = (bf16[128,2048]{1,0:T(8,128)(2,1)}, bf16[128,2048]{1,0:T(8,128)(2,1)}, u32[]{:S(2)}, u32[]{:S(2)}) collective-permute-start(bf16[128,2048]{1,0:T(8,128)(2,1)} %add_convert_fusion.19), channel_id=1, source_target_pairs={{0,1},{1,0},{2,3},{3,2},{4,5},{5,4},{6,7},{7,6},{8,9},{9,8},{10,11... | collective-permute-start | bytes 1572872 | tf_op jit(solution)/shard_map/ppermute | solution.py:177
  1049.1 31.3 %collective-permute-start.69 = (bf16[128,2048]{1,0:T(8,128)(2,1)}, bf16[128,2048]{1,0:T(8,128)(2,1)S(1)}, u32[]{:S(2)}, u32[]{:S(2)}) collective-permute-start(bf16[128,2048]{1,0:T(8,128)(2,1)} %get-tuple-element.57), channel_id=1, source_target_pairs={{0,1},{1,0},{2,3},{3,2},{4,5},{5,4},{6,7},{7,6},{8,9},{9,8},{10,11... | collective-permute-start | bytes 1572872 | tf_op jit(solution)/shard_map/ppermute | solution.py:177
  (151 other events, 2311.9 us)

commit v2 on v1

v2 whole, which is shorter than its diff:
```python
import functools
import math

import jax
import jax.numpy as jnp
from jax import lax
from jax.experimental import pallas as pl
from jax.experimental.pallas import tpu as pltpu
from jax.sharding import PartitionSpec as P

HD = 128
IMG = 256
EPS = 1e-06
THETA = 500000.0
NEG = -1e30
AXES = ("dp", "ctx")
F32 = jnp.float32
BF16 = jnp.bfloat16
SCALE = 1.0 / math.sqrt(HD)
LOG2E = math.log2(math.e)


def dot(left, right, left_dim, right_dim, kind=F32):
    return lax.dot_general(
        left, right, (((left_dim,), (right_dim,)), ((), ())), preferred_element_type=kind
    )


def probs_of(q, k, limit, places):
    scores = dot(q, k, 1, 1)
    scores = jnp.where(places <= limit, scores, NEG)
    peak = jnp.max(scores, axis=-1, keepdims=True)
    weights = jnp.exp2((scores - peak) * (SCALE * LOG2E))
    return weights * (1.0 / jnp.sum(weights, axis=-1, keepdims=True))


def attend_kernel(q_ref, k_ref, v_ref, limit_ref, place_ref, out_ref):
    probs = probs_of(q_ref[...], k_ref[...], limit_ref[...], place_ref[0])
    out_ref[...] = dot(probs.astype(BF16), v_ref[...], 1, 0).astype(BF16)


def attend_back_kernel(
    q_ref, k_ref, v_ref, g_ref, limit_ref, place_ref, dq_ref, dk_ref, dv_ref
):
    step = pl.program_id(2)

    @pl.when(step == 0)
    def _():
        dk_ref[...] = jnp.zeros_like(dk_ref)
        dv_ref[...] = jnp.zeros_like(dv_ref)

    q, k, v, g = q_ref[...], k_ref[...], v_ref[...], g_ref[...]
    probs = probs_of(q, k, limit_ref[...], place_ref[0])
    grad_probs = dot(g, v, 1, 1)
    inner = jnp.sum(probs * grad_probs, axis=-1, keepdims=True)
    grad_scores = (probs * (grad_probs - inner)).astype(BF16)
    dq_ref[...] = dot(grad_scores, k, 1, 0) * SCALE
    dk_ref[...] += dot(grad_scores, q, 0, 0) * SCALE
    dv_ref[...] += dot(probs.astype(BF16), g, 0, 0)


def attention_specs(seq_len, rows):
    steps = seq_len // rows
    query = pl.BlockSpec((rows, HD), lambda s, h, i: (s * steps + i, h))
    keys = pl.BlockSpec((seq_len, HD), lambda s, h, i: (s, h))
    limit = pl.BlockSpec((rows, 1), lambda s, h, i: (s * steps + i, 0))
    places = pl.BlockSpec((1, 1, seq_len), lambda s, h, i: (s, 0, 0))
    return query, keys, limit, places


def attend(q, k, v, limits, places, seq_len):
    rows = min(256, seq_len)
    total, width = q.shape
    query, keys, limit, place = attention_specs(seq_len, rows)
    return pl.pallas_call(
        attend_kernel,
        out_shape=jax.ShapeDtypeStruct((total, width), BF16),
        grid=(total // seq_len, width // HD, seq_len // rows),
        in_specs=[query, keys, keys, limit, place],
        out_specs=query,
        compiler_params=pltpu.CompilerParams(vmem_limit_bytes=48 * 2**20),
        cost_estimate=pl.CostEstimate(
            flops=4 * total * seq_len * width,
            bytes_accessed=8 * total * width,
            transcendentals=total * seq_len * (width // HD),
        ),
        name="attend",
    )(q, k, v, limits, places)


def attend_back(q, k, v, g, limits, places, seq_len):
    rows = min(256, seq_len)
    total, width = q.shape
    query, keys, limit, place = attention_specs(seq_len, rows)
    shape = jax.ShapeDtypeStruct((total, width), F32)
    return pl.pallas_call(
        attend_back_kernel,
        out_shape=(shape, shape, shape),
        grid=(total // seq_len, width // HD, seq_len // rows),
        in_specs=[query, keys, keys, query, limit, place],
        out_specs=(query, keys, keys),
        compiler_params=pltpu.CompilerParams(vmem_limit_bytes=48 * 2**20),
        cost_estimate=pl.CostEstimate(
            flops=10 * total * seq_len * width,
            bytes_accessed=20 * total * width,
            transcendentals=total * seq_len * (width // HD),
        ),
        name="attend_back",
    )(q, k, v, g, limits, places)


MESH = pl.DeviceIdType.MESH
ANY = pl.BlockSpec(memory_space=pl.ANY)


def flipped(at, mask):
    bit = 1
    while bit <= mask:
        if mask & bit:
            at = at + bit - 2 * bit * lax.rem(lax.div(at, bit), 2)
        bit *= 2
    return at


def bit_orders(C):
    bits = [1 << b for b in range(C.bit_length() - 1)]
    return bits, bits[::-1]


def tree(order):
    found = [(0, order, 0)]
    for place, bit in enumerate(order):
        found += [(mask | bit, order[place + 1 :], bit) for mask, _, _ in list(found)]
    return found


def greet(peers):
    barrier = pltpu.get_barrier_semaphore()
    for peer in peers:
        pl.semaphore_signal(barrier, inc=1, device_id=peer, device_id_type=MESH)
    pl.semaphore_wait(barrier, len(peers))


def remote(src, dst, sent, arrived, device):
    return pltpu.make_async_remote_copy(
        src_ref=src, dst_ref=dst, send_sem=sent, recv_sem=arrived, device_id=device, device_id_type=MESH
    )


def places_of():
    dp, ctx = lax.axis_index("dp"), lax.axis_index("ctx")
    return dp, ctx, dp + 1 - 2 * lax.rem(dp, 2)


class Gather:
    def __init__(self, C, source, slot, over, from_over, sems):
        self.C = C
        self.source, self.slot, self.over, self.from_over = source, slot, over, from_over
        self.ctx_sent, self.ctx_came, self.core_sent, self.core_came = sems
        self.dp, self.ctx, self.twin = places_of()
        self.trees = [tree(order) for order in bit_orders(C)]
        self.sends = []

    def held(self, half, mask):
        return self.slot(flipped(self.ctx, mask), half) if mask else self.source(half)

    def by_ctx(self, half, mask, bit):
        return remote(
            self.held(half, mask),
            self.slot(flipped(self.ctx, mask), half),
            self.ctx_sent.at[half, mask | bit],
            self.ctx_came.at[half, mask | bit],
            (self.dp, flipped(self.ctx, bit)),
        )

    def by_core(self, half, mask):
        return remote(
            self.held(half, mask),
            self.over(flipped(self.ctx, mask), half),
            self.core_sent.at[half, mask],
            self.core_came.at[half, mask],
            (self.twin, self.ctx),
        )

    def landed(self, half, mask, bit):
        slot = self.slot(flipped(self.ctx, mask), half)
        remote(
            slot,
            slot,
            self.ctx_sent.at[half, mask],
            self.ctx_came.at[half, mask],
            (self.dp, flipped(self.ctx, bit)),
        ).wait_recv()

    def start(self, copy):
        copy.start()
        self.sends.append(copy)

    def step(self, index):
        for half in range(2):
            mask, onward, bit = self.trees[half][index]
            if mask:
                self.landed(half, mask, bit)
            for further in onward:
                self.start(self.by_ctx(half, mask, further))
            if mask:
                self.start(self.by_core(half, mask))
        if index == 0:
            for half in range(2):
                self.start(self.by_core(half, 0))

    def finish(self):
        for copy in self.sends:
            copy.wait_send()
        for half in range(2):
            for mask in range(self.C):
                slot = self.from_over(flipped(self.ctx, mask), half)
                remote(
                    slot,
                    slot,
                    self.core_sent.at[half, mask],
                    self.core_came.at[half, mask],
                    (self.twin, self.ctx),
                ).wait_recv()


def rows_gather(C, x_ref, out_ref, sems):
    count = x_ref.shape[0]
    size = count // 2

    def rows(seat, half):
        return pl.ds(seat * count + half * size, size)

    return Gather(
        C,
        lambda half: x_ref.at[pl.ds(half * size, size)],
        lambda seat, half: out_ref.at[0, rows(seat, half)],
        lambda seat, half: out_ref.at[1, rows(seat, half)],
        lambda seat, half: out_ref.at[1, rows(seat, half)],
        sems,
    )


class Spread:
    def __init__(self, C, Z, x_ref, out_ref, own_sem, ring_sent, ring_came, sems):
        dp, ctx, _ = places_of()
        core = lax.rem(dp, 2)
        self.Z, self.z, self.ctx = Z, lax.div(dp, 2), ctx
        self.ahead, self.behind = lax.rem(dp + 2, 2 * Z), lax.rem(dp + 2 * Z - 2, 2 * Z)
        self.out, self.place = out_ref, core * C + ctx
        self.ring_sent, self.ring_came = ring_sent, ring_came
        self.own = pltpu.make_async_copy(x_ref, out_ref.at[self.z, self.place], own_sem)
        size = Z // 2

        def slot(side, seat, half):
            return out_ref.at[pl.ds(half * size, size), side * C + seat]

        self.gather = Gather(
            C,
            lambda half: slot(core, ctx, half),
            lambda seat, half: slot(core, seat, half),
            lambda seat, half: slot(core, seat, half),
            lambda seat, half: slot(1 - core, seat, half),
            sems,
        )

    def hop(self, step):
        block = self.out.at[lax.rem(self.z + self.Z - step, self.Z), self.place]
        return remote(
            block, block, self.ring_sent.at[step], self.ring_came.at[step], (self.ahead, self.ctx)
        )

    def hop_landed(self, step):
        block = self.out.at[lax.rem(self.z + 2 * self.Z - 1 - step, self.Z), self.place]
        remote(
            block, block, self.ring_sent.at[step], self.ring_came.at[step], (self.behind, self.ctx)
        ).wait_recv()

    def finish(self):
        for step in range(self.Z - 1):
            self.hop(step).wait_send()
        self.gather.finish()


def gather_sems(C):
    return [pltpu.SemaphoreType.DMA((2, C))] * 4


def plane_neighbours(C):
    dp, ctx, twin = places_of()
    return [(dp, flipped(ctx, bit)) for bit in bit_orders(C)[0]] + [(twin, ctx)]


def comm_params(number, megabytes=16):
    return pltpu.CompilerParams(
        collective_id=number, has_side_effects=True, vmem_limit_bytes=megabytes * 2**20
    )


def cost_of(microseconds):
    return pl.CostEstimate(flops=int(microseconds * 1e6), bytes_accessed=1024, transcendentals=0)


def gather_kernel(C, x_ref, out_ref, own_sem, *sems):
    greet(plane_neighbours(C))
    count = x_ref.shape[0]
    own = pltpu.make_async_copy(
        x_ref, out_ref.at[0, pl.ds(lax.axis_index("ctx") * count, count)], own_sem
    )
    gather = rows_gather(C, x_ref, out_ref, sems)
    for index in range(C):
        gather.step(index)
        if index == 0:
            own.start()
    own.wait()
    gather.finish()


def gather_rows(x, C, number):
    return pl.pallas_call(
        functools.partial(gather_kernel, C),
        out_shape=jax.ShapeDtypeStruct((2, C * x.shape[0], x.shape[1]), x.dtype),
        in_specs=[ANY],
        out_specs=ANY,
        scratch_shapes=[pltpu.SemaphoreType.DMA] + gather_sems(C),
        compiler_params=comm_params(number),
        cost_estimate=cost_of(40),
        name="gather_rows",
    )(x)


def plane_peers(C):
    dp, ctx, twin = places_of()
    peers = [(there, flipped(ctx, mask)) for there in (dp, twin) for mask in range(C)]
    return list(enumerate(peers))[1:]


def place_in_plane(C, device):
    return lax.rem(device[0], 2) * C + device[1]


class Deal:
    def __init__(self, C, weights, wide, blocks, out_ref, row_at, sent, came, own_sem):
        self.C, self.out, self.wide, self.sems = C, out_ref, wide, (sent, came, own_sem)
        self.peers, self.row_at = plane_peers(C), row_at
        self.shard = weights[0].shape[0]
        dp, ctx, _ = places_of()
        self.parts = []
        for weight in weights:
            for block in range(blocks):
                self.parts.append((weight, block * 2 * C))
        self.own_device = (dp, ctx)
        self.copies = []

    def spot(self, device, number):
        rows = pl.ds(self.row_at(device), self.shard)
        return self.out.at[rows, pl.ds(number * self.wide, self.wide)]

    def start(self):
        sent, came, own_sem = self.sems
        for number, (weight, first) in enumerate(self.parts):
            for index, device in [(0, self.own_device)] + self.peers:
                at = (first + place_in_plane(self.C, device)) * self.wide
                source = weight.at[:, pl.ds(pl.multiple_of(at, 128), self.wide)]
                target = self.spot(self.own_device, number)
                if index == 0:
                    copy = pltpu.make_async_copy(source, target, own_sem.at[number])
                else:
                    copy = remote(
                        source, target, sent.at[number, index], came.at[number, index], device
                    )
                copy.start()
                self.copies.append((copy, index))

    def landed(self):
        sent, came, _ = self.sems
        for number in range(len(self.parts)):
            for index, device in self.peers:
                spot = self.spot(device, number)
                remote(
                    spot, spot, sent.at[number, index], came.at[number, index], device
                ).wait_recv()
        for copy, index in self.copies:
            if index:
                copy.wait_send()
            else:
                copy.wait()


def deal_sems(C, parts):
    return [
        pltpu.SemaphoreType.DMA((parts, 2 * C)),
        pltpu.SemaphoreType.DMA((parts, 2 * C)),
        pltpu.SemaphoreType.DMA((parts,)),
    ]


def first_kernel(C, Z, dealt, *refs):
    x_ref, wq_ref, wk_ref, wv_ref, wo_ref, gains_ref = refs[:6]
    refs = refs[6:]
    if dealt:
        (wg_ref, wu_ref), refs = refs[:2], refs[2:]
    x_out, w_out, wo_out, gains_out = refs[:4]
    refs = refs[4:]
    if dealt:
        gu_out, refs = refs[0], refs[1:]
    own_sem, gather_set, refs = refs[0], refs[1:5], refs[5:]
    deal_set, (ring_sent, ring_came), refs = refs[:3], refs[3:5], refs[5:]
    spread_sets, refs = (refs[:7], refs[7:14]), refs[14:]
    A = 2 * C
    dp, ctx, _ = places_of()
    z = lax.div(dp, 2)
    ahead, behind = lax.rem(dp + 2, 2 * Z), lax.rem(dp + 2 * Z - 2, 2 * Z)
    greet([device for _, device in plane_peers(C)] + [(ahead, ctx), (behind, ctx)])
    shard = wq_ref.shape[0]
    spreads = [
        Spread(C, Z, x, out, sems[0], sems[1], sems[2], sems[3:])
        for x, out, sems in ((gains_ref, gains_out, spread_sets[0]), (wo_ref, wo_out, spread_sets[1]))
    ]
    for spread in spreads:
        spread.own.start()
    deal = Deal(
        C, (wq_ref, wk_ref, wv_ref), wq_ref.shape[1] // A, 1, w_out,
        lambda device: (device[0] * C + device[1]) * shard, *deal_set,
    )
    deal.start()
    for spread in spreads:
        spread.own.wait()
        spread.hop(0).start()
    count = x_ref.shape[0]
    own = pltpu.make_async_copy(x_ref, x_out.at[0, pl.ds(ctx * count, count)], own_sem)
    own.start()
    gather = rows_gather(C, x_ref, x_out, gather_set)
    gather.step(0)

    def ring(step):
        block = w_out.at[pl.ds(lax.rem(z + Z - step, Z) * (A * shard), A * shard)]
        return remote(block, block, ring_sent.at[step], ring_came.at[step], (ahead, ctx))

    def ring_landed(step):
        block = w_out.at[pl.ds(lax.rem(z + 2 * Z - 1 - step, Z) * (A * shard), A * shard)]
        remote(block, block, ring_sent.at[step], ring_came.at[step], (behind, ctx)).wait_recv()

    deal.landed()
    ring(0).start()
    if dealt:
        columns = Deal(
            C, (wg_ref, wu_ref), wg_ref.shape[1] // (Z * A), Z, gu_out,
            lambda device: place_in_plane(C, device) * shard, *refs,
        )
        columns.start()
    for step in range(Z - 2):
        for spread in spreads:
            spread.hop_landed(step)
            spread.hop(step + 1).start()
        ring_landed(step)
        ring(step + 1).start()
        if step + 1 < C:
            gather.step(step + 1)
    for spread in spreads:
        spread.hop_landed(Z - 2)
    for index in range(Z - 1, C):
        gather.step(index)
    for index in range(C):
        for spread in spreads:
            spread.gather.step(index)
    if dealt:
        columns.landed()
    own.wait()
    gather.finish()
    for spread in spreads:
        spread.finish()
    ring_landed(Z - 2)
    for step in range(Z - 1):
        ring(step).wait_send()


def first_gather(x, w_query, w_key, w_value, w_out, gains, w_gate, w_up, dealt, C, Z, number):
    width = x.shape[1]
    A = 2 * C
    shard = w_query.shape[0]

    def shape(*sizes):
        return jax.ShapeDtypeStruct(sizes, x.dtype)

    outs = [
        shape(2, C * x.shape[0], width),
        shape(width, 3 * width // A),
        shape(Z, A, shard, width),
        shape(Z, A, *gains.shape),
    ]
    operands = [x, w_query, w_key, w_value, w_out, gains]
    spread = [
        pltpu.SemaphoreType.DMA,
        pltpu.SemaphoreType.DMA((Z,)),
        pltpu.SemaphoreType.DMA((Z,)),
    ] + gather_sems(C)
    scratch = (
        [pltpu.SemaphoreType.DMA]
        + gather_sems(C)
        + deal_sems(C, 3)
        + [pltpu.SemaphoreType.DMA((Z,))] * 2
        + spread * 2
    )
    if dealt:
        operands += [w_gate, w_up]
        outs.append(shape(A * shard, 2 * w_gate.shape[1] // A))
        scratch += deal_sems(C, 2 * Z)
    return pl.pallas_call(
        functools.partial(first_kernel, C, Z, dealt),
        out_shape=tuple(outs),
        in_specs=[ANY] * len(operands),
        out_specs=(ANY,) * len(outs),
        scratch_shapes=scratch,
        compiler_params=comm_params(number),
        cost_estimate=cost_of(100),
        name="first_gather",
    )(*operands)


ROWS = 256


def row_of_sums(values):
    high = values.astype(BF16)
    rest = (values - high.astype(F32)).astype(BF16)
    ones = jnp.ones((8, values.shape[1]), BF16)
    return dot(ones, high, 1, 1) + dot(ones, rest, 1, 1)


def pair_of_rows(first, second):
    return jnp.where(lax.broadcasted_iota(jnp.int32, first.shape, 0) == 0, first, second)


def columns_of(rows):
    eye = (
        lax.broadcasted_iota(jnp.int32, (8, 8), 0) == lax.broadcasted_iota(jnp.int32, (8, 8), 1)
    ).astype(BF16)
    high = rows.astype(BF16)
    rest = rows - high.astype(F32)
    middle = rest.astype(BF16)
    low = (rest - middle.astype(F32)).astype(BF16)
    return dot(high, eye, 0, 0) + dot(middle, eye, 0, 0) + dot(low, eye, 0, 0)


def start_sum(C, stats, landing, sent, came):
    for index, device in plane_peers(C):
        remote(stats, landing.at[index], sent.at[index], came.at[index], device).start()


def finish_sum(C, stats, landing, sent, came, total):
    blocks = stats.shape[0]
    for index, device in plane_peers(C):
        remote(stats, landing.at[index], sent.at[index], came.at[index], device).wait()
    for block in range(blocks):
        value = stats[block]
        for index in range(1, 2 * C):
            value = value + landing[index, block if index < C else (block + blocks // 2) % blocks]
        total[block] = value


def turned(value, cosine, sine):
    return value * cosine + pltpu.roll(value, HD // 2, 1) * sine


def project_kernel(
    C, x_ref, w_ref, gain_ref, cos_ref, sin_ref, rq_ref, rk_ref, v_ref, q_ref, k_ref, total,
    stats, landing, sent, came,
):
    greet([device for _, device in plane_peers(C)])
    wide = rq_ref.shape[1]
    width = x_ref.shape[1]
    blocks = stats.shape[0]

    def rows_at(block):
        return pl.ds(pl.multiple_of(block * ROWS, ROWS), ROWS)

    @pl.loop(0, blocks)
    def _(block):
        here = rows_at(block)
        raw = dot(x_ref[here, :], w_ref[...], 1, 0)
        query, key = raw[:, :wide], raw[:, wide : 2 * wide]
        rq_ref[here, :] = query
        rk_ref[here, :] = key
        v_ref[here, :] = raw[:, 2 * wide :].astype(BF16)
        stats[block] = pair_of_rows(row_of_sums(query * query), row_of_sums(key * key))

    start_sum(C, stats, landing, sent, came)
    finish_sum(C, stats, landing, sent, came, total)

    @pl.loop(0, blocks)
    def _(block):
        here = rows_at(block)
        factors = columns_of(lax.rsqrt(total[block] * (1.0 / width) + EPS))
        cosine, sine = cos_ref[here, :], sin_ref[here, :]
        for which, (raw, out) in enumerate(((rq_ref, q_ref), (rk_ref, k_ref))):
            factor = factors[:, which : which + 1]
            for head in range(wide // HD):
                lanes = slice(head * HD, (head + 1) * HD)
                value = raw[here, lanes] * factor * gain_ref[which : which + 1, lanes]
                out[here, lanes] = turned(value, cosine, sine).astype(BF16)


def plane_sum_scratch(C, blocks):
    return [
        pltpu.VMEM((blocks, 8, ROWS), F32),
        pltpu.VMEM((2 * C, blocks, 8, ROWS), F32),
        pltpu.SemaphoreType.DMA((2 * C,)),
        pltpu.SemaphoreType.DMA((2 * C,)),
    ]


VM = pl.BlockSpec(memory_space=pltpu.VMEM)


def project(x, w, gains, cosine, sine, C, number):
    total, width = x.shape
    wide = w.shape[1] // 3
    blocks = total // ROWS
    raw = jax.ShapeDtypeStruct((total, wide), F32)
    low = jax.ShapeDtypeStruct((total, wide), BF16)
    return pl.pallas_call(
        functools.partial(project_kernel, C),
        out_shape=(raw, raw, low, low, low, jax.ShapeDtypeStruct((blocks, 8, ROWS), F32)),
        in_specs=[VM] * 5,
        out_specs=(VM,) * 6,
        scratch_shapes=plane_sum_scratch(C, blocks),
        compiler_params=comm_params(number, 48),
        cost_estimate=cost_of(18),
        name="project",
    )(x, w, gains, cosine, sine)


def project_back_kernel(
    C, dq_ref, dk_ref, dv_ref, rq_ref, rk_ref, total, gain_ref, cos_ref, sin_ref,
    out_ref, term_ref, eq, ek, inner, stats, landing, sent, came,
):
    greet([device for _, device in plane_peers(C)])
    wide = rq_ref.shape[1]
    width = wide * 2 * C
    blocks = stats.shape[0]

    def rows_at(block):
        return pl.ds(pl.multiple_of(block * ROWS, ROWS), ROWS)

    def factors_of(block):
        return columns_of(lax.rsqrt(total[block] * (1.0 / width) + EPS))

    term_ref[...] = jnp.zeros_like(term_ref)

    @pl.loop(0, blocks)
    def _(block):
        here = rows_at(block)
        factors = factors_of(block)
        cosine, sine = cos_ref[here, :], sin_ref[here, :]
        sums = []
        for which, (grad, raw, kept) in enumerate(((dq_ref, rq_ref, eq), (dk_ref, rk_ref, ek))):
            for head in range(wide // HD):
                lanes = slice(head * HD, (head + 1) * HD)
                kept[here, lanes] = turned(grad[here, lanes], cosine, -sine)
            product = kept[here, :] * raw[here, :] * factors[:, which : which + 1]
            term_ref[which : which + 1, :] += jnp.sum(product, axis=0, keepdims=True)
            sums.append(row_of_sums(product * gain_ref[which : which + 1, :]))
        stats[block] = pair_of_rows(*sums)

    start_sum(C, stats, landing, sent, came)
    finish_sum(C, stats, landing, sent, came, inner)

    @pl.loop(0, blocks)
    def _(block):
        here = rows_at(block)
        factors = factors_of(block)
        means = columns_of(inner[block] * (1.0 / width))
        for which, (kept, raw) in enumerate(((eq, rq_ref), (ek, rk_ref))):
            factor, mean = factors[:, which : which + 1], means[:, which : which + 1]
            weighted = kept[here, :] * gain_ref[which : which + 1, :]
            value = factor * (weighted - raw[here, :] * factor * mean)
            out_ref[here, which * wide : (which + 1) * wide] = value.astype(BF16)
        out_ref[here, 2 * wide :] = dv_ref[here, :].astype(BF16)


def project_back(dq, dk, dv, raw_q, raw_k, sums, gains, cosine, sine, C, number):
    total, wide = dq.shape
    blocks = total // ROWS
    return pl.pallas_call(
        functools.partial(project_back_kernel, C),
        out_shape=(
            jax.ShapeDtypeStruct((total, 3 * wide), BF16),
            jax.ShapeDtypeStruct((8, wide), F32),
        ),
        in_specs=[VM] * 9,
        out_specs=(VM, VM),
        scratch_shapes=[
            pltpu.VMEM((total, wide), F32),
            pltpu.VMEM((total, wide), F32),
            pltpu.VMEM((blocks, 8, ROWS), F32),
        ]
        + plane_sum_scratch(C, blocks),
        compiler_params=comm_params(number, 48),
        cost_estimate=cost_of(15),
        name="project_back",
    )(dq, dk, dv, raw_q, raw_k, sums, gains, cosine, sine)


def return_kernel(C, groups, blocks, x_ref, *refs):
    outs, (landing, sent, came, own_sem) = refs[:groups], refs[groups:]
    A = 2 * C
    shard = outs[0].shape[0]
    part = outs[0].shape[1] // (blocks * A)
    dp, ctx, _ = places_of()
    own_at = place_in_plane(C, (dp, ctx))
    peers = plane_peers(C)
    greet([device for _, device in peers])
    own = pltpu.make_async_copy(
        x_ref.at[pl.ds(own_at * shard, shard)], landing.at[own_at], own_sem
    )
    own.start()

    def copy_to(index, device):
        rows = pl.ds(place_in_plane(C, device) * shard, shard)
        return remote(
            x_ref.at[rows], landing.at[own_at], sent.at[index], came.at[index], device
        )

    def landed(index, device):
        spot = landing.at[place_in_plane(C, device)]
        remote(spot, spot, sent.at[index], came.at[index], device).wait_recv()

    for index, device in peers:
        copy_to(index, device).start()
    own.wait()
    for index, device in peers:
        landed(index, device)
    for index, device in peers:
        copy_to(index, device).wait_send()
    for group in range(groups):
        for block in range(blocks):
            for at in range(A):
                lanes = (group * blocks + block) * part
                to = (block * A + at) * part
                outs[group][:, to : to + part] = landing[at, :, lanes : lanes + part]


def return_rows(x, C, groups, blocks, number):
    A = 2 * C
    shard = x.shape[0] // A
    width = x.shape[1] * A // groups
    return pl.pallas_call(
        functools.partial(return_kernel, C, groups, blocks),
        out_shape=(jax.ShapeDtypeStruct((shard, width), x.dtype),) * groups,
        in_specs=[ANY],
        out_specs=(VM,) * groups,
        scratch_shapes=[
            pltpu.VMEM((A, shard, x.shape[1]), x.dtype),
            pltpu.SemaphoreType.DMA((A,)),
            pltpu.SemaphoreType.DMA((A,)),
            pltpu.SemaphoreType.DMA,
        ],
        compiler_params=comm_params(number, 24),
        cost_estimate=cost_of(20),
        name="return_rows",
    )(x)


def scatter_kernel(
    C, own_ref, other_ref, out_ref, own, twin_part, landing,
    own_sem, core_sent, core_came, ctx_sent, ctx_came,
):
    count = out_ref.shape[0]
    half_rows = count // 2
    dp, ctx, twin = places_of()
    greet(plane_neighbours(C))
    trees = [tree(order)[::-1] for order in bit_orders(C)]

    def rows(half, mask):
        return pl.ds(flipped(ctx, mask) * count + half * half_rows, half_rows)

    def from_twin(half, mask):
        return remote(
            other_ref.at[rows(half, mask)],
            twin_part.at[rows(half, mask)],
            core_sent.at[half, mask],
            core_came.at[half, mask],
            (twin, ctx),
        )

    def local_copy(half, mask):
        return pltpu.make_async_copy(
            own_ref.at[rows(half, mask)], own.at[rows(half, mask)], own_sem.at[half, mask]
        )

    def onward(half, mask, bit):
        return remote(
            own.at[rows(half, mask)],
            landing.at[half, mask],
            ctx_sent.at[half, mask],
            ctx_came.at[half, mask],
            (dp, flipped(ctx, bit)),
        )

    for index in range(C):
        for half in range(2):
            mask = trees[half][index][0]
            local_copy(half, mask).start()
            from_twin(half, mask).start()
    for index in range(C):
        for half in range(2):
            mask, along, bit = trees[half][index]
            local_copy(half, mask).wait()
            from_twin(half, mask).wait_recv()
            here = rows(half, mask)
            total = own[here, :].astype(F32) + twin_part[here, :].astype(F32)
            for came in along:
                onward(half, mask | came, came).wait_recv()
                total = total + landing[half, mask | came].astype(F32)
            if mask:
                own[here, :] = total.astype(BF16)
                onward(half, mask, bit).start()
            else:
                out_ref[pl.ds(half * half_rows, half_rows), :] = total
    for half in range(2):
        for mask, _, bit in trees[half]:
            from_twin(half, mask).wait_send()
            if mask:
                onward(half, mask, bit).wait_send()


def scatter_rows(own, other, C, number):
    total, width = own.shape
    count = total // C
    return pl.pallas_call(
        functools.partial(scatter_kernel, C),
        out_shape=jax.ShapeDtypeStruct((count, width), F32),
        in_specs=[ANY, ANY],
        out_specs=pl.BlockSpec(memory_space=pltpu.VMEM),
        scratch_shapes=[
            pltpu.VMEM((total, width), BF16),
            pltpu.VMEM((total, width), BF16),
            pltpu.VMEM((2, C, count // 2, width), BF16),
        ]
        + [pltpu.SemaphoreType.DMA((2, C))] * 5,
        compiler_params=comm_params(number, 40),
        cost_estimate=cost_of(40),
        name="scatter_rows",
    )(own, other)


def rope_tables(places):
    half = HD // 2
    frequency = THETA ** (-(jnp.arange(half, dtype=F32) * 2.0) / HD)
    angles = places.astype(F32)[:, None] * frequency[None, :]
    cosine, sine = jnp.cos(angles), jnp.sin(angles)
    return jnp.concatenate([cosine, cosine], axis=1), jnp.concatenate([-sine, sine], axis=1)


def row_norm(tensor):
    factor = lax.rsqrt(jnp.mean(tensor * tensor, axis=-1, keepdims=True) + EPS)
    return tensor * factor, factor


def row_norm_back(unit, factor, gain, incoming):
    weighted = incoming * gain
    inner = jnp.mean(weighted * unit, axis=-1, keepdims=True)
    return factor * (weighted - unit * inner), jnp.sum(incoming * unit, axis=0)


def layer(
    ctx_size,
    dp_size,
    tokens,
    w_query,
    w_key,
    w_value,
    w_out,
    gain_query,
    gain_key,
    gain_attn,
    w_gate,
    w_up,
    w_down,
    gain_ffn,
    positions,
    image_starts,
    cotangent,
):
    C, Z = ctx_size, dp_size // 2
    A = 2 * C
    N = Z * A
    ctx, dp = lax.axis_index("ctx"), lax.axis_index("dp")
    core, z = lax.rem(dp, 2), lax.div(dp, 2)
    plane_at = core * C + ctx
    own_at = dp * C + ctx
    rows, width = tokens.shape
    ffn_width = w_gate.shape[1]
    shard = w_query.shape[0]
    down_shard = w_down.shape[0]
    seq_len = rows * C
    slice_width = width // A
    ffn_slice = ffn_width // A
    bits = [1 << b for b in range(C.bit_length() - 1)]
    planes = [[zz * A + p for p in range(A)] for zz in range(Z)]
    columns = [[zz * 2 + k for zz in range(Z)] for k in range(2)]

    def swap(x, bit):
        return lax.ppermute(x, AXES, [(i, i ^ bit) for i in range(N)])

    def swap_core(x):
        return swap(x, C)

    def ring(x):
        return lax.ppermute(x, AXES, [(i, (i + A) % N) for i in range(N)])

    def rows_of(x, at, count):
        return lax.dynamic_slice_in_dim(x, at, count, 0)

    def put(x, part, at):
        return lax.dynamic_update_slice_in_dim(x, part, at, 0)

    def gather_z_aside(x):
        return lax.all_gather(x, "dp", axis=0, tiled=True, axis_index_groups=columns)

    def scatter_z_aside(x):
        return lax.psum_scatter(
            x, "dp", scatter_dimension=0, tiled=True, axis_index_groups=columns
        )

    def exchange(x):
        return lax.all_to_all(x, AXES, 0, 0, tiled=True, axis_index_groups=planes)

    def sum_everywhere(x):
        for power in range(N.bit_length() - 1):
            x = x + swap(x, 1 << power)
        return x

    def sorted_cores(own, other):
        return jnp.where(core == 0, jnp.stack([own, other]), jnp.stack([other, own]))

    full_down = gather_z_aside(w_down)
    part = down_shard
    dealt = part % 128 == 0
    gains = jnp.stack([gain_query, gain_key, gain_attn, gain_ffn])
    gains = jnp.pad(gains, ((0, 12), (0, -shard % 128)))
    x_both, full_qkv, full_out, all_gains, *gate_up = first_gather(
        tokens, w_query, w_key, w_value, w_out, gains, w_gate, w_up, dealt, C, Z, 1
    )
    if dealt:
        gate_up = gate_up[0]
    else:
        gate_up = jnp.stack([w.reshape(shard, Z, A, part) for w in (w_gate, w_up)], axis=1)
        gate_up = exchange(gate_up.transpose(3, 0, 1, 2, 4).reshape(A * shard, 2 * ffn_slice))
    full_qkv, full_down, gate_up = lax.optimization_barrier((full_qkv, full_down, gate_up))
    full_gate_up = gather_z_aside(gate_up)
    full_out = full_out.reshape(width, width)
    all_gains = all_gains[:, :, :4, :shard].astype(F32).transpose(2, 0, 1, 3).reshape(4, width)
    head_gains = lax.dynamic_slice(all_gains, (0, plane_at * slice_width), (2, slice_width))
    head_gains = jnp.pad(head_gains, ((0, 6), (0, 0)))
    gain_a, gain_f = all_gains[2:3], all_gains[3:4]

    x_all = x_both.reshape(2 * seq_len, width)
    other_dp = dp + 1 - 2 * core
    places = jnp.concatenate(
        [rows_of(positions, dp * seq_len, seq_len), rows_of(positions, other_dp * seq_len, seq_len)]
    )
    starts = jnp.concatenate([rows_of(image_starts, dp, 1), rows_of(image_starts, other_dp, 1)])
    start_rows = jnp.repeat(starts, seq_len, axis=0)
    inside = (places[:, None] >= start_rows) & (places[:, None] < start_rows + IMG)
    limits = jnp.max(jnp.where(inside, start_rows + (IMG - 1), places[:, None]), axis=1)
    limit_column = limits[:, None]
    place_rows = places.reshape(2, 1, seq_len)
    cosine, sine = rope_tables(places)
    raw_q, raw_k, value, query_turned, key_turned, squares = project(
        x_all, full_qkv, head_gains, cosine, sine, C, 8
    )
    attended = attend(query_turned, key_turned, value, limit_column, place_rows, seq_len)
    by_core = sorted_cores(attended[:seq_len], attended[seq_len:])
    attended_own = (
        exchange(by_core.reshape(A * rows, slice_width))
        .reshape(A, rows, slice_width)
        .transpose(1, 0, 2)
        .reshape(rows, width)
    )
    attn_proj = dot(attended_own, full_out, 1, 0)
    attn_unit, attn_factor = row_norm(attn_proj)
    hidden = tokens.astype(F32) + attn_unit * gain_a

    h_both = gather_rows(hidden.astype(BF16), C, 2)
    h_own, h_other, h_all = h_both[0], h_both[1], h_both.reshape(2 * seq_len, width)

    def mix(h):
        pre = dot(h, full_gate_up, 1, 0)
        gate, up = pre[:, :ffn_slice], pre[:, ffn_slice:]
        return gate, up, (gate * jax.nn.sigmoid(gate) * up).astype(BF16)

    gate_other, up_other, mixed_other = mix(h_other)
    gate_own, up_own, mixed_own = mix(h_own)
    ffn_other = dot(mixed_other, full_down, 1, 0, BF16)
    ffn_own = dot(mixed_own, full_down, 1, 0, BF16)
    ffn_proj = scatter_rows(ffn_own, ffn_other, C, 4)
    ffn_unit, ffn_factor = row_norm(ffn_proj)
    output = (hidden + ffn_unit * gain_f).astype(BF16)

    grad_out = cotangent.astype(F32)
    grad_ffn, term_gain_ffn = row_norm_back(ffn_unit, ffn_factor, gain_f, grad_out)
    f_both = gather_rows(grad_ffn.astype(BF16), C, 3)
    f_own, f_other, f_all = f_both[0], f_both[1], f_both.reshape(2 * seq_len, width)
    mixed_all = jnp.concatenate([mixed_own, mixed_other], axis=0)
    term_down = dot(mixed_all, f_all, 0, 0, BF16)
    term_down, f_both = lax.optimization_barrier((term_down, f_both))
    f_own, f_other = f_both[0], f_both[1]
    grad_w_down = scatter_z_aside(term_down).astype(F32)

    def mix_back(f, gate, up):
        grad_mixed = dot(f, full_down, 1, 1)
        sig = jax.nn.sigmoid(gate)
        grad_gate = grad_mixed * up * sig * (1.0 + gate * (1.0 - sig))
        return jnp.concatenate([grad_gate.astype(BF16), (grad_mixed * (gate * sig)).astype(BF16)], axis=1)

    b_other = mix_back(f_other, gate_other, up_other)
    b_own = mix_back(f_own, gate_own, up_own)
    b_all = jnp.concatenate([b_own, b_other], axis=0)
    term_gate_up = dot(h_all, b_all, 0, 0, BF16)
    back_other = dot(b_other, full_gate_up, 1, 1, BF16)
    back_own = dot(b_own, full_gate_up, 1, 1, BF16)
    term_gate_up, back_own, back_other, grad_w_down = lax.optimization_barrier(
        (term_gate_up, back_own, back_other, grad_w_down)
    )
    grad_gate_up = scatter_z_aside(term_gate_up)
    grad_hidden = grad_out + scatter_rows(back_own, back_other, C, 5)

    grad_attn, term_gain_attn = row_norm_back(attn_unit, attn_factor, gain_a, grad_hidden)
    a_all = gather_rows(grad_attn.astype(BF16), C, 7).reshape(2 * seq_len, width)
    grad_attended = dot(
        a_all, rows_of(full_out, plane_at * slice_width, slice_width), 1, 1, BF16
    )
    term_out = dot(attended, a_all, 0, 0, BF16)
    grad_q, grad_k, grad_v = attend_back(
        query_turned, key_turned, value, grad_attended, limit_column, place_rows, seq_len
    )
    grad_raw, head_terms = project_back(
        grad_q, grad_k, grad_v, raw_q, raw_k, squares, head_gains, cosine, sine, C, 9
    )
    term_qkv = dot(x_all, grad_raw, 0, 0, BF16)
    last = jnp.concatenate(
        [term_qkv, term_out.reshape(width, slice_width)], axis=1
    )
    last, grad_raw, grad_gate_up = lax.optimization_barrier((last, grad_raw, grad_gate_up))
    last = scatter_z_aside(last)
    input_other = dot(grad_raw[seq_len:], full_qkv, 1, 1, BF16)
    input_own = dot(grad_raw[:seq_len], full_qkv, 1, 1, BF16)
    if dealt:
        grad_gate_up = return_rows(grad_gate_up, C, 2, Z, 10)
        *grad_gate_up, input_own, input_other = lax.optimization_barrier(
            (*grad_gate_up, input_own, input_other)
        )
    else:
        grad_gate_up = (
            exchange(grad_gate_up)
            .reshape(A, shard, 2, Z, part)
            .transpose(2, 1, 3, 0, 4)
            .reshape(2, shard, ffn_width)
        )
    grad_input = grad_hidden + scatter_rows(input_own, input_other, C, 6)
    grad_qkv = return_rows(last[:, : 3 * slice_width], C, 3, 1, 11)
    grad_w_out = lax.ppermute(
        last[:, 3 * slice_width :].reshape(shard, width),
        AXES,
        [(zz * A + p, p * Z + zz) for zz in range(Z) for p in range(A)],
    ).astype(F32)

    head_terms = lax.dynamic_update_slice(
        jnp.zeros((2, width), F32), head_terms[:2], (0, plane_at * slice_width)
    )
    gain_terms = jnp.concatenate([head_terms, term_gain_attn[None], term_gain_ffn[None]], axis=0)
    gain_sums = lax.dynamic_slice(sum_everywhere(gain_terms), (0, own_at * shard), (4, shard))

    return (
        output,
        grad_input,
        grad_qkv[0].astype(F32),
        grad_qkv[1].astype(F32),
        grad_qkv[2].astype(F32),
        grad_w_out,
        gain_sums[0],
        gain_sums[1],
        gain_sums[2],
        grad_gate_up[0].astype(F32),
        grad_gate_up[1].astype(F32),
        grad_w_down,
        gain_sums[3],
    )


def solution(mesh):
    split, line, copied = P(AXES, None), P(AXES), P()
    return jax.shard_map(
        functools.partial(layer, mesh.shape["ctx"], mesh.shape["dp"]),
        mesh=mesh,
        in_specs=(split,) * 5 + (line,) * 3 + (split,) * 3 + (line, copied, copied, split),
        out_specs=(split,) * 6 + (line,) * 3 + (split,) * 3 + (line,),
        check_vma=False,
    )
```

time: 1090 us -> 879 us (0.81)
  Pallas kernels: 36.4 us -> 537 us
  waiting for transfers between devices: 449 us -> 63.3 us
  other arithmetic: 146 us -> 28.9 us
  starting transfers between devices: 119 us -> 9.08 us
  local copies, waits for them, and re-layouts: 162 us -> 57.5 us
  between operations: 2.88 us -> 15.2 us
    pallas_call x0 -> x11, Pallas kernels: none -> 500 us  [the longest x1 162 us: first_gather(): pl.pallas_call(functools.partial(first_kernel, C, Z, dealt), out_shape=tu...]
    ppermute x24 -> x1, waiting for transfers between devices: 237 us -> 0.01 us  [layer(): lax.ppermute(last[:, 3 * slice_width:].reshape(shard, width), AXES, [(zz...]
    ppermute x72 -> x5, waiting for transfers between devices: 209 us -> 20.5 us  [swap(): return lax.ppermute(x, AXES, [(i, i ^ bit) for i in range(N)])]
    ppermute x72 -> x5, starting transfers between devices: 74.4 us -> 2.93 us  [swap(): return lax.ppermute(x, AXES, [(i, i ^ bit) for i in range(N)])]
    dynamic_update_slice x45 -> x1, local copies, waits for them, and re-layouts: 46.5 us -> 0.01 us  [layer(): lax.dynamic_update_slice(jnp.zeros((2, width), F32), head_terms[:2], (0,...]
    convert_element_type x25 -> x10, other arithmetic: 45.4 us -> 12 us  [the longest x1 2.79 us: layer(): grad_w_down = scatter_z_aside(term_down).astype(F32)]
    all_gather x0 -> x2, waiting for transfers between devices: none -> 27.8 us  [gather_z_aside(): lax.all_gather(x, 'dp', axis=0, tiled=True, axis_index_groups=columns)]
    unnamed x206 -> x142, local copies, waits for them, and re-layouts: 25.1 us -> 50.8 us
  transfers between devices with their start and end apart: 102 -> 12, of which waited for: 44 -> 7; matrix products, arithmetic and copies ran while one was open for 37% -> 16% of each run, Pallas kernels for 3% -> 52%
where the time goes in v2:
time: 879 us; the launch traced here: 871 us
  Pallas kernels  537 us (61%)
  matrix products  160 us (18%)
  waiting for transfers between devices  63.3 us (7%)
  local copies, waits for them, and re-layouts  57.5 us (7%)
  other arithmetic  28.9 us (3%)
  between operations  15.2 us (2%)
  starting transfers between devices  9.08 us (1%)
    pallas_call x1, Pallas kernels, first_gather(): pl.pallas_call(functools.partial(first_kernel, C, Z, dealt), out_shape=tu...  162 us
    dot_general x16, matrix products, dot(): lax.dot_general(left, right, (((left_dim,), (right_dim,)), ((), ())), pre...  160 us
    pallas_call x3, Pallas kernels, scatter_rows(): pl.pallas_call(functools.partial(scatter_kernel, C), out_shape=jax.ShapeD...  123 us
    pallas_call x3, Pallas kernels, gather_rows(): pl.pallas_call(functools.partial(gather_kernel, C), out_shape=jax.ShapeDt...  118 us
    unnamed x142, local copies, waits for them, and re-layouts  50.8 us
    pallas_call x2, Pallas kernels, return_rows(): pl.pallas_call(functools.partial(return_kernel, C, groups, blocks), out_s...  40 us
    pallas_call x1, Pallas kernels, project(): pl.pallas_call(functools.partial(project_kernel, C), out_shape=(raw, raw,...  33.4 us
    all_gather x2, waiting for transfers between devices, gather_z_aside(): lax.all_gather(x, 'dp', axis=0, tiled=True, axis_index_groups=columns)  27.8 us
  transfers between devices with their start and end apart: 12, of which 7 were waited for; matrix products, arithmetic and copies ran while one was open for 16% of the time, Pallas kernels for 52%

profile of v2, /device:TPU:0, one launch (start us, length us, event | category | flops | bytes accessed | tf_op | source)
XLA Modules:
  0.0 870.7 jit_solution(13971427698107516127)
XLA Ops:
  16.2 162.1 %first_gather.1 = (bf16[2,1024,2048]{2,1,0:T(8,128)(2,1)S(1)}, bf16[2048,768]{1,0:T(8,128)(2,1)S(1)}, bf16[4,8,64,2048]{3,2,1,0:T(8,128)(2,1)S(1)}, bf16[4,8,16,128]{3,2,1,0:T(8,128)(2,1)S(1)}, bf16[512,2048]{1,0:T(8,128)(2,1)}) custom-call(bf16[256,2048]{1,0:T(8,128)(2,1)S(1)} %copy-done.4, bf16[64,2048]{1,0:T(8,128)(2,1)S(1)} %copy-done.33, ...), custom_call_target="tpu_custom_call" | custom-call | flops 100000000 | bytes 1024 | tf_op jit(solution)/shard_map/first_gather/pallas_call | solution.py:509
  178.3 3.3 copy-done.3
  181.6 3.3 copy-done.16
  188.6 3.7 fusion.47
  193.0 33.4 %project.1 = (f32[2048,256]{1,0:T(8,128)}, f32[2048,256]{1,0:T(8,128)}, bf16[2048,256]{1,0:T(8,128)(2,1)S(1)}, bf16[2048,256]{1,0:T(8,128)(2,1)S(1)}, bf16[2048,...) custom-call(bf16[2048,2048]{1,0:T(8,128)(2,1)} %bitcast.80, bf16[2048,768]{1,0:T(8,128)(2,1)} %copy-done.21, ...), custom_call_target="tpu_custom_call" | custom-call | flops 18000000 | bytes 1024 | tf_op jit(solution)/shard_map/project/pallas_call | solution.py:622
  226.5 13.7 %attend.1 = bf16[2048,256]{1,0:T(8,128)(2,1)S(1)} custom-call(bf16[2048,256]{1,0:T(8,128)(2,1)S(1)} %get-tuple-element.55.q_ref, bf16[2048,256]{1,0:T(8,128)(2,1)S(1)} %get-tuple-element.56.k_ref, bf16[2048,256]{1,0:T(8,128)(2,1)S(1)} %get-tuple-element.57.v_ref, s32[2048,1]{1,0:T(8,128)S(1)} %bitcast.84, s32[2,1,1024]{2,1,0:T(1,128)S(1)} %pad_add_fusion.1.place_ref), custom_call_target="tpu_custom_call" | custom-call | flops 2147483648 | bytes 4194304 | tf_op jit(solution)/shard_map/attend/pallas_call | solution.py:75
  242.8 3.6 all-to-all-start
  246.9 14.2 %all-to-all-done = bf16[8,256,256]{1,2,0:T(8,128)(2,1)S(1)} async-done(((bf16[8,256,256]{1,2,0:T(8,128)(2,1)}), bf16[8,256,256]{1,2,0:T(8,128)(2,1)S(1)}, u32[]{:S(2)}, u32[]{:S(2)}) %all-to-all-start) | async-done | bytes 1048608 | tf_op jit(solution)/shard_map/all_to_all | solution.py:928
  261.2 6.0 multiply_reduce_fusion.3
  268.5 39.8 %gather_rows.3 = bf16[2,1024,2048]{2,1,0:T(8,128)(2,1)S(1)} custom-call(bf16[256,2048]{1,0:T(8,128)(2,1)S(1)} %fusion.44.x_ref), custom_call_target="tpu_custom_call" | custom-call | flops 40000000 | bytes 1024 | tf_op jit(solution)/shard_map/gather_rows/pallas_call | solution.py:320
  308.2 3.3 copy-done.12
  311.5 27.8 %all-gather.5.cloned.1.call-done = bf16[2048,2048]{1,0:T(8,128)(2,1)} async-done(((bf16[512,2048]{1,0:T(8,128)(2,1)}), bf16[2048,2048]{1,0:T(8,128)(2,1)}) %all-gather.5.cloned.1.call-update) | async-done | bytes 8388624 | tf_op jit(solution)/shard_map/all_gather | solution.py:920
  339.3 12.6 %fusion.24 = f32[1024,2048]{1,0:T(8,128)S(1)} fusion(bf16[2048,2048]{1,0:T(8,128)(2,1)} %all-gather.5.cloned.1.call-done, bf16[2,1024,2048]{2,1,0:T(8,128)(2,1)} %copy-done.12), kind=kOutput, calls=%fused_computation.25 | convolution fusion | flops 8589934592 | bytes 20971520 | tf_op jit(solution)/shard_map/dot_general | solution.py:24
  352.0 3.3 copy-done.52
  358.7 8.8 %fusion.26 = f32[1024,2048]{1,0:T(8,128)S(1)} fusion(bf16[2048,2048]{1,0:T(8,128)(2,1)S(1)} %copy-done.61, bf16[2,1024,2048]{2,1,0:T(8,128)(2,1)S(1)} %copy-done.13), kind=kOutput, calls=%fused_computation.27 | convolution fusion | flops 8589934592 | bytes 20971520 | tf_op jit(solution)/shard_map/dot_general | solution.py:24
  367.5 3.3 copy-done.51
  373.0 13.2 %fusion.71.other_ref = bf16[1024,2048]{1,0:T(8,128)(2,1)S(1)} fusion(bf16[1024,1024]{1,0:T(8,128)(2,1)S(1)} %multiply_convert_fusion.4, bf16[1024,2048]{1,0:T(8,128)(2,1)S(1)} %copy-done.62), kind=kOutput, calls=%fused_computation.123 | convolution fusion | flops 4294967296 | bytes 10485760 | tf_op jit(solution)/shard_map/dot_general | solution.py:24
  386.2 4.8 fusion.70.own_ref
  391.0 41.3 %scatter_rows.3 = f32[256,2048]{1,0:T(8,128)S(1)} custom-call(bf16[1024,2048]{1,0:T(8,128)(2,1)S(1)} %fusion.70.own_ref, bf16[1024,2048]{1,0:T(8,128)(2,1)S(1)} %fusion.71.other_ref), custom_call_target="tpu_custom_call" | custom-call | flops 40000000 | bytes 1024 | tf_op jit(solution)/shard_map/scatter_rows/pallas_call | solution.py:831
  434.4 39.1 %gather_rows.4 = bf16[2,1024,2048]{2,1,0:T(8,128)(2,1)S(1)} custom-call(bf16[256,2048]{1,0:T(8,128)(2,1)S(1)} %fusion.38.x_ref), custom_call_target="tpu_custom_call" | custom-call | flops 40000000 | bytes 1024 | tf_op jit(solution)/shard_map/gather_rows/pallas_call | solution.py:320
  473.5 3.3 copy-done.14
  476.8 11.0 %fusion.8 = bf16[1024,2048]{1,0:T(8,128)(2,1)} fusion(bf16[2048,2048]{1,0:T(8,128)(2,1)S(1)} %bitcast.79, bf16[1024,1024]{1,0:T(8,128)(2,1)S(1)} %multiply_convert_fusion.4, bf16[1024,1024]{1,0:T(8,128)(2,1)S(1)} %multiply_convert_fusion.5), kind=kOutput, calls=%fused_computation.8 | convolution fusion | flops 8598323200 | bytes 16777216 | tf_op jit(solution)/shard_map/dot_general | solution.py:24
  488.3 13.9 %multiply_convert_fusion.1 = (bf16[1024,1024]{1,0:T(8,128)(2,1)S(1)}, bf16[1024,1024]{1,0:T(8,128)(2,1)}) fusion(f32[1024,2048]{1,0:T(8,128)} %copy-done.52, bf16[1024,2048]{1,0:T(8,128)(2,1)} %all-gather.3.cloned.1.call-done, bf16[2,1024,2048]{2,1,0:T(8,128)(2,1)} %copy-done.14), kind=kOutput, calls=%fused_computation.30 | convolution fusion | flops 4308598784 | bytes 20971520 | tf_op jit(solution)/shard_map/dot_general | solution.py:24
  502.2 10.5 %multiply_convert_fusion.3 = (bf16[1024,1024]{1,0:T(8,128)(2,1)}, bf16[1024,1024]{1,0:T(8,128)(2,1)}) fusion(f32[1024,2048]{1,0:T(8,128)} %copy-done.51, bf16[1024,2048]{1,0:T(8,128)(2,1)S(1)} %copy-done.63, bf16[2,1024,2048]{2,1,0:T(8,128)(2,1)S(1)} %copy-done.15), kind=kOutput, calls=%fused_computation.33 | convolution fusion | flops 4308598784 | bytes 20971520 | tf_op jit(solution)/shard_map/dot_general | solution.py:24
  512.8 13.4 %fusion.16.other_ref = bf16[1024,2048]{1,0:T(8,128)(2,1)} fusion(bf16[2048,2048]{1,0:T(8,128)(2,1)} %all-gather.5.cloned.1.call-done, bf16[1024,1024]{1,0:T(8,128)(2,1)} %get-tuple-element.98, bf16[1024,1024]{1,0:T(8,128)(2,1)S(1)} %get-tuple-element.97), kind=kOutput, calls=%fused_computation.16 | convolution fusion | flops 8598323200 | bytes 16777216 | tf_op jit(solution)/shard_map/dot_general | solution.py:24
  526.2 12.6 %fusion.12.own_ref = bf16[1024,2048]{1,0:T(8,128)(2,1)} fusion(bf16[2048,2048]{1,0:T(8,128)(2,1)} %all-gather.5.cloned.1.call-done, bf16[1024,1024]{1,0:T(8,128)(2,1)S(1)} %copy-done.67, bf16[1024,1024]{1,0:T(8,128)(2,1)S(1)} %copy-done.66), kind=kOutput, calls=%fused_computation.12 | convolution fusion | flops 8598323200 | bytes 16777216 | tf_op jit(solution)/shard_map/dot_general | solution.py:24
  538.8 26.1 %fusion = bf16[2048,2048]{1,0:T(8,128)(2,1)} fusion(bf16[2048,2048]{1,0:T(8,128)(2,1)} %bitcast.78, bf16[1024,1024]{1,0:T(8,128)(2,1)} %get-tuple-element.98, bf16[1024,1024]{1,0:T(8,128)(2,1)} %copy-done.65, bf16[1024,1024]{1,0:T(8,128)(2,1)} %get-tuple-element.96, bf16[1024,1024]{1,0:T(8,128)(2,1)} %get-tuple-element.95), kind=kOutput, calls=%fused_computation | convolution fusion | flops 17213423616 | bytes 25165824 | tf_op jit(solution)/shard_map/dot_general | solution.py:24
  565.0 2.8 convert_element_type.81
  570.0 2.9 copy-done.20
  573.0 40.7 %scatter_rows.4 = f32[256,2048]{1,0:T(8,128)S(1)} custom-call(bf16[1024,2048]{1,0:T(8,128)(2,1)S(1)} %copy-done.20, bf16[1024,2048]{1,0:T(8,128)(2,1)S(1)} %copy-done.19), custom_call_target="tpu_custom_call" | custom-call | flops 40000000 | bytes 1024 | tf_op jit(solution)/shard_map/scatter_rows/pallas_call | solution.py:831
  617.8 38.9 %gather_rows.5 = bf16[2,1024,2048]{2,1,0:T(8,128)(2,1)S(1)} custom-call(bf16[256,2048]{1,0:T(8,128)(2,1)S(1)} %get-tuple-element.99.x_ref), custom_call_target="tpu_custom_call" | custom-call | flops 40000000 | bytes 1024 | tf_op jit(solution)/shard_map/gather_rows/pallas_call | solution.py:320
  656.8 3.3 copy-done
  660.0 2.3 fusion.73
  663.7 6.2 fusion.45.g_ref
  670.0 22.7 %attend_back.1 = (f32[2048,256]{1,0:T(8,128)}, f32[2048,256]{1,0:T(8,128)}, f32[2048,256]{1,0:T(8,128)}) custom-call(bf16[2048,256]{1,0:T(8,128)(2,1)S(1)} %copy-done.44, bf16[2048,256]{1,0:T(8,128)(2,1)S(1)} %copy-done.46, bf16[2048,256]{1,0:T(8,128)(2,1)S(1)} %copy-done.42, bf16[2048,256]{1,0:T(8,128)(2,1)S(1)} %fusion.45.g_ref, s32[2048,1]{1,0:T(8,128)S(1)} %bitcast.85, ...), custom_call_target="tpu_custom_call" | custom-call | flops 5368709120 | bytes 10485760 | tf_op jit(solution)/shard_map/attend_back/pallas_call | solution.py:96
  694.3 23.7 %project_back.1 = (bf16[2048,768]{1,0:T(8,128)(2,1)}, f32[8,256]{1,0:T(8,128)S(1)}) custom-call(f32[2048,256]{1,0:T(8,128)S(1)} %copy-done.24, f32[2048,256]{1,0:T(8,128)} %get-tuple-element.66.dk_ref, f32[2048,256]{1,0:T(8,128)} %get-tuple-element.67.dv_ref, f32[2048,256]{1,0:T(8,128)} %get-tuple-element.68.rq_ref, f32[2048,256]{1,0:T(8,128)} %get-tuple-element.69.rk_ref, ...), custom_call_target="tpu_custom_call" | custom-call | flops 15000000 | bytes 1024 | tf_op jit(solution)/shard_map/project_back/pallas_call | solution.py:685
  718.1 9.5 %fusion.72 = bf16[2048,768]{1,0:T(8,128)(2,1)S(1)} fusion(bf16[2048,2048]{1,0:T(8,128)(2,1)S(1)} %bitcast.83, bf16[2048,768]{1,0:T(8,128)(2,1)} %get-tuple-element.76), kind=kOutput, calls=%fused_computation.124 | convolution fusion | flops 6442450944 | bytes 14680064 | tf_op jit(solution)/shard_map/dot_general | solution.py:24
  727.6 2.6 pad_maximum_fusion
  732.3 2.6 collective-permute-done.1
  736.3 2.6 collective-permute-done.2
  740.3 7.1 collective-permute-done.4
  747.5 6.9 collective-permute-done.5
  756.6 26.3 %return_rows.2 = (bf16[64,8192]{1,0:T(8,128)(2,1)S(1)}, bf16[64,8192]{1,0:T(8,128)(2,1)S(1)}) custom-call(bf16[512,2048]{1,0:T(8,128)(2,1)S(1)} %copy-done.23), custom_call_target="tpu_custom_call" | custom-call | flops 20000000 | bytes 1024 | tf_op jit(solution)/shard_map/return_rows/pallas_call | solution.py:748
  784.9 5.2 fusion.40.other_ref
  790.2 3.7 fusion.42.own_ref
  793.9 41.2 %scatter_rows.5 = f32[256,2048]{1,0:T(8,128)S(1)} custom-call(bf16[1024,2048]{1,0:T(8,128)(2,1)S(1)} %fusion.42.own_ref, bf16[1024,2048]{1,0:T(8,128)(2,1)S(1)} %fusion.40.other_ref), custom_call_target="tpu_custom_call" | custom-call | flops 40000000 | bytes 1024 | tf_op jit(solution)/shard_map/scatter_rows/pallas_call | solution.py:831
  840.0 3.6 fusion.48
  846.7 13.7 %return_rows.3 = (bf16[64,2048]{1,0:T(8,128)(2,1)S(1)}, bf16[64,2048]{1,0:T(8,128)(2,1)S(1)}, bf16[64,2048]{1,0:T(8,128)(2,1)S(1)}) custom-call(bf16[512,768]{1,0:T(8,128)(2,1)S(1)} %slice.98.x_ref), custom_call_target="tpu_custom_call" | custom-call | flops 20000000 | bytes 1024 | tf_op jit(solution)/shard_map/return_rows/pallas_call | solution.py:748
  (213 shorter events, 55.2 us)
Async XLA Ops:
  7.2 180.4 %copy-start.60 = (s32[8,2]{0,1:T(2,128)S(1)}, s32[8,2]{0,1:T(2,128)}, u32[]{:S(2)}) copy-start(s32[8,2]{0,1:T(2,128)} %param.28) | copy-start | bytes 196
  7.2 179.5 %all-gather.3.cloned.1.call-start = ((), (), s32[]{:S(2)}) async-start(), calls=%async_computation.4 | async-start | bytes 5242880 | tf_op jit(solution)/shard_map/all_gather | solution.py:920
  7.9 331.4 %all-gather.5.cloned.1.call-start = ((), (), s32[]{:S(2)}) async-start(), calls=%async_computation.5 | async-start | bytes 10485760 | tf_op jit(solution)/shard_map/all_gather | solution.py:920
  188.5 37.9 %copy-start.31 = (s32[1,2048]{0,1:T(8,128)}, s32[1,2048]{0,1:T(8,128)S(1)}, u32[]{:S(2)}) copy-start(s32[1,2048]{0,1:T(8,128)S(1)} %copy.65) | copy-start | bytes 24580
  188.6 37.9 %copy-start.39 = (s32[2,1,1024]{2,1,0:T(1,128)}, s32[2,1,1024]{2,1,0:T(1,128)S(1)}, u32[]{:S(2)}) copy-start(s32[2,1,1024]{2,1,0:T(1,128)S(1)} %pad_add_fusion.1.place_ref) | copy-start | bytes 24580
  192.9 33.5 %copy-start.7 = (f32[2048,128]{1,0:T(8,128)}, f32[2048,128]{1,0:T(8,128)S(1)}, u32[]{:S(2)}) copy-start(f32[2048,128]{1,0:T(8,128)S(1)} %get-tuple-element.118.cos_ref) | copy-start | bytes 3145732
  193.0 33.5 %copy-start.9 = (f32[2048,128]{1,0:T(8,128)}, f32[2048,128]{1,0:T(8,128)S(1)}, u32[]{:S(2)}) copy-start(f32[2048,128]{1,0:T(8,128)S(1)} %get-tuple-element.119.sin_ref) | copy-start | bytes 3145732
  226.4 14.8 %copy-start.41 = (bf16[2048,256]{1,0:T(8,128)(2,1)}, bf16[2048,256]{1,0:T(8,128)(2,1)S(1)}, u32[]{:S(2)}) copy-start(bf16[2048,256]{1,0:T(8,128)(2,1)S(1)} %get-tuple-element.57.v_ref) | copy-start | bytes 3145732
  226.4 14.8 %copy-start.43 = (bf16[2048,256]{1,0:T(8,128)(2,1)}, bf16[2048,256]{1,0:T(8,128)(2,1)S(1)}, u32[]{:S(2)}) copy-start(bf16[2048,256]{1,0:T(8,128)(2,1)S(1)} %get-tuple-element.55.q_ref) | copy-start | bytes 3145732
  226.4 14.8 %copy-start.45 = (bf16[2048,256]{1,0:T(8,128)(2,1)}, bf16[2048,256]{1,0:T(8,128)(2,1)S(1)}, u32[]{:S(2)}) copy-start(bf16[2048,256]{1,0:T(8,128)(2,1)S(1)} %get-tuple-element.56.k_ref) | copy-start | bytes 3145732
  242.8 18.4 %all-to-all-start = ((bf16[8,256,256]{1,2,0:T(8,128)(2,1)}), bf16[8,256,256]{1,2,0:T(8,128)(2,1)S(1)}, u32[]{:S(2)}, u32[]{:S(2)}) async-start(bf16[8,256,256]{1,2,0:T(8,128)(2,1)} %copy.54), calls=%async_computation | async-start | bytes 2097152 | tf_op jit(solution)/shard_map/all_to_all | solution.py:928
  246.4 318.6 %reduce-scatter.4.cloned.1.call-start = ((), (), s32[]{:S(2)}) async-start(), calls=%async_computation.6 | async-start | bytes 5242880 | tf_op jit(solution)/shard_map/reduce_scatter | solution.py:923
  246.8 20.3 %copy-start.55 = (f32[2048]{0:T(1024)}, f32[2048]{0:T(1024)S(1)}, u32[]{:S(2)}) copy-start(f32[2048]{0:T(1024)S(1)} %mul.197) | copy-start | bytes 24580
  261.2 6.6 copy-start.5
  339.3 17.4 %copy-start.61 = (bf16[2048,2048]{1,0:T(8,128)(2,1)S(1)}, bf16[2048,2048]{1,0:T(8,128)(2,1)}, u32[]{:S(2)}) copy-start(bf16[2048,2048]{1,0:T(8,128)(2,1)} %all-gather.5.cloned.1.call-done) | copy-start | bytes 25165828
  390.9 41.6 %copy-start.49 = (bf16[256,2048]{1,0:T(8,128)(2,1)S(1)}, bf16[256,2048]{1,0:T(8,128)(2,1)}, u32[]{:S(2)}) copy-start(bf16[256,2048]{1,0:T(8,128)(2,1)} %param.29) | copy-start | bytes 3145732
  487.9 242.3 %reduce-scatter.6.cloned.1.call-start = ((), (), s32[]{:S(2)}) async-start(), calls=%async_computation.7 | async-start | bytes 10485760 | tf_op jit(solution)/shard_map/reduce_scatter | solution.py:923
  488.3 13.9 %copy-start.15 = (bf16[2,1024,2048]{2,1,0:T(8,128)(2,1)S(1)}, bf16[2,1024,2048]{2,1,0:T(8,128)(2,1)}, u32[]{:S(2)}) copy-start(bf16[2,1024,2048]{2,1,0:T(8,128)(2,1)} %copy-done.14) | copy-start | bytes 25165828
  488.3 13.9 %copy-start.63 = (bf16[1024,2048]{1,0:T(8,128)(2,1)S(1)}, bf16[1024,2048]{1,0:T(8,128)(2,1)}, u32[]{:S(2)}) copy-start(bf16[1024,2048]{1,0:T(8,128)(2,1)} %all-gather.3.cloned.1.call-done) | copy-start | bytes 12582916
  502.2 10.5 %copy-start.65 = (bf16[1024,1024]{1,0:T(8,128)(2,1)}, bf16[1024,1024]{1,0:T(8,128)(2,1)S(1)}, u32[]{:S(2)}) copy-start(bf16[1024,1024]{1,0:T(8,128)(2,1)S(1)} %get-tuple-element.97) | copy-start | bytes 6291460
  512.8 13.5 %copy-start.66 = (bf16[1024,1024]{1,0:T(8,128)(2,1)S(1)}, bf16[1024,1024]{1,0:T(8,128)(2,1)}, u32[]{:S(2)}) copy-start(bf16[1024,1024]{1,0:T(8,128)(2,1)} %get-tuple-element.95) | copy-start | bytes 6291460
  512.8 13.5 %copy-start.67 = (bf16[1024,1024]{1,0:T(8,128)(2,1)S(1)}, bf16[1024,1024]{1,0:T(8,128)(2,1)}, u32[]{:S(2)}) copy-start(bf16[1024,1024]{1,0:T(8,128)(2,1)} %get-tuple-element.96) | copy-start | bytes 6291460
  567.8 268.6 %reduce-scatter.8.cloned.1.call-start = ((), (), s32[]{:S(2)}) async-start(), calls=%async_computation.8 | async-start | bytes 5242880 | tf_op jit(solution)/shard_map/reduce_scatter | solution.py:923
  573.0 40.7 %copy-start.48 = (f32[256,2048]{1,0:T(8,128)S(1)}, f32[256,2048]{1,0:T(8,128)}, u32[]{:S(2)}) copy-start(f32[256,2048]{1,0:T(8,128)} %copy-done.47) | copy-start | bytes 6291460
  573.0 40.7 %copy-start.50 = (bf16[256,2048]{1,0:T(8,128)(2,1)S(1)}, bf16[256,2048]{1,0:T(8,128)(2,1)}, u32[]{:S(2)}) copy-start(bf16[256,2048]{1,0:T(8,128)(2,1)} %param.29) | copy-start | bytes 3145732
  573.0 40.8 %copy-start.56 = (f32[2048]{0:T(1024)S(1)}, f32[2048]{0:T(1024)}, u32[]{:S(2)}) copy-start(f32[2048]{0:T(1024)} %copy-done.55) | copy-start | bytes 24580
  573.0 40.8 %copy-start.59 = (f32[256]{0:T(256)S(1)}, f32[256]{0:T(256)}, u32[]{:S(2)}) copy-start(f32[256]{0:T(256)} %copy-done.58) | copy-start | bytes 3076
  617.8 42.2 %copy-start.18 = (bf16[2048,256]{1,0:T(8,128)(2,1)S(1)}, bf16[2048,256]{1,0:T(8,128)(2,1)}, u32[]{:S(2)}) copy-start(bf16[2048,256]{1,0:T(8,128)(2,1)} %copy-done.17) | copy-start | bytes 3145732
  663.7 6.2 copy-start.40
  663.7 6.2 copy-start.42
  663.7 6.2 copy-start.44
  663.7 6.2 copy-start.46
  663.7 54.3 %slice-start = ((s8[8388608]{0:T(1024)(128)(4,1)}), s8[4194304]{0:T(1024)(128)(4,1)S(1)}, s32[]{:S(2)}) async-start(s8[8388608]{0:T(1024)(128)(4,1)} %bitcast.81), calls=%async_computation.9 | async-start | bytes 8388608
  670.0 22.7 %copy-start.8 = (f32[2048,128]{1,0:T(8,128)S(1)}, f32[2048,128]{1,0:T(8,128)}, u32[]{:S(2)}) copy-start(f32[2048,128]{1,0:T(8,128)} %copy-done.7) | copy-start | bytes 3145732
  670.0 22.7 %copy-start.10 = (f32[2048,128]{1,0:T(8,128)S(1)}, f32[2048,128]{1,0:T(8,128)}, u32[]{:S(2)}) copy-start(f32[2048,128]{1,0:T(8,128)} %copy-done.9) | copy-start | bytes 3145732
  670.0 22.7 %copy-start.38 = (f32[8,256]{1,0:T(8,128)S(1)}, f32[8,256]{1,0:T(8,128)}, u32[]{:S(2)}) copy-start(f32[8,256]{1,0:T(8,128)} %copy-done.37) | copy-start | bytes 24580
  670.0 48.0 %slice-start.1 = ((s8[8388608]{0:T(1024)(128)(4,1)}), s8[4194304]{0:T(1024)(128)(4,1)S(1)}, s32[]{:S(2)}) async-start(s8[8388608]{0:T(1024)(128)(4,1)} %bitcast.81), calls=%async_computation.10 | async-start | bytes 8388608
  718.0 9.5 %copy-start.53 = (bf16[2048,256]{1,0:T(8,128)(2,1)S(1)}, bf16[2048,256]{1,0:T(8,128)(2,1)}, u32[]{:S(2)}) copy-start(bf16[2048,256]{1,0:T(8,128)(2,1)} %reshape.141) | copy-start | bytes 3145732
  730.2 54.8 %copy-start.22 = (bf16[2048,768]{1,0:T(8,128)(2,1)S(1)}, bf16[2048,768]{1,0:T(8,128)(2,1)}, u32[]{:S(2)}) copy-start(bf16[2048,768]{1,0:T(8,128)(2,1)} %copy-done.21) | copy-start | bytes 9437188
  730.9 4.0 collective-permute-start.1
  734.9 4.0 collective-permute-start.2
  738.9 1.3 collective-permute-start.3
  740.2 7.2 collective-permute-start.4
  747.4 7.0 collective-permute-start.5
  793.9 46.1 %copy-start.2 = (f32[256,2048]{1,0:T(8,128)S(1)}, f32[256,2048]{1,0:T(8,128)}, u32[]{:S(2)}) copy-start(f32[256,2048]{1,0:T(8,128)} %copy-done.1) | copy-start | bytes 6291460
  836.4 7.3 copy-start.30
  838.3 6.8 copy-start.28
  838.3 24.6 %collective-permute-start = (bf16[64,2048]{1,0:T(8,128)(2,1)}, bf16[64,2048]{1,0:T(8,128)(2,1)S(1)}, u32[]{:S(2)}, u32[]{:S(2)}) collective-permute-start(bf16[64,2048]{1,0:T(8,128)(2,1)} %reshape.142), channel_id=1, source_target_pairs={{0,0},{1,4},{2,8},{3,12},{4,16},{5,20},{6,24},{7,28},{8,1},{9,5},{... | collective-permute-start | bytes 786440 | tf_op jit(solution)/shard_map/ppermute | solution.py:1064
  (34 other events, 77.9 us)
Sparse Core Ops, SparseCore 0:
  9.6 138.6 all-gather.2
  186.8 152.5 all-gather.4
  488.0 74.0 reduce-scatter.3
  567.9 142.0 reduce-scatter.5
  730.3 75.4 reduce-scatter.7

commit v3 on v2

--- a/solution.py
+++ b/solution.py
@@ -134,11 +134,15 @@
     return found
 
 
-def greet(peers):
+def signal_barrier(peers):
     barrier = pltpu.get_barrier_semaphore()
     for peer in peers:
         pl.semaphore_signal(barrier, inc=1, device_id=peer, device_id_type=MESH)
-    pl.semaphore_wait(barrier, len(peers))
+    return barrier
+
+
+def greet(peers):
+    pl.semaphore_wait(signal_barrier(peers), len(peers))
 
 
 def remote(src, dst, sent, arrived, device):
@@ -209,19 +213,29 @@
             for half in range(2):
                 self.start(self.by_core(half, 0))
 
-    def finish(self):
+    def crossed(self, half, mask):
+        slot = self.from_over(flipped(self.ctx, mask), half)
+        remote(
+            slot,
+            slot,
+            self.core_sent.at[half, mask],
+            self.core_came.at[half, mask],
+            (self.twin, self.ctx),
+        ).wait_recv()
+
+    def sent(self):
         for copy in self.sends:
             copy.wait_send()
+
+    def finish(self):
+        self.sent()
         for half in range(2):
             for mask in range(self.C):
-                slot = self.from_over(flipped(self.ctx, mask), half)
-                remote(
-                    slot,
-                    slot,
-                    self.core_sent.at[half, mask],
-                    self.core_came.at[half, mask],
-                    (self.twin, self.ctx),
-                ).wait_recv()
+                self.crossed(half, mask)
+
+    def complete(self, index):
+        place = [{m: at for at, (m, _, _) in enumerate(tree)} for tree in self.trees]
+        return [m for m in range(self.C) if max(place[0][m], place[1][m]) == index]
 
 
 def rows_gather(C, x_ref, out_ref, sems):
@@ -241,45 +255,42 @@
     )
 
 
-class Spread:
-    def __init__(self, C, Z, x_ref, out_ref, own_sem, ring_sent, ring_came, sems):
+class Ring:
+    def __init__(self, Z, block, sent, came, way=1):
         dp, ctx, _ = places_of()
-        core = lax.rem(dp, 2)
-        self.Z, self.z, self.ctx = Z, lax.div(dp, 2), ctx
-        self.ahead, self.behind = lax.rem(dp + 2, 2 * Z), lax.rem(dp + 2 * Z - 2, 2 * Z)
-        self.out, self.place = out_ref, core * C + ctx
-        self.ring_sent, self.ring_came = ring_sent, ring_came
-        self.own = pltpu.make_async_copy(x_ref, out_ref.at[self.z, self.place], own_sem)
-        size = Z // 2
-
-        def slot(side, seat, half):
-            return out_ref.at[pl.ds(half * size, size), side * C + seat]
-
-        self.gather = Gather(
-            C,
-            lambda half: slot(core, ctx, half),
-            lambda seat, half: slot(core, seat, half),
-            lambda seat, half: slot(core, seat, half),
-            lambda seat, half: slot(1 - core, seat, half),
-            sems,
-        )
+        self.Z, self.z, self.block, self.sems, self.way = Z, lax.div(dp, 2), block, (sent, came), way
+        self.ahead = lax.rem(dp + 2 * Z + 2 * way, 2 * Z), ctx
+        self.behind = lax.rem(dp + 2 * Z - 2 * way, 2 * Z), ctx
 
     def hop(self, step):
-        block = self.out.at[lax.rem(self.z + self.Z - step, self.Z), self.place]
-        return remote(
-            block, block, self.ring_sent.at[step], self.ring_came.at[step], (self.ahead, self.ctx)
-        )
-
-    def hop_landed(self, step):
-        block = self.out.at[lax.rem(self.z + 2 * self.Z - 1 - step, self.Z), self.place]
-        remote(
-            block, block, self.ring_sent.at[step], self.ring_came.at[step], (self.behind, self.ctx)
-        ).wait_recv()
-
-    def finish(self):
+        spot = self.block(lax.rem(self.z + self.Z - self.way * step, self.Z))
+        return remote(spot, spot, self.sems[0].at[step], self.sems[1].at[step], self.ahead)
+
+    def landed(self, step):
+        spot = self.block(lax.rem(self.z + 2 * self.Z - self.way * (1 + step), self.Z))
+        remote(spot, spot, self.sems[0].at[step], self.sems[1].at[step], self.behind).wait_recv()
+
+    def sent(self):
         for step in range(self.Z - 1):
             self.hop(step).wait_send()
-        self.gather.finish()
+
+
+def lines_gather(C, line_ref, out_ref, sems):
+    dp, ctx, _ = places_of()
+    core = lax.rem(dp, 2)
+    size = line_ref.shape[0] // 2
+
+    def slot(side, seat, half):
+        return out_ref.at[pl.ds(half * size, size), side * C + seat]
+
+    return Gather(
+        C,
+        lambda half: line_ref.at[pl.ds(half * size, size)],
+        lambda seat, half: slot(core, seat, half),
+        lambda seat, half: slot(core, seat, half),
+        lambda seat, half: slot(1 - core, seat, half),
+        sems,
+    )
 
 
 def gather_sems(C):
@@ -400,49 +411,54 @@
     refs = refs[6:]
     if dealt:
         (wg_ref, wu_ref), refs = refs[:2], refs[2:]
-    x_out, w_out, wo_out, gains_out = refs[:4]
-    refs = refs[4:]
+    x_out, w_out, wo_out, gains_line, gains_out = refs[:5]
+    refs = refs[5:]
     if dealt:
         gu_out, refs = refs[0], refs[1:]
-    own_sem, gather_set, refs = refs[0], refs[1:5], refs[5:]
-    deal_set, (ring_sent, ring_came), refs = refs[:3], refs[3:5], refs[5:]
-    spread_sets, refs = (refs[:7], refs[7:14]), refs[14:]
+    own_sem, ring_sent, ring_came, gather_set, refs = refs[0], refs[1], refs[2], refs[3:7], refs[7:]
+    gains_set, deal_set, refs = refs[:4], refs[4:7], refs[7:]
     A = 2 * C
     dp, ctx, _ = places_of()
-    z = lax.div(dp, 2)
-    ahead, behind = lax.rem(dp + 2, 2 * Z), lax.rem(dp + 2 * Z - 2, 2 * Z)
-    greet([device for _, device in plane_peers(C)] + [(ahead, ctx), (behind, ctx)])
+    z, place = lax.div(dp, 2), lax.rem(dp, 2) * C + ctx
     shard = wq_ref.shape[0]
-    spreads = [
-        Spread(C, Z, x, out, sems[0], sems[1], sems[2], sems[3:])
-        for x, out, sems in ((gains_ref, gains_out, spread_sets[0]), (wo_ref, wo_out, spread_sets[1]))
+    rings = [
+        Ring(Z, lambda at: gains_line.at[at], ring_sent.at[0], ring_came.at[0]),
+        Ring(Z, lambda at: wo_out.at[at], ring_sent.at[1], ring_came.at[1]),
     ]
-    for spread in spreads:
-        spread.own.start()
+    size = A * shard // 2
+    for half, way in enumerate((1, -1)):
+        rings.append(
+            Ring(
+                Z,
+                lambda at, half=half: w_out.at[pl.ds(at * (A * shard) + half * size, size)],
+                ring_sent.at[2 + half],
+                ring_came.at[2 + half],
+                way,
+            )
+        )
+    greet([device for _, device in plane_peers(C)] + [rings[0].ahead, rings[0].behind])
+    lines = [
+        pltpu.make_async_copy(gains_ref, gains_line.at[z], own_sem.at[0]),
+        pltpu.make_async_copy(wo_ref, wo_out.at[z], own_sem.at[1]),
+    ]
+    for line in lines:
+        line.start()
     deal = Deal(
         C, (wq_ref, wk_ref, wv_ref), wq_ref.shape[1] // A, 1, w_out,
         lambda device: (device[0] * C + device[1]) * shard, *deal_set,
     )
     deal.start()
-    for spread in spreads:
-        spread.own.wait()
-        spread.hop(0).start()
+    for line, ring in zip(lines, rings):
+        line.wait()
+        ring.hop(0).start()
     count = x_ref.shape[0]
-    own = pltpu.make_async_copy(x_ref, x_out.at[0, pl.ds(ctx * count, count)], own_sem)
+    own = pltpu.make_async_copy(x_ref, x_out.at[0, pl.ds(ctx * count, count)], own_sem.at[2])
     own.start()
     gather = rows_gather(C, x_ref, x_out, gather_set)
     gather.step(0)
-
-    def ring(step):
-        block = w_out.at[pl.ds(lax.rem(z + Z - step, Z) * (A * shard), A * shard)]
-        return remote(block, block, ring_sent.at[step], ring_came.at[step], (ahead, ctx))
-
-    def ring_landed(step):
-        block = w_out.at[pl.ds(lax.rem(z + 2 * Z - 1 - step, Z) * (A * shard), A * shard)]
-        remote(block, block, ring_sent.at[step], ring_came.at[step], (behind, ctx)).wait_recv()
-
     deal.landed()
-    ring(0).start()
+    for ring in rings[2:]:
+        ring.hop(0).start()
     if dealt:
         columns = Deal(
             C, (wg_ref, wu_ref), wg_ref.shape[1] // (Z * A), Z, gu_out,
@@ -450,29 +466,30 @@
         )
         columns.start()
     for step in range(Z - 2):
-        for spread in spreads:
-            spread.hop_landed(step)
-            spread.hop(step + 1).start()
-        ring_landed(step)
-        ring(step + 1).start()
+        for ring in rings:
+            ring.landed(step)
+            ring.hop(step + 1).start()
         if step + 1 < C:
             gather.step(step + 1)
-    for spread in spreads:
-        spread.hop_landed(Z - 2)
+    for ring in rings[:2]:
+        ring.landed(Z - 2)
+    own_gains = pltpu.make_async_copy(gains_line, gains_out.at[:, place], own_sem.at[3])
+    own_gains.start()
     for index in range(Z - 1, C):
         gather.step(index)
+    gains = lines_gather(C, gains_line, gains_out, gains_set)
     for index in range(C):
-        for spread in spreads:
-            spread.gather.step(index)
+        gains.step(index)
     if dealt:
         columns.landed()
     own.wait()
+    own_gains.wait()
     gather.finish()
-    for spread in spreads:
-        spread.finish()
-    ring_landed(Z - 2)
-    for step in range(Z - 1):
-        ring(step).wait_send()
+    gains.finish()
+    for ring in rings[2:]:
+        ring.landed(Z - 2)
+    for ring in rings:
+        ring.sent()
 
 
 def first_gather(x, w_query, w_key, w_value, w_out, gains, w_gate, w_up, dealt, C, Z, number):
@@ -486,21 +503,16 @@
     outs = [
         shape(2, C * x.shape[0], width),
         shape(width, 3 * width // A),
-        shape(Z, A, shard, width),
+        shape(Z, shard, width),
+        shape(Z, *gains.shape),
         shape(Z, A, *gains.shape),
     ]
     operands = [x, w_query, w_key, w_value, w_out, gains]
-    spread = [
-        pltpu.SemaphoreType.DMA,
-        pltpu.SemaphoreType.DMA((Z,)),
-        pltpu.SemaphoreType.DMA((Z,)),
-    ] + gather_sems(C)
     scratch = (
-        [pltpu.SemaphoreType.DMA]
-        + gather_sems(C)
+        [pltpu.SemaphoreType.DMA((4,))]
+        + [pltpu.SemaphoreType.DMA((4, Z))] * 2
+        + gather_sems(C) * 2
         + deal_sems(C, 3)
-        + [pltpu.SemaphoreType.DMA((Z,))] * 2
-        + spread * 2
     )
     if dealt:
         operands += [w_gate, w_up]
@@ -512,7 +524,7 @@
         in_specs=[ANY] * len(operands),
         out_specs=(ANY,) * len(outs),
         scratch_shapes=scratch,
-        compiler_params=comm_params(number),
+        compiler_params=comm_params(number, 60),
         cost_estimate=cost_of(100),
         name="first_gather",
     )(*operands)
@@ -564,10 +576,16 @@
 
 
 def project_kernel(
-    C, x_ref, w_ref, gain_ref, cos_ref, sin_ref, rq_ref, rk_ref, v_ref, q_ref, k_ref, total,
-    stats, landing, sent, came,
+    C, x_ref, w_ref, gain_ref, cos_ref, sin_ref, line_ref,
+    rq_ref, rk_ref, v_ref, q_ref, k_ref, total, out_ref,
+    own_sem, ctx_sent, ctx_came, core_sent, core_came, stats, landing, sent, came,
 ):
     greet([device for _, device in plane_peers(C)])
+    dp, ctx, _ = places_of()
+    gather = lines_gather(C, line_ref, out_ref, (ctx_sent, ctx_came, core_sent, core_came))
+    own = pltpu.make_async_copy(line_ref, out_ref.at[:, lax.rem(dp, 2) * C + ctx], own_sem)
+    own.start()
+    gather.step(0)
     wide = rq_ref.shape[1]
     width = x_ref.shape[1]
     blocks = stats.shape[0]
@@ -587,6 +605,7 @@
 
     start_sum(C, stats, landing, sent, came)
     finish_sum(C, stats, landing, sent, came, total)
+    gather.step(1)
 
     @pl.loop(0, blocks)
     def _(block):
@@ -600,6 +619,11 @@
                 value = raw[here, lanes] * factor * gain_ref[which : which + 1, lanes]
                 out[here, lanes] = turned(value, cosine, sine).astype(BF16)
 
+    for index in range(2, C):
+        gather.step(index)
+    own.wait()
+    gather.finish()
+
 
 def plane_sum_scratch(C, blocks):
     return [
@@ -613,7 +637,7 @@
 VM = pl.BlockSpec(memory_space=pltpu.VMEM)
 
 
-def project(x, w, gains, cosine, sine, C, number):
+def project(x, w, gains, cosine, sine, lines, C, number):
     total, width = x.shape
     wide = w.shape[1] // 3
     blocks = total // ROWS
@@ -621,19 +645,24 @@
     low = jax.ShapeDtypeStruct((total, wide), BF16)
     return pl.pallas_call(
         functools.partial(project_kernel, C),
-        out_shape=(raw, raw, low, low, low, jax.ShapeDtypeStruct((blocks, 8, ROWS), F32)),
-        in_specs=[VM] * 5,
-        out_specs=(VM,) * 6,
-        scratch_shapes=plane_sum_scratch(C, blocks),
+        out_shape=(
+            raw, raw, low, low, low,
+            jax.ShapeDtypeStruct((blocks, 8, ROWS), F32),
+            jax.ShapeDtypeStruct((lines.shape[0], 2 * C) + lines.shape[1:], BF16),
+        ),
+        in_specs=[VM] * 5 + [ANY],
+        out_specs=(VM,) * 6 + (ANY,),
+        scratch_shapes=[pltpu.SemaphoreType.DMA] + gather_sems(C) + plane_sum_scratch(C, blocks),
         compiler_params=comm_params(number, 48),
         cost_estimate=cost_of(18),
         name="project",
-    )(x, w, gains, cosine, sine)
+    )(x, w, gains, cosine, sine, lines)
 
 
 def project_back_kernel(
-    C, dq_ref, dk_ref, dv_ref, rq_ref, rk_ref, total, gain_ref, cos_ref, sin_ref,
-    out_ref, term_ref, eq, ek, inner, stats, landing, sent, came,
+    C, dq_ref, dk_ref, dv_ref, rq_ref, rk_ref, total, gain_ref, cos_ref, sin_ref, known_ref,
+    out_ref, sum_ref, term_ref, own_terms, all_terms, terms_sent, terms_came,
+    eq, ek, inner, stats, landing, sent, came,
 ):
     greet([device for _, device in plane_peers(C)])
     wide = rq_ref.shape[1]
@@ -664,6 +693,14 @@
         stats[block] = pair_of_rows(*sums)
 
     start_sum(C, stats, landing, sent, came)
+    dp, ctx, _ = places_of()
+    lanes = pl.ds(pl.multiple_of(place_in_plane(C, (dp, ctx)) * wide, 128), wide)
+    own_terms[...] = known_ref[...]
+    own_terms[:, lanes] = own_terms[:, lanes] + term_ref[...]
+    for index, device in plane_peers(C):
+        remote(
+            own_terms, all_terms.at[index], terms_sent.at[index], terms_came.at[index], device
+        ).start()
     finish_sum(C, stats, landing, sent, came, inner)
 
     @pl.loop(0, blocks)
@@ -678,19 +715,32 @@
             out_ref[here, which * wide : (which + 1) * wide] = value.astype(BF16)
         out_ref[here, 2 * wide :] = dv_ref[here, :].astype(BF16)
 
-
-def project_back(dq, dk, dv, raw_q, raw_k, sums, gains, cosine, sine, C, number):
+    terms = own_terms[...]
+    for index, device in plane_peers(C):
+        remote(
+            own_terms, all_terms.at[index], terms_sent.at[index], terms_came.at[index], device
+        ).wait()
+        terms = terms + all_terms[index]
+    sum_ref[...] = terms
+
+
+def project_back(dq, dk, dv, raw_q, raw_k, sums, gains, cosine, sine, terms, C, number):
     total, wide = dq.shape
     blocks = total // ROWS
     return pl.pallas_call(
         functools.partial(project_back_kernel, C),
         out_shape=(
             jax.ShapeDtypeStruct((total, 3 * wide), BF16),
-            jax.ShapeDtypeStruct((8, wide), F32),
+            jax.ShapeDtypeStruct(terms.shape, F32),
         ),
-        in_specs=[VM] * 9,
+        in_specs=[VM] * 10,
         out_specs=(VM, VM),
         scratch_shapes=[
+            pltpu.VMEM((8, wide), F32),
+            pltpu.VMEM(terms.shape, F32),
+            pltpu.VMEM((2 * C,) + terms.shape, F32),
+            pltpu.SemaphoreType.DMA((2 * C,)),
+            pltpu.SemaphoreType.DMA((2 * C,)),
             pltpu.VMEM((total, wide), F32),
             pltpu.VMEM((total, wide), F32),
             pltpu.VMEM((blocks, 8, ROWS), F32),
@@ -699,27 +749,144 @@
         compiler_params=comm_params(number, 48),
         cost_estimate=cost_of(15),
         name="project_back",
-    )(dq, dk, dv, raw_q, raw_k, sums, gains, cosine, sine)
-
-
-def return_kernel(C, groups, blocks, x_ref, *refs):
-    outs, (landing, sent, came, own_sem) = refs[:groups], refs[groups:]
+    )(dq, dk, dv, raw_q, raw_k, sums, gains, cosine, sine, terms)
+
+
+def attention_out_kernel(
+    C, attended_ref, w_ref, tokens_ref, gain_ref, heads, proj, hidden_ref, h_out,
+    low, own_sem, part_sent, part_came, copy_sem, *sems,
+):
+    count, width = tokens_ref.shape
+    wide = width // (2 * C)
+    dp, ctx, _ = places_of()
+    here = place_in_plane(C, (dp, ctx))
+    peers = plane_peers(C)
+    greet([device for _, device in peers])
+
+    def columns(at):
+        return heads.at[:, pl.ds(pl.multiple_of(at * wide, 128), wide)]
+
+    own = pltpu.make_async_copy(attended_ref.at[pl.ds(ctx * count, count)], columns(here), own_sem)
+    own.start()
+    copies = []
+    for index, device in peers:
+        rows = pl.ds(index // C * (C * count) + device[1] * count, count)
+        copy = remote(
+            attended_ref.at[rows], columns(here), part_sent.at[index], part_came.at[index], device
+        )
+        copy.start()
+        copies.append(copy)
+    own.wait()
+    for index, device in peers:
+        spot = columns(place_in_plane(C, device))
+        remote(spot, spot, part_sent.at[index], part_came.at[index], device).wait_recv()
+    for copy in copies:
+        copy.wait_send()
+    outs, size = tiles(width, 512)
+
+    @pl.loop(0, outs)
+    def _(number):
+        lanes = at_tile(number, size)
+        proj[:, lanes] = dot(heads[...], w_ref[:, lanes], 1, 0)
+
+    chunks, chunk = tiles(count, 32)
+    gain = gain_ref[0:1, :]
+
+    @pl.loop(0, chunks)
+    def _(number):
+        rows = at_tile(number, chunk)
+        value = proj[rows, :]
+        factor = lax.rsqrt(jnp.mean(value * value, axis=-1, keepdims=True) + EPS)
+        hidden = tokens_ref[rows, :].astype(F32) + value * factor * gain
+        hidden_ref[rows, :] = hidden
+        low[rows, :] = hidden.astype(BF16)
+
+    gather = rows_gather(C, low, h_out, sems)
+    copy = pltpu.make_async_copy(low, h_out.at[0, pl.ds(ctx * count, count)], copy_sem)
+    for index in range(C):
+        gather.step(index)
+        if index == 0:
+            copy.start()
+    copy.wait()
+    gather.finish()
+
+
+def attention_out(attended, w, tokens, gain, C, number):
+    count, width = tokens.shape
+    whole = jax.ShapeDtypeStruct((count, width), F32)
+    return pl.pallas_call(
+        functools.partial(attention_out_kernel, C),
+        out_shape=(
+            jax.ShapeDtypeStruct((count, width), BF16),
+            whole,
+            whole,
+            jax.ShapeDtypeStruct((2, C * count, width), BF16),
+        ),
+        in_specs=[VM] * 4,
+        out_specs=(VM, VM, VM, ANY),
+        scratch_shapes=[
+            pltpu.VMEM((count, width), BF16),
+            pltpu.SemaphoreType.DMA,
+            pltpu.SemaphoreType.DMA((2 * C,)),
+            pltpu.SemaphoreType.DMA((2 * C,)),
+            pltpu.SemaphoreType.DMA,
+        ]
+        + gather_sems(C),
+        compiler_params=comm_params(number, 40),
+        cost_estimate=cost_of(60),
+        name="attention_out",
+    )(attended, w, tokens, gain)
+
+
+def return_kernel(C, Z, groups, blocks, carried, x_ref, *refs):
+    outs, refs = refs[:groups], refs[groups:]
+    if carried:
+        y_out, refs = refs[0], refs[1:]
+    landing, sent, came, own_sem = refs[:4]
     A = 2 * C
     shard = outs[0].shape[0]
     part = outs[0].shape[1] // (blocks * A)
+    wide = groups * blocks * part
     dp, ctx, _ = places_of()
     own_at = place_in_plane(C, (dp, ctx))
     peers = plane_peers(C)
-    greet([device for _, device in peers])
+    if not carried:
+        greet([device for _, device in peers])
+    else:
+        y_sent, y_came = refs[4:]
+        here = dp * C + ctx
+        target = own_at * Z + lax.div(dp, 2)
+        origin = lax.rem(here, Z) * A + lax.div(here, Z)
+        ahead = lax.div(target, C), lax.rem(target, C)
+        behind = lax.div(origin, C), lax.rem(origin, C)
+        y_ref = x_ref.at[:, pl.ds(wide, carried)]
+        carry = remote(y_ref, y_out, y_sent, y_came, ahead)
+
+        barrier = signal_barrier([device for _, device in peers])
+
+        @pl.when(target != here)
+        def _():
+            signal_barrier([ahead, behind])
+            pl.semaphore_wait(barrier, len(peers) + 2)
+            carry.start()
+
+        @pl.when(target == here)
+        def _():
+            pl.semaphore_wait(barrier, len(peers))
+
     own = pltpu.make_async_copy(
-        x_ref.at[pl.ds(own_at * shard, shard)], landing.at[own_at], own_sem
+        x_ref.at[pl.ds(own_at * shard, shard), pl.ds(0, wide)], landing.at[own_at], own_sem
     )
     own.start()
 
     def copy_to(index, device):
         rows = pl.ds(place_in_plane(C, device) * shard, shard)
         return remote(
-            x_ref.at[rows], landing.at[own_at], sent.at[index], came.at[index], device
+            x_ref.at[rows, pl.ds(0, wide)],
+            landing.at[own_at],
+            sent.at[index],
+            came.at[index],
+            device,
         )
 
     def landed(index, device):
@@ -739,110 +906,418 @@
                 lanes = (group * blocks + block) * part
                 to = (block * A + at) * part
                 outs[group][:, to : to + part] = landing[at, :, lanes : lanes + part]
-
-
-def return_rows(x, C, groups, blocks, number):
+    if carried:
+
+        @pl.when(target != here)
+        def _():
+            carry.wait()
+
+        @pl.when(target == here)
+        def _():
+            keep = pltpu.make_async_copy(y_ref, y_out, y_sent)
+            keep.start()
+            keep.wait()
+
+
+def return_rows(x, C, Z, groups, blocks, number, carried=0):
     A = 2 * C
     shard = x.shape[0] // A
-    width = x.shape[1] * A // groups
+    wide = x.shape[1] - carried
+    shapes = (jax.ShapeDtypeStruct((shard, wide * A // groups), x.dtype),) * groups
+    scratch = [
+        pltpu.VMEM((A, shard, wide), x.dtype),
+        pltpu.SemaphoreType.DMA((A,)),
+        pltpu.SemaphoreType.DMA((A,)),
+        pltpu.SemaphoreType.DMA,
+    ]
+    if carried:
+        shapes += (jax.ShapeDtypeStruct((x.shape[0], carried), x.dtype),)
+        scratch += [pltpu.SemaphoreType.DMA, pltpu.SemaphoreType.DMA]
     return pl.pallas_call(
-        functools.partial(return_kernel, C, groups, blocks),
-        out_shape=(jax.ShapeDtypeStruct((shard, width), x.dtype),) * groups,
+        functools.partial(return_kernel, C, Z, groups, blocks, carried),
+        out_shape=shapes,
         in_specs=[ANY],
-        out_specs=(VM,) * groups,
-        scratch_shapes=[
-            pltpu.VMEM((A, shard, x.shape[1]), x.dtype),
-            pltpu.SemaphoreType.DMA((A,)),
-            pltpu.SemaphoreType.DMA((A,)),
-            pltpu.SemaphoreType.DMA,
-        ],
+        out_specs=(VM,) * len(shapes),
+        scratch_shapes=scratch,
         compiler_params=comm_params(number, 24),
         cost_estimate=cost_of(20),
         name="return_rows",
     )(x)
 
 
-def scatter_kernel(
-    C, own_ref, other_ref, out_ref, own, twin_part, landing,
-    own_sem, core_sent, core_came, ctx_sent, ctx_came,
+class Scatter:
+    def __init__(self, C, count, own, other, twin_part, landing, sems, final):
+        self.C, self.count, self.half = C, count, count // 2
+        self.own, self.other, self.twin_part, self.landing = own, other, twin_part, landing
+        self.core_sent, self.core_came, self.ctx_sent, self.ctx_came = sems
+        self.dp, self.ctx, self.twin = places_of()
+        self.onward = [{m: (bits, bit) for m, bits, bit in tree(order)} for order in bit_orders(C)]
+        self.final = final
+
+    def rows(self, half, mask):
+        return pl.ds(flipped(self.ctx, mask) * self.count + half * self.half, self.half)
+
+    def block(self, mask):
+        return pl.ds(flipped(self.ctx, mask) * self.count, self.count)
+
+    def across(self, half, mask):
+        return remote(
+            self.other.at[self.rows(half, mask)],
+            self.twin_part.at[self.rows(half, mask)],
+            self.core_sent.at[half, mask],
+            self.core_came.at[half, mask],
+            (self.twin, self.ctx),
+        )
+
+    def back(self, half, mask, bit):
+        return remote(
+            self.own.at[self.rows(half, mask)],
+            self.landing.at[half, mask],
+            self.ctx_sent.at[half, mask],
+            self.ctx_came.at[half, mask],
+            (self.dp, flipped(self.ctx, bit)),
+        )
+
+    def settle(self, half, mask):
+        along, bit = self.onward[half][mask]
+        self.across(half, mask).wait_recv()
+        here = self.rows(half, mask)
+        total = self.own[here, :].astype(F32) + self.twin_part[here, :].astype(F32)
+        for came in along:
+            self.back(half, mask | came, came).wait_recv()
+            total = total + self.landing[half, mask | came].astype(F32)
+        if mask:
+            self.own[here, :] = total.astype(BF16)
+            self.back(half, mask, bit).start()
+        else:
+            self.final(half, total)
+
+    def order(self):
+        return sorted(range(self.C), key=lambda mask: (-bin(mask).count("1"), mask))
+
+    def run(self, compute):
+        waiting = []
+        for mask in self.order():
+            compute(1, mask)
+            for half in range(2):
+                self.across(half, mask).start()
+            compute(0, mask)
+            ready = [half for half in range(2) if mask and not self.onward[half][mask][0]]
+            for half in ready:
+                self.settle(half, mask)
+            for half, earlier in waiting:
+                self.settle(half, earlier)
+            waiting = [(half, mask) for half in range(2) if half not in ready]
+        for half, earlier in waiting:
+            self.settle(half, earlier)
+        for half in range(2):
+            for mask in range(self.C):
+                self.across(half, mask).wait_send()
+                if mask:
+                    self.back(half, mask, self.onward[half][mask][1]).wait_send()
+
+
+def scatter_scratch(C, count, width):
+    rows = pltpu.VMEM((C * count, width), BF16)
+    return [rows, rows, rows, pltpu.VMEM((2, C, count // 2, width), BF16)] + [
+        pltpu.SemaphoreType.DMA((2, C))
+    ] * 4
+
+
+def tiles(total, size):
+    size = min(total, size)
+    return total // size, size
+
+
+def at_tile(number, size, base=0):
+    return pl.ds(pl.multiple_of(base + number * size, size), size)
+
+
+def mix_kernel(h_ref, wgu_ref, gu_ref, mixed_ref, turned_ref):
+    ffn = mixed_ref.shape[1]
+    steps, tile = tiles(ffn, 256)
+    for number in range(steps):
+        first = slice(number * tile, (number + 1) * tile)
+        second = slice(ffn + number * tile, ffn + (number + 1) * tile)
+        gate = dot(h_ref[...], wgu_ref[:, first], 1, 0)
+        up = dot(h_ref[...], wgu_ref[:, second], 1, 0)
+        gu_ref[:, first] = gate.astype(BF16)
+        gu_ref[:, second] = up.astype(BF16)
+        mixed = gate * jax.nn.sigmoid(gate) * up
+        mixed_ref[:, first] = mixed.astype(BF16)
+        turned_ref[first, :] = mixed.T.astype(BF16)
+
+
+def mix(h, w_gate_up):
+    total, width = h.shape
+    ffn = w_gate_up.shape[1] // 2
+    rows = min(256, total)
+    return pl.pallas_call(
+        mix_kernel,
+        out_shape=(
+            jax.ShapeDtypeStruct((total, 2 * ffn), BF16),
+            jax.ShapeDtypeStruct((total, ffn), BF16),
+            jax.ShapeDtypeStruct((ffn, total), BF16),
+        ),
+        grid=(total // rows,),
+        in_specs=[
+            pl.BlockSpec((rows, width), lambda i: (i, 0)),
+            pl.BlockSpec((width, 2 * ffn), lambda i: (0, 0)),
+        ],
+        out_specs=(
+            pl.BlockSpec((rows, 2 * ffn), lambda i: (i, 0)),
+            pl.BlockSpec((rows, ffn), lambda i: (i, 0)),
+            pl.BlockSpec((ffn, rows), lambda i: (0, i)),
+        ),
+        compiler_params=pltpu.CompilerParams(vmem_limit_bytes=48 * 2**20),
+        cost_estimate=cost_of(20),
+        name="mix",
+    )(h, w_gate_up)
+
+
+def feed_forward_kernel(
+    C, mixed_ref, turned_ref, gu_ref, wd_ref, hidden_ref, cot_ref, gain_ref,
+    out_ref, f_out, b_out, down_ref, term_ref,
+    mixed_buf, proj, f_own, f_buf, turned_buf, gu_buf, b_buf, total,
+    mixed_sem, f_sem, turned_sem, gu_sem, b_sem, own_sem,
+    ctx_sent, ctx_came, core_sent, core_came,
+    own, other, twin_part, landing, *sems,
 ):
-    count = out_ref.shape[0]
+    greet(plane_neighbours(C))
+    count, width = hidden_ref.shape
+    ffn = wd_ref.shape[0]
+    seq = C * count
     half_rows = count // 2
-    dp, ctx, twin = places_of()
+
+    def final(half, value):
+        proj[pl.ds(half * half_rows, half_rows), :] = value
+
+    scatter = Scatter(C, count, own, other, twin_part, landing, sems, final)
+    sequence = [(side, mask) for mask in scatter.order() for side in (1, 0)]
+
+    def rows_of(side, mask):
+        return pl.ds(pl.multiple_of(side * seq + flipped(scatter.ctx, mask) * count, count), count)
+
+    def fetch(index):
+        return pltpu.make_async_copy(
+            mixed_ref.at[rows_of(*sequence[index])], mixed_buf.at[index % 2], mixed_sem.at[index % 2]
+        )
+
+    fetch(0).start()
+    steps, tile = tiles(ffn, 256)
+    outs, wide = tiles(width, 512)
+
+    def compute(side, mask):
+        index = sequence.index((side, mask))
+        slot = index % 2
+        fetch(index).wait()
+        if index + 1 < len(sequence):
+            fetch(index + 1).start()
+        target, here = (own, other)[side], scatter.block(mask)
+
+        @pl.loop(0, outs)
+        def _(number):
+            lanes = at_tile(number, wide)
+            target[here, lanes] = dot(mixed_buf[slot], wd_ref[:, lanes], 1, 0).astype(BF16)
+
+    scatter.run(compute)
+    gain = gain_ref[0:1, :]
+    term_ref[...] = jnp.zeros_like(term_ref)
+    chunks, chunk = tiles(count, 32)
+
+    @pl.loop(0, chunks)
+    def _(number):
+        here = at_tile(number, chunk)
+        value = proj[here, :]
+        factor = lax.rsqrt(jnp.mean(value * value, axis=-1, keepdims=True) + EPS)
+        unit = value * factor
+        out_ref[here, :] = (hidden_ref[here, :] + unit * gain).astype(BF16)
+        incoming = cot_ref[here, :].astype(F32)
+        weighted = incoming * gain
+        inner = jnp.mean(weighted * unit, axis=-1, keepdims=True)
+        f_own[here, :] = (factor * (weighted - unit * inner)).astype(BF16)
+        term_ref[0:1, :] += jnp.sum(incoming * unit, axis=0, keepdims=True)
+
+    gather = rows_gather(C, f_own, f_out, (ctx_sent, ctx_came, core_sent, core_came))
+    copy = pltpu.make_async_copy(f_own, f_out.at[0, pl.ds(scatter.ctx * count, count)], own_sem)
+    blocks = [
+        (side, mask, index)
+        for index in range(C)
+        for mask in gather.complete(index)
+        for side in (0, 1)
+    ]
+
+    def fetch_kept(number):
+        side, mask, _ = blocks[number]
+        slot, rows = number % 2, rows_of(side, mask)
+        return (
+            pltpu.make_async_copy(turned_ref.at[:, rows], turned_buf.at[slot], turned_sem.at[slot]),
+            pltpu.make_async_copy(gu_ref.at[rows], gu_buf.at[slot], gu_sem.at[slot]),
+        )
+
+    def fetch_grad(number):
+        side, mask, _ = blocks[number]
+        return pltpu.make_async_copy(
+            f_out.at[side, scatter.block(mask)], f_buf.at[number % 2], f_sem.at[number % 2]
+        )
+
+    def keep(number):
+        side, mask, _ = blocks[number]
+        return pltpu.make_async_copy(
+            b_buf.at[number % 2], b_out.at[rows_of(side, mask)], b_sem.at[number % 2]
+        )
+
+    def back(number, grads):
+        slot = number % 2
+        for arrived in fetch_kept(number):
+            arrived.wait()
+        if number >= 2:
+            keep(number - 2).wait()
+
+        @pl.loop(0, steps)
+        def _(at):
+            first, second = at_tile(at, tile), at_tile(at, tile, ffn)
+            grad = dot(grads[...], wd_ref[first, :], 1, 1)
+            gate, up = gu_buf[slot, :, first].astype(F32), gu_buf[slot, :, second].astype(F32)
+            sig = jax.nn.sigmoid(gate)
+            b_buf[slot, :, first] = (grad * up * sig * (1.0 + gate * (1.0 - sig))).astype(BF16)
+            b_buf[slot, :, second] = (grad * (gate * sig)).astype(BF16)
+
+        keep(number).start()
+
+        @pl.loop(0, outs)
+        def _(at):
+            lanes = at_tile(at, wide)
+            value = dot(turned_buf[slot], grads[:, lanes], 1, 0)
+            if number == 0:
+                total[:, lanes] = value
+            elif number < len(blocks) - 1:
+                total[:, lanes] += value
+            else:
+                down_ref[:, lanes] = (total[:, lanes] + value).astype(BF16)
+
+    for arriving in fetch_kept(0):
+        arriving.start()
+    done = 0
+    for index in range(C):
+        gather.step(index)
+        if index == 0:
+            copy.start()
+        while done < len(blocks) and blocks[done][2] == index:
+            side, mask, _ = blocks[done]
+            if done + 1 < len(blocks):
+                for arriving in fetch_kept(done + 1):
+                    arriving.start()
+            if (side, mask) == (0, 0):
+                back(done, f_own)
+            else:
+                if side:
+                    for half in range(2):
+                        gather.crossed(half, mask)
+                fetch_grad(done).start()
+                fetch_grad(done).wait()
+                back(done, f_buf.at[done % 2])
+            done += 1
+    for number in (len(blocks) - 2, len(blocks) - 1):
+        keep(number).wait()
+    copy.wait()
+    gather.sent()
+
+
+def feed_forward(mixed, turned_units, gate_up, w_down, hidden, cotangent, gain, C, number):
+    count, width = hidden.shape
+    total, ffn = 2 * C * count, w_down.shape[0]
+    pair = pltpu.SemaphoreType.DMA((2,))
+    return pl.pallas_call(
+        functools.partial(feed_forward_kernel, C),
+        out_shape=(
+            jax.ShapeDtypeStruct((count, width), BF16),
+            jax.ShapeDtypeStruct((2, C * count, width), BF16),
+            jax.ShapeDtypeStruct((total, 2 * ffn), BF16),
+            jax.ShapeDtypeStruct((ffn, width), BF16),
+            jax.ShapeDtypeStruct((8, width), F32),
+        ),
+        in_specs=[ANY] * 3 + [VM] * 4,
+        out_specs=(VM, ANY, ANY, VM, VM),
+        scratch_shapes=[
+            pltpu.VMEM((2, count, ffn), BF16),
+            pltpu.VMEM((count, width), F32),
+            pltpu.VMEM((count, width), BF16),
+            pltpu.VMEM((2, count, width), BF16),
+            pltpu.VMEM((2, ffn, count), BF16),
+            pltpu.VMEM((2, count, 2 * ffn), BF16),
+            pltpu.VMEM((2, count, 2 * ffn), BF16),
+            pltpu.VMEM((ffn, width), F32),
+            pair,
+            pair,
+            pair,
+            pair,
+            pair,
+            pltpu.SemaphoreType.DMA,
+        ]
+        + gather_sems(C)
+        + scatter_scratch(C, count, width),
+        compiler_params=comm_params(number, 60),
+        cost_estimate=cost_of(80),
+        name="feed_forward",
+    )(mixed, turned_units, gate_up, w_down, hidden, cotangent, gain)
+
+
+def back_scatter_kernel(
+    C, b_ref, w_ref, add_ref, out_ref, b_buf, b_sem, own, other, twin_part, landing, *sems
+):
     greet(plane_neighbours(C))
-    trees = [tree(order)[::-1] for order in bit_orders(C)]
-
-    def rows(half, mask):
-        return pl.ds(flipped(ctx, mask) * count + half * half_rows, half_rows)
-
-    def from_twin(half, mask):
-        return remote(
-            other_ref.at[rows(half, mask)],
-            twin_part.at[rows(half, mask)],
-            core_sent.at[half, mask],
-            core_came.at[half, mask],
-            (twin, ctx),
-        )
-
-    def local_copy(half, mask):
-        return pltpu.make_async_copy(
-            own_ref.at[rows(half, mask)], own.at[rows(half, mask)], own_sem.at[half, mask]
-        )
-
-    def onward(half, mask, bit):
-        return remote(
-            own.at[rows(half, mask)],
-            landing.at[half, mask],
-            ctx_sent.at[half, mask],
-            ctx_came.at[half, mask],
-            (dp, flipped(ctx, bit)),
-        )
-
-    for index in range(C):
-        for half in range(2):
-            mask = trees[half][index][0]
-            local_copy(half, mask).start()
-            from_twin(half, mask).start()
-    for index in range(C):
-        for half in range(2):
-            mask, along, bit = trees[half][index]
-            local_copy(half, mask).wait()
-            from_twin(half, mask).wait_recv()
-            here = rows(half, mask)
-            total = own[here, :].astype(F32) + twin_part[here, :].astype(F32)
-            for came in along:
-                onward(half, mask | came, came).wait_recv()
-                total = total + landing[half, mask | came].astype(F32)
-            if mask:
-                own[here, :] = total.astype(BF16)
-                onward(half, mask, bit).start()
-            else:
-                out_ref[pl.ds(half * half_rows, half_rows), :] = total
-    for half in range(2):
-        for mask, _, bit in trees[half]:
-            from_twin(half, mask).wait_send()
-            if mask:
-                onward(half, mask, bit).wait_send()
-
-
-def scatter_rows(own, other, C, number):
-    total, width = own.shape
-    count = total // C
+    count, width = out_ref.shape
+    seq = C * count
+    half_rows = count // 2
+
+    def final(half, total):
+        rows = pl.ds(half * half_rows, half_rows)
+        out_ref[rows, :] = total + add_ref[rows, :].astype(F32)
+
+    scatter = Scatter(C, count, own, other, twin_part, landing, sems, final)
+    sequence = [(side, mask) for mask in scatter.order() for side in (1, 0)]
+
+    def fetch(index):
+        side, mask = sequence[index]
+        rows = pl.ds(side * seq + flipped(scatter.ctx, mask) * count, count)
+        return pltpu.make_async_copy(b_ref.at[rows], b_buf.at[index % 2], b_sem.at[index % 2])
+
+    fetch(0).start()
+    outs, wide = tiles(width, 512)
+
+    def compute(side, mask):
+        index = sequence.index((side, mask))
+        slot = index % 2
+        fetch(index).wait()
+        if index + 1 < len(sequence):
+            fetch(index + 1).start()
+        target, here = (own, other)[side], scatter.block(mask)
+
+        @pl.loop(0, outs)
+        def _(number):
+            lanes = at_tile(number, wide)
+            target[here, lanes] = dot(b_buf[slot], w_ref[lanes, :], 1, 1).astype(BF16)
+
+    scatter.run(compute)
+
+
+def back_scatter(b, w, add, C, number):
+    count, width = add.shape
     return pl.pallas_call(
-        functools.partial(scatter_kernel, C),
+        functools.partial(back_scatter_kernel, C),
         out_shape=jax.ShapeDtypeStruct((count, width), F32),
-        in_specs=[ANY, ANY],
-        out_specs=pl.BlockSpec(memory_space=pltpu.VMEM),
+        in_specs=[ANY, VM, VM],
+        out_specs=VM,
         scratch_shapes=[
-            pltpu.VMEM((total, width), BF16),
-            pltpu.VMEM((total, width), BF16),
-            pltpu.VMEM((2, C, count // 2, width), BF16),
+            pltpu.VMEM((2, count, b.shape[1]), BF16),
+            pltpu.SemaphoreType.DMA((2,)),
         ]
-        + [pltpu.SemaphoreType.DMA((2, C))] * 5,
-        compiler_params=comm_params(number, 40),
-        cost_estimate=cost_of(40),
-        name="scatter_rows",
-    )(own, other)
+        + scatter_scratch(C, count, width),
+        compiler_params=comm_params(number, 48),
+        cost_estimate=cost_of(50),
+        name="back_scatter",
+    )(b, w, add)
 
 
 def rope_tables(places):
@@ -897,24 +1372,14 @@
     seq_len = rows * C
     slice_width = width // A
     ffn_slice = ffn_width // A
-    bits = [1 << b for b in range(C.bit_length() - 1)]
     planes = [[zz * A + p for p in range(A)] for zz in range(Z)]
     columns = [[zz * 2 + k for zz in range(Z)] for k in range(2)]
 
     def swap(x, bit):
         return lax.ppermute(x, AXES, [(i, i ^ bit) for i in range(N)])
 
-    def swap_core(x):
-        return swap(x, C)
-
-    def ring(x):
-        return lax.ppermute(x, AXES, [(i, (i + A) % N) for i in range(N)])
-
     def rows_of(x, at, count):
         return lax.dynamic_slice_in_dim(x, at, count, 0)
-
-    def put(x, part, at):
-        return lax.dynamic_update_slice_in_dim(x, part, at, 0)
 
     def gather_z_aside(x):
         return lax.all_gather(x, "dp", axis=0, tiled=True, axis_index_groups=columns)
@@ -927,20 +1392,11 @@
     def exchange(x):
         return lax.all_to_all(x, AXES, 0, 0, tiled=True, axis_index_groups=planes)
 
-    def sum_everywhere(x):
-        for power in range(N.bit_length() - 1):
-            x = x + swap(x, 1 << power)
-        return x
-
-    def sorted_cores(own, other):
-        return jnp.where(core == 0, jnp.stack([own, other]), jnp.stack([other, own]))
-
-    full_down = gather_z_aside(w_down)
     part = down_shard
     dealt = part % 128 == 0
     gains = jnp.stack([gain_query, gain_key, gain_attn, gain_ffn])
     gains = jnp.pad(gains, ((0, 12), (0, -shard % 128)))
-    x_both, full_qkv, full_out, all_gains, *gate_up = first_gather(
+    x_both, full_qkv, out_lines, _, all_gains, *gate_up = first_gather(
         tokens, w_query, w_key, w_value, w_out, gains, w_gate, w_up, dealt, C, Z, 1
     )
     if dealt:
@@ -948,9 +1404,8 @@
     else:
         gate_up = jnp.stack([w.reshape(shard, Z, A, part) for w in (w_gate, w_up)], axis=1)
         gate_up = exchange(gate_up.transpose(3, 0, 1, 2, 4).reshape(A * shard, 2 * ffn_slice))
-    full_qkv, full_down, gate_up = lax.optimization_barrier((full_qkv, full_down, gate_up))
+    full_qkv, gate_up = lax.optimization_barrier((full_qkv, gate_up))
     full_gate_up = gather_z_aside(gate_up)
-    full_out = full_out.reshape(width, width)
     all_gains = all_gains[:, :, :4, :shard].astype(F32).transpose(2, 0, 1, 3).reshape(4, width)
     head_gains = lax.dynamic_slice(all_gains, (0, plane_at * slice_width), (2, slice_width))
     head_gains = jnp.pad(head_gains, ((0, 6), (0, 0)))
@@ -968,65 +1423,34 @@
     limit_column = limits[:, None]
     place_rows = places.reshape(2, 1, seq_len)
     cosine, sine = rope_tables(places)
-    raw_q, raw_k, value, query_turned, key_turned, squares = project(
-        x_all, full_qkv, head_gains, cosine, sine, C, 8
-    )
+    raw_q, raw_k, value, query_turned, key_turned, squares, full_out = project(
+        x_all, full_qkv, head_gains, cosine, sine, out_lines, C, 8
+    )
+    full_out = full_out.reshape(width, width)
     attended = attend(query_turned, key_turned, value, limit_column, place_rows, seq_len)
-    by_core = sorted_cores(attended[:seq_len], attended[seq_len:])
-    attended_own = (
-        exchange(by_core.reshape(A * rows, slice_width))
-        .reshape(A, rows, slice_width)
-        .transpose(1, 0, 2)
-        .reshape(rows, width)
-    )
-    attn_proj = dot(attended_own, full_out, 1, 0)
+    attended_own, attn_proj, hidden, h_both = attention_out(
+        attended, full_out, tokens, jnp.pad(gain_a, ((0, 7), (0, 0))), C, 2
+    )
+
+    h_all = h_both.reshape(2 * seq_len, width)
+    full_gate_up, w_down, h_all = lax.optimization_barrier((full_gate_up, w_down, h_all))
+    full_down = gather_z_aside(w_down)
+    gate_up_low, mixed, turned_units = mix(h_all, full_gate_up)
+    output, f_both, b_all, term_down, term_gain_ffn = feed_forward(
+        mixed, turned_units, gate_up_low, full_down, hidden, cotangent,
+        jnp.pad(gain_f, ((0, 7), (0, 0))), C, 3,
+    )
+
+    term_down, b_all = lax.optimization_barrier((term_down, b_all))
+    grad_w_down = scatter_z_aside(term_down)
+    grad_hidden = back_scatter(b_all, full_gate_up, cotangent, C, 5)
+    term_gate_up = dot(h_all, b_all, 0, 0, BF16)
+    term_gate_up, grad_hidden, grad_w_down = lax.optimization_barrier(
+        (term_gate_up, grad_hidden, grad_w_down)
+    )
+    grad_gate_up = scatter_z_aside(term_gate_up)
+
     attn_unit, attn_factor = row_norm(attn_proj)
-    hidden = tokens.astype(F32) + attn_unit * gain_a
-
-    h_both = gather_rows(hidden.astype(BF16), C, 2)
-    h_own, h_other, h_all = h_both[0], h_both[1], h_both.reshape(2 * seq_len, width)
-
-    def mix(h):
-        pre = dot(h, full_gate_up, 1, 0)
-        gate, up = pre[:, :ffn_slice], pre[:, ffn_slice:]
-        return gate, up, (gate * jax.nn.sigmoid(gate) * up).astype(BF16)
-
-    gate_other, up_other, mixed_other = mix(h_other)
-    gate_own, up_own, mixed_own = mix(h_own)
-    ffn_other = dot(mixed_other, full_down, 1, 0, BF16)
-    ffn_own = dot(mixed_own, full_down, 1, 0, BF16)
-    ffn_proj = scatter_rows(ffn_own, ffn_other, C, 4)
-    ffn_unit, ffn_factor = row_norm(ffn_proj)
-    output = (hidden + ffn_unit * gain_f).astype(BF16)
-
-    grad_out = cotangent.astype(F32)
-    grad_ffn, term_gain_ffn = row_norm_back(ffn_unit, ffn_factor, gain_f, grad_out)
-    f_both = gather_rows(grad_ffn.astype(BF16), C, 3)
-    f_own, f_other, f_all = f_both[0], f_both[1], f_both.reshape(2 * seq_len, width)
-    mixed_all = jnp.concatenate([mixed_own, mixed_other], axis=0)
-    term_down = dot(mixed_all, f_all, 0, 0, BF16)
-    term_down, f_both = lax.optimization_barrier((term_down, f_both))
-    f_own, f_other = f_both[0], f_both[1]
-    grad_w_down = scatter_z_aside(term_down).astype(F32)
-
-    def mix_back(f, gate, up):
-        grad_mixed = dot(f, full_down, 1, 1)
-        sig = jax.nn.sigmoid(gate)
-        grad_gate = grad_mixed * up * sig * (1.0 + gate * (1.0 - sig))
-        return jnp.concatenate([grad_gate.astype(BF16), (grad_mixed * (gate * sig)).astype(BF16)], axis=1)
-
-    b_other = mix_back(f_other, gate_other, up_other)
-    b_own = mix_back(f_own, gate_own, up_own)
-    b_all = jnp.concatenate([b_own, b_other], axis=0)
-    term_gate_up = dot(h_all, b_all, 0, 0, BF16)
-    back_other = dot(b_other, full_gate_up, 1, 1, BF16)
-    back_own = dot(b_own, full_gate_up, 1, 1, BF16)
-    term_gate_up, back_own, back_other, grad_w_down = lax.optimization_barrier(
-        (term_gate_up, back_own, back_other, grad_w_down)
-    )
-    grad_gate_up = scatter_z_aside(term_gate_up)
-    grad_hidden = grad_out + scatter_rows(back_own, back_other, C, 5)
-
     grad_attn, term_gain_attn = row_norm_back(attn_unit, attn_factor, gain_a, grad_hidden)
     a_all = gather_rows(grad_attn.astype(BF16), C, 7).reshape(2 * seq_len, width)
     grad_attended = dot(
@@ -1036,22 +1460,20 @@
     grad_q, grad_k, grad_v = attend_back(
         query_turned, key_turned, value, grad_attended, limit_column, place_rows, seq_len
     )
-    grad_raw, head_terms = project_back(
-        grad_q, grad_k, grad_v, raw_q, raw_k, squares, head_gains, cosine, sine, C, 9
+    known = jnp.concatenate(
+        [jnp.zeros((2, width), F32), term_gain_attn[None], term_gain_ffn[:1], jnp.zeros((4, width), F32)]
+    )
+    grad_raw, gain_terms = project_back(
+        grad_q, grad_k, grad_v, raw_q, raw_k, squares, head_gains, cosine, sine, known, C, 9
     )
     term_qkv = dot(x_all, grad_raw, 0, 0, BF16)
-    last = jnp.concatenate(
-        [term_qkv, term_out.reshape(width, slice_width)], axis=1
-    )
-    last, grad_raw, grad_gate_up = lax.optimization_barrier((last, grad_raw, grad_gate_up))
+    last = jnp.concatenate([term_qkv, term_out.reshape(width, slice_width)], axis=1)
+    last, grad_raw, grad_gate_up, gain_terms = lax.optimization_barrier(
+        (last, grad_raw, grad_gate_up, gain_terms)
+    )
     last = scatter_z_aside(last)
-    input_other = dot(grad_raw[seq_len:], full_qkv, 1, 1, BF16)
-    input_own = dot(grad_raw[:seq_len], full_qkv, 1, 1, BF16)
     if dealt:
-        grad_gate_up = return_rows(grad_gate_up, C, 2, Z, 10)
-        *grad_gate_up, input_own, input_other = lax.optimization_barrier(
-            (*grad_gate_up, input_own, input_other)
-        )
+        grad_gate_up = return_rows(grad_gate_up, C, Z, 2, Z, 10)
     else:
         grad_gate_up = (
             exchange(grad_gate_up)
@@ -1059,19 +1481,17 @@
             .transpose(2, 1, 3, 0, 4)
             .reshape(2, shard, ffn_width)
         )
-    grad_input = grad_hidden + scatter_rows(input_own, input_other, C, 6)
-    grad_qkv = return_rows(last[:, : 3 * slice_width], C, 3, 1, 11)
-    grad_w_out = lax.ppermute(
-        last[:, 3 * slice_width :].reshape(shard, width),
-        AXES,
-        [(zz * A + p, p * Z + zz) for zz in range(Z) for p in range(A)],
-    ).astype(F32)
-
-    head_terms = lax.dynamic_update_slice(
-        jnp.zeros((2, width), F32), head_terms[:2], (0, plane_at * slice_width)
-    )
-    gain_terms = jnp.concatenate([head_terms, term_gain_attn[None], term_gain_ffn[None]], axis=0)
-    gain_sums = lax.dynamic_slice(sum_everywhere(gain_terms), (0, own_at * shard), (4, shard))
+    gain_terms = gain_terms[:4]
+    gain_terms = gain_terms + swap(gain_terms, A)
+    *grad_gate_up, gain_terms, grad_raw = lax.optimization_barrier(
+        (grad_gate_up[0].astype(F32), grad_gate_up[1].astype(F32), gain_terms, grad_raw)
+    )
+    for power in range(1, Z.bit_length() - 1):
+        gain_terms = gain_terms + swap(gain_terms, A << power)
+    grad_input = back_scatter(grad_raw, full_qkv, grad_hidden, C, 6)
+    last, grad_input = lax.optimization_barrier((last, grad_input))
+    *grad_qkv, grad_w_out = return_rows(last, C, Z, 3, 1, 11, slice_width)
+    gain_sums = lax.dynamic_slice(gain_terms, (0, own_at * shard), (4, shard))
 
     return (
         output,
@@ -1079,13 +1499,13 @@
         grad_qkv[0].astype(F32),
         grad_qkv[1].astype(F32),
         grad_qkv[2].astype(F32),
-        grad_w_out,
+        grad_w_out.reshape(shard, width).astype(F32),
         gain_sums[0],
         gain_sums[1],
         gain_sums[2],
-        grad_gate_up[0].astype(F32),
-        grad_gate_up[1].astype(F32),
-        grad_w_down,
+        grad_gate_up[0],
+        grad_gate_up[1],
+        grad_w_down.astype(F32),
         gain_sums[3],
     )
 

time: 879 us -> 780 us (0.89)
  matrix products: 160 us -> 41.3 us
  Pallas kernels: 537 us -> 583 us
  local copies, waits for them, and re-layouts: 57.5 us -> 26.9 us
  waiting for transfers between devices: 63.3 us -> 82.7 us
  other arithmetic: 28.9 us -> 19.5 us
    pallas_call x5 -> x7, Pallas kernels: 163 us -> 336 us  [the longest x1 107 us: feed_forward(): pl.pallas_call(functools.partial(feed_forward_kernel, C), out_shape=(jax....]
    dot_general x16 -> x4, matrix products: 160 us -> 41.3 us  [dot(): lax.dot_general(left, right, (((left_dim,), (right_dim,)), ((), ())), pre...]
    pallas_call x3 -> x1, Pallas kernels: 118 us -> 40.3 us  [gather_rows(): pl.pallas_call(functools.partial(gather_kernel, C), out_shape=jax.ShapeDt...]
    pallas_call x1, Pallas kernels: 162 us -> 88.3 us  [first_gather(): pl.pallas_call(functools.partial(first_kernel, C, Z, dealt), out_shape=tu...]
    unnamed x142 -> x60, local copies, waits for them, and re-layouts: 50.8 us -> 20 us
    all_gather x2, waiting for transfers between devices: 27.8 us -> 55.9 us  [gather_z_aside(): lax.all_gather(x, 'dp', axis=0, tiled=True, axis_index_groups=columns)]
    reduce_scatter x3, waiting for transfers between devices: 0.01 us -> 26.7 us  [scatter_z_aside(): lax.psum_scatter(x, 'dp', scatter_dimension=0, tiled=True, axis_index_gro...]
    pallas_call x1, Pallas kernels: 33.4 us -> 56.3 us  [project(): pl.pallas_call(functools.partial(project_kernel, C), out_shape=(raw, raw,...]
  transfers between devices with their start and end apart: 12 -> 7, of which waited for: 7 -> 4; matrix products, arithmetic and copies ran while one was open for 16% -> 8% of each run, Pallas kernels for 52% -> 48%
where the time goes in v3:
time: 780 us; the launch traced here: 772 us
  Pallas kernels  583 us (75%)
  waiting for transfers between devices  82.7 us (11%)
  matrix products  41.3 us (5%)
  local copies, waits for them, and re-layouts  26.9 us (3%)
  other arithmetic  19.5 us (2%)
  between operations  14.5 us (2%)
    pallas_call x1, Pallas kernels, feed_forward(): pl.pallas_call(functools.partial(feed_forward_kernel, C), out_shape=(jax....  107 us
    pallas_call x2, Pallas kernels, back_scatter(): pl.pallas_call(functools.partial(back_scatter_kernel, C), out_shape=jax.S...  96 us
    pallas_call x1, Pallas kernels, first_gather(): pl.pallas_call(functools.partial(first_kernel, C, Z, dealt), out_shape=tu...  88.3 us
    pallas_call x1, Pallas kernels, attention_out(): pl.pallas_call(functools.partial(attention_out_kernel, C), out_shape=(jax...  64.2 us
    pallas_call x1, Pallas kernels, project(): pl.pallas_call(functools.partial(project_kernel, C), out_shape=(raw, raw,...  56.3 us
    all_gather x2, waiting for transfers between devices, gather_z_aside(): lax.all_gather(x, 'dp', axis=0, tiled=True, axis_index_groups=columns)  55.9 us
    pallas_call x2, Pallas kernels, return_rows(): pl.pallas_call(functools.partial(return_kernel, C, Z, groups, blocks, car...  44.3 us
    dot_general x4, matrix products, dot(): lax.dot_general(left, right, (((left_dim,), (right_dim,)), ((), ())), pre...  41.3 us
  transfers between devices with their start and end apart: 7, of which 4 were waited for; matrix products, arithmetic and copies ran while one was open for 8% of the time, Pallas kernels for 48%

profile of v3, /device:TPU:0, one launch (start us, length us, event | category | flops | bytes accessed | tf_op | source)
XLA Modules:
  0.0 772.0 jit_solution(14843297968226575862)
XLA Ops:
  7.2 1.3 fusion.12.refs_5_
  8.5 88.3 %first_gather.1 = (bf16[2,1024,2048]{2,1,0:T(8,128)(2,1)}, bf16[2048,768]{1,0:T(8,128)(2,1)}, bf16[4,64,2048]{2,1,0:T(8,128)(2,1)}, bf16[4,16,128]{2,1,0:T(8,128...) custom-call(bf16[256,2048]{1,0:T(8,128)(2,1)} %tokens_ref.1, bf16[64,2048]{1,0:T(8,128)(2,1)} %refs_1_.1, ...), custom_call_target="tpu_custom_call" | custom-call | flops 100000000 | bytes 1024 | tf_op jit(solution)/shard_map/first_gather/pallas_call | solution.py:521
  98.6 0.9 convert_bitcast_fusion
  99.9 3.7 fusion.2
  104.2 56.3 %project.1 = (f32[2048,256]{1,0:T(8,128)}, f32[2048,256]{1,0:T(8,128)}, bf16[2048,256]{1,0:T(8,128)(2,1)S(1)}, bf16[2048,256]{1,0:T(8,128)(2,1)S(1)}, bf16[2048,...) custom-call(bf16[2048,2048]{1,0:T(8,128)(2,1)} %bitcast.41, ...), custom_call_target="tpu_custom_call" | custom-call | flops 18000000 | bytes 1024 | tf_op jit(solution)/shard_map/project/pallas_call | solution.py:646
  160.6 13.7 %attend.1.attended_ref = bf16[2048,256]{1,0:T(8,128)(2,1)S(1)} custom-call(bf16[2048,256]{1,0:T(8,128)(2,1)S(1)} %get-tuple-element.73.q_ref, bf16[2048,256]{1,0:T(8,128)(2,1)S(1)} %get-tuple-element.74.k_ref, bf16[2048,256]{1,0:T(8,128)(2,1)S(1)} %get-tuple-element.75.v_ref, s32[2048,1]{1,0:T(8,128)S(1)} %bitcast.37, s32[2,1,1024]{2,1,0:T(1,128)S(1)} %pad_add_fusion.1.place_ref), custom_call_target="tpu_custom_call" | custom-call | flops 2147483648 | bytes 4194304 | tf_op jit(solution)/shard_map/attend/pallas_call | solution.py:75
  174.4 64.2 %attention_out.1 = (bf16[256,2048]{1,0:T(8,128)(2,1)}, f32[256,2048]{1,0:T(8,128)S(1)}, f32[256,2048]{1,0:T(8,128)S(1)}, bf16[2,1024,2048]{2,1,0:T(8,128)(2,1)}) custom-call(bf16[2048,256]{1,0:T(8,128)(2,1)S(1)} %attend.1.attended_ref, bf16[2048,2048]{1,0:T(8,128)(2,1)} %bitcast.39, bf16[256,2048]{1,0:T(8,128)(2,1)S(1)} %copy-done.9, f32[8,2048]{1,0:T(8,128)S(1)} %pad.17.gain_ref), custom_call_target="tpu_custom_call" | custom-call | flops 60000000 | bytes 1024 | tf_op jit(solution)/shard_map/attention_out/pallas_call | solution.py:817
  238.6 1.3 copy-done.1
  239.9 1.0 copy-done.7
  240.9 1.3 copy-done.12
  242.2 2.8 all-gather.3.cloned.1.call-done.wgu_ref.w_ref
  246.0 24.6 %mix.1 = (bf16[2048,2048]{1,0:T(8,128)(2,1)}, bf16[2048,1024]{1,0:T(8,128)(2,1)S(1)}, bf16[1024,2048]{1,0:T(8,128)(2,1)}) custom-call(bf16[2048,2048]{1,0:T(8,128)(2,1)} %bitcast.43, bf16[2048,2048]{1,0:T(8,128)(2,1)} %all-gather.3.cloned.1.call-done.wgu_ref.w_ref), custom_call_target="tpu_custom_call" | custom-call | flops 20000000 | bytes 1024 | tf_op jit(solution)/shard_map/mix/pallas_call | solution.py:1055
  270.6 2.0 copy-done.11
  272.5 53.1 %all-gather.5.cloned.1.call-done.wd_ref = bf16[1024,2048]{1,0:T(8,128)(2,1)} async-done(((bf16[256,2048]{1,0:T(8,128)(2,1)}), bf16[1024,2048]{1,0:T(8,128)(2,1)}) %all-gather.5.cloned.1.call-update) | async-done | bytes 4194320 | tf_op jit(solution)/shard_map/all_gather | solution.py:1385
  325.6 107.4 %feed_forward.1 = (bf16[256,2048]{1,0:T(8,128)(2,1)}, bf16[2,1024,2048]{2,1,0:T(8,128)(2,1)}, bf16[2048,2048]{1,0:T(8,128)(2,1)}, bf16[1024,2048]{1,0:T(8,128)(2,1)}, f32[8,2048]{1,0:T(8,128)}) custom-call(bf16[2048,1024]{1,0:T(8,128)(2,1)} %copy-done.11, bf16[1024,2048]{1,0:T(8,128)(2,1)} %get-tuple-element.81.turned_ref, ...), custom_call_target="tpu_custom_call" | custom-call | flops 80000000 | bytes 1024 | tf_op jit(solution)/shard_map/feed_forward/pallas_call | solution.py:1231
  433.1 1.2 copy-done.10
  434.3 50.0 %back_scatter.2.add_ref = f32[256,2048]{1,0:T(8,128)S(1)} custom-call(bf16[2048,2048]{1,0:T(8,128)(2,1)} %get-tuple-element.89.b_ref, bf16[2048,2048]{1,0:T(8,128)(2,1)} %all-gather.3.cloned.1.call-done.wgu_ref.w_ref, bf16[256,2048]{1,0:T(8,128)(2,1)S(1)} %copy-done.10), custom_call_target="tpu_custom_call" | custom-call | flops 50000000 | bytes 1024 | tf_op jit(solution)/shard_map/back_scatter/pallas_call | solution.py:1307
  484.4 21.3 %fusion.19 = bf16[2048,2048]{1,0:T(8,128)(2,1)} fusion(bf16[2048,2048]{1,0:T(8,128)(2,1)} %bitcast.44, bf16[2048,2048]{1,0:T(8,128)(2,1)S(1)} %copy-done.24), kind=kOutput, calls=%fused_computation.52 | convolution fusion | flops 17179869184 | bytes 25165824 | tf_op jit(solution)/shard_map/dot_general | solution.py:24
  505.7 1.7 reduce-scatter.4.cloned.1.call-done
  507.6 2.0 multiply_reduce_fusion.2
  509.6 0.8 slice.38
  511.6 40.3 %gather_rows.1 = bf16[2,1024,2048]{2,1,0:T(8,128)(2,1)S(1)} custom-call(bf16[256,2048]{1,0:T(8,128)(2,1)S(1)} %multiply_convert_fusion.x_ref), custom_call_target="tpu_custom_call" | custom-call | flops 40000000 | bytes 1024 | tf_op jit(solution)/shard_map/gather_rows/pallas_call | solution.py:331
  551.9 3.2 copy-done
  555.1 3.3 fusion.21
  558.5 2.4 reshape.109
  560.9 6.3 fusion.g_ref
  567.3 22.7 %attend_back.1 = (f32[2048,256]{1,0:T(8,128)}, f32[2048,256]{1,0:T(8,128)}, f32[2048,256]{1,0:T(8,128)}) custom-call(bf16[2048,256]{1,0:T(8,128)(2,1)S(1)} %copy-done.21, bf16[2048,256]{1,0:T(8,128)(2,1)S(1)} %copy-done.23, bf16[2048,256]{1,0:T(8,128)(2,1)S(1)} %copy-done.19, bf16[2048,256]{1,0:T(8,128)(2,1)S(1)} %fusion.g_ref, s32[2048,1]{1,0:T(8,128)S(1)} %bitcast.38, ...), custom_call_target="tpu_custom_call" | custom-call | flops 5368709120 | bytes 10485760 | tf_op jit(solution)/shard_map/attend_back/pallas_call | solution.py:96
  589.9 1.6 copy-done.14
  591.5 25.3 %project_back.1 = (bf16[2048,768]{1,0:T(8,128)(2,1)}, f32[8,2048]{1,0:T(8,128)S(1)}) custom-call(f32[2048,256]{1,0:T(8,128)S(1)} %copy-done.14, f32[2048,256]{1,0:T(8,128)} %get-tuple-element.93.dk_ref, f32[2048,256]{1,0:T(8,128)} %get-tuple-element.94.dv_ref, f32[2048,256]{1,0:T(8,128)} %get-tuple-element.95.rq_ref, f32[2048,256]{1,0:T(8,128)} %get-tuple-element.96.rk_ref, ...), custom_call_target="tpu_custom_call" | custom-call | flops 15000000 | bytes 1024 | tf_op jit(solution)/shard_map/project_back/pallas_call | solution.py:730
  616.8 10.4 %fusion.20 = bf16[2048,768]{1,0:T(8,128)(2,1)S(1)} fusion(bf16[2048,2048]{1,0:T(8,128)(2,1)} %bitcast.42, bf16[2048,768]{1,0:T(8,128)(2,1)} %get-tuple-element.108.b_ref), kind=kOutput, calls=%fused_computation.53 | convolution fusion | flops 6442450944 | bytes 14680064 | tf_op jit(solution)/shard_map/dot_general | solution.py:24
  627.2 2.6 pad_maximum_fusion
  629.8 25.0 %reduce-scatter.6.cloned.1.call-done.x_ref = bf16[512,2048]{1,0:T(8,128)(2,1)} async-done(((bf16[2048,2048]{1,0:T(8,128)(2,1)}), bf16[512,2048]{1,0:T(8,128)(2,1)}) %reduce-scatter.6.cloned.1.call-update) | async-done | bytes 2097168 | tf_op jit(solution)/shard_map/reduce_scatter | solution.py:1388
  654.8 1.2 collective-permute-start
  656.0 1.6 copy-done.13
  657.6 26.3 %return_rows.2 = (bf16[64,8192]{1,0:T(8,128)(2,1)S(1)}, bf16[64,8192]{1,0:T(8,128)(2,1)S(1)}) custom-call(bf16[512,2048]{1,0:T(8,128)(2,1)S(1)} %copy-done.13), custom_call_target="tpu_custom_call" | custom-call | flops 20000000 | bytes 1024 | tf_op jit(solution)/shard_map/return_rows/pallas_call | solution.py:936
  684.0 1.5 convert_element_type.44
  685.4 1.5 convert_element_type.45
  686.9 2.5 collective-permute-start.1
  689.4 1.6 convert_element_type.51
  691.0 46.0 %back_scatter.3 = f32[256,2048]{1,0:T(8,128)S(1)} custom-call(bf16[2048,768]{1,0:T(8,128)(2,1)} %get-tuple-element.108.b_ref, bf16[2048,768]{1,0:T(8,128)(2,1)} %get-tuple-element.70.w_ref, f32[256,2048]{1,0:T(8,128)S(1)} %back_scatter.2.add_ref), custom_call_target="tpu_custom_call" | custom-call | flops 50000000 | bytes 1024 | tf_op jit(solution)/shard_map/back_scatter/pallas_call | solution.py:1307
  736.9 1.3 copy-done.5
  738.9 1.4 copy-done.17
  740.2 17.9 %return_rows.3 = (bf16[64,2048]{1,0:T(8,128)(2,1)S(1)}, bf16[64,2048]{1,0:T(8,128)(2,1)S(1)}, bf16[64,2048]{1,0:T(8,128)(2,1)S(1)}, bf16[512,256]{1,0:T(8,128)(2,1)S(1)}) custom-call(bf16[512,1024]{1,0:T(8,128)(2,1)S(1)} %copy-done.17), custom_call_target="tpu_custom_call" | custom-call | flops 20000000 | bytes 1024 | tf_op jit(solution)/shard_map/return_rows/pallas_call | solution.py:936
  758.2 0.8 convert_element_type.46
  759.0 0.8 convert_element_type.47
  760.7 0.9 reshape.110
  761.6 2.3 copy.52
  763.9 1.3 copy.53
  (98 shorter events, 6.7 us)
Async XLA Ops:
  7.2 237.8 %all-gather.3.cloned.1.call-start = ((), (), s32[]{:S(2)}) async-start(), calls=%async_computation.3 | async-start | bytes 10485760 | tf_op jit(solution)/shard_map/all_gather | solution.py:1385
  8.5 88.4 %copy-start.27 = (s32[8,2]{0,1:T(2,128)S(1)}, s32[8,2]{0,1:T(2,128)}, u32[]{:S(2)}) copy-start(s32[8,2]{0,1:T(2,128)} %param.28) | copy-start | bytes 196
  96.9 228.7 %all-gather.5.cloned.1.call-start = ((), (), s32[]{:S(2)}) async-start(), calls=%async_computation.4 | async-start | bytes 5242880 | tf_op jit(solution)/shard_map/all_gather | solution.py:1385
  98.6 62.0 %copy-start.15 = (s32[1,2048]{0,1:T(8,128)}, s32[1,2048]{0,1:T(8,128)S(1)}, u32[]{:S(2)}) copy-start(s32[1,2048]{0,1:T(8,128)S(1)} %copy.49) | copy-start | bytes 24580
  104.2 56.3 %copy-start.3 = (f32[2048,128]{1,0:T(8,128)}, f32[2048,128]{1,0:T(8,128)S(1)}, u32[]{:S(2)}) copy-start(f32[2048,128]{1,0:T(8,128)S(1)} %get-tuple-element.140.sin_ref) | copy-start | bytes 3145732
  160.6 13.8 %copy-start.18 = (bf16[2048,256]{1,0:T(8,128)(2,1)}, bf16[2048,256]{1,0:T(8,128)(2,1)S(1)}, u32[]{:S(2)}) copy-start(bf16[2048,256]{1,0:T(8,128)(2,1)S(1)} %get-tuple-element.75.v_ref) | copy-start | bytes 3145732
  160.6 13.8 %copy-start.20 = (bf16[2048,256]{1,0:T(8,128)(2,1)}, bf16[2048,256]{1,0:T(8,128)(2,1)S(1)}, u32[]{:S(2)}) copy-start(bf16[2048,256]{1,0:T(8,128)(2,1)S(1)} %get-tuple-element.73.q_ref) | copy-start | bytes 3145732
  160.6 13.8 %copy-start.22 = (bf16[2048,256]{1,0:T(8,128)(2,1)}, bf16[2048,256]{1,0:T(8,128)(2,1)S(1)}, u32[]{:S(2)}) copy-start(bf16[2048,256]{1,0:T(8,128)(2,1)S(1)} %get-tuple-element.74.k_ref) | copy-start | bytes 3145732
  160.6 13.8 %copy-start.9 = (bf16[256,2048]{1,0:T(8,128)(2,1)S(1)}, bf16[256,2048]{1,0:T(8,128)(2,1)}, u32[]{:S(2)}) copy-start(bf16[256,2048]{1,0:T(8,128)(2,1)} %tokens_ref.1) | copy-start | bytes 3145732
  238.6 1.3 copy-start.1
  239.9 1.0 copy-start.7
  240.9 1.3 copy-start.12
  245.1 262.4 %reduce-scatter.4.cloned.1.call-start = ((), (), s32[]{:S(2)}) async-start(), calls=%async_computation.5 | async-start | bytes 5242880 | tf_op jit(solution)/shard_map/reduce_scatter | solution.py:1388
  270.6 2.0 copy-start.11
  433.1 221.7 %reduce-scatter.6.cloned.1.call-start = ((), (), s32[]{:S(2)}) async-start(), calls=%async_computation.6 | async-start | bytes 10485760 | tf_op jit(solution)/shard_map/reduce_scatter | solution.py:1388
  433.1 1.2 copy-start.10
  434.3 50.1 %copy-start.24 = (bf16[2048,2048]{1,0:T(8,128)(2,1)S(1)}, bf16[2048,2048]{1,0:T(8,128)(2,1)}, u32[]{:S(2)}) copy-start(bf16[2048,2048]{1,0:T(8,128)(2,1)} %get-tuple-element.89.b_ref) | copy-start | bytes 25165828
  507.4 231.4 %reduce-scatter.8.cloned.1.call-start = ((), (), s32[]{:S(2)}) async-start(), calls=%async_computation.7 | async-start | bytes 5242880 | tf_op jit(solution)/shard_map/reduce_scatter | solution.py:1388
  507.6 2.8 copy-start.2
  511.6 43.5 %copy-start.8 = (bf16[2048,256]{1,0:T(8,128)(2,1)S(1)}, bf16[2048,256]{1,0:T(8,128)(2,1)}, u32[]{:S(2)}) copy-start(bf16[2048,256]{1,0:T(8,128)(2,1)} %copy-done.7) | copy-start | bytes 3145732
  551.9 3.2 copy-start
  560.9 6.3 copy-start.16
  560.9 6.3 copy-start.19
  560.9 6.3 copy-start.21
  560.9 6.3 copy-start.23
  567.2 22.7 %copy-start.4 = (f32[2048,128]{1,0:T(8,128)S(1)}, f32[2048,128]{1,0:T(8,128)}, u32[]{:S(2)}) copy-start(f32[2048,128]{1,0:T(8,128)} %copy-done.3) | copy-start | bytes 3145732
  589.9 1.6 copy-start.14
  616.8 10.4 %copy-start.25 = (bf16[2048,256]{1,0:T(8,128)(2,1)S(1)}, bf16[2048,256]{1,0:T(8,128)(2,1)}, u32[]{:S(2)}) copy-start(bf16[2048,256]{1,0:T(8,128)(2,1)} %reshape.109) | copy-start | bytes 3145732
  654.8 32.1 %collective-permute-start = (f32[4,2048]{1,0:T(4,128)S(1)}, f32[4,2048]{1,0:T(4,128)S(1)}, u32[]{:S(2)}, u32[]{:S(2)}) collective-permute-start(f32[4,2048]{1,0:T(4,128)S(1)} %slice.39), channel_id=1, source_target_pairs={{0,8},{1,9},{2,10},{3,11},{4,12},{5,13},{6,14},{7,15},{8,0},{9,1},... | collective-permute-start | bytes 98312 | tf_op jit(solution)/shard_map/ppermute | solution.py:1379
  656.0 1.6 copy-start.13
  684.0 5.4 copy-start.26
  686.9 51.4 %collective-permute-start.1 = (f32[4,2048]{1,0:T(4,128)S(1)}, f32[4,2048]{1,0:T(4,128)S(1)}, u32[]{:S(2)}, u32[]{:S(2)}) collective-permute-start(f32[4,2048]{1,0:T(4,128)S(1)} %slice_add_fusion), channel_id=1, source_target_pairs={{0,16},{1,17},{2,18},{3,19},{4,20},{5,21},{6,22},{7,23},{8,24},{9,... | collective-permute-start | bytes 98312 | tf_op jit(solution)/shard_map/ppermute | solution.py:1379
  736.9 1.3 copy-start.5
  738.9 25.0 %copy-start.6 = (f32[256,2048]{1,0:T(8,128)S(1)}, f32[256,2048]{1,0:T(8,128)}, u32[]{:S(2)}) copy-start(f32[256,2048]{1,0:T(8,128)} %copy-done.5) | copy-start | bytes 6291460
  738.9 1.4 copy-start.17
Sparse Core Ops, SparseCore 0:
  97.0 147.9 all-gather.2
  246.6 78.9 all-gather.4
  433.2 74.1 reduce-scatter.3
  509.7 144.9 reduce-scatter.5
  657.0 78.1 reduce-scatter.7

commit v4 on v3

--- a/solution.py
+++ b/solution.py
@@ -660,8 +660,8 @@
 
 
 def project_back_kernel(
-    C, dq_ref, dk_ref, dv_ref, rq_ref, rk_ref, total, gain_ref, cos_ref, sin_ref, known_ref,
-    out_ref, sum_ref, term_ref, own_terms, all_terms, terms_sent, terms_came,
+    C, dq_ref, dk_ref, dv_ref, rq_ref, rk_ref, total, gain_ref, cos_ref, sin_ref, known_ref, deal_ref,
+    out_ref, sum_ref, dealt_ref, deal_sent, deal_came, deal_own, term_ref, own_terms, all_terms, terms_sent, terms_came,
     eq, ek, inner, stats, landing, sent, came,
 ):
     greet([device for _, device in plane_peers(C)])
@@ -671,6 +671,30 @@
 
     def rows_at(block):
         return pl.ds(pl.multiple_of(block * ROWS, ROWS), ROWS)
+
+    Z, shard, _ = dealt_ref.shape
+    dp, ctx, _ = places_of()
+    line = dp - lax.rem(dp, 2)
+    seat = place_in_plane(C, (dp, ctx))
+
+    def deal(number):
+        at = seat * Z + number
+        to = lax.rem(at, 2 * C)
+        source, target = deal_ref.at[pl.ds(number * shard, shard)], dealt_ref.at[lax.div(at, 2 * C)]
+        device = line + lax.div(to, C), lax.rem(to, C)
+        away = remote(source, target, deal_sent.at[number], deal_came.at[lax.div(at, 2 * C)], device)
+        return to, away, pltpu.make_async_copy(source, target, deal_own.at[number])
+
+    for number in range(Z):
+        to, away, stay = deal(number)
+
+        @pl.when(to != seat)
+        def _():
+            away.start()
+
+        @pl.when(to == seat)
+        def _():
+            stay.start()
 
     def factors_of(block):
         return columns_of(lax.rsqrt(total[block] * (1.0 / width) + EPS))
@@ -693,8 +717,7 @@
         stats[block] = pair_of_rows(*sums)
 
     start_sum(C, stats, landing, sent, came)
-    dp, ctx, _ = places_of()
-    lanes = pl.ds(pl.multiple_of(place_in_plane(C, (dp, ctx)) * wide, 128), wide)
+    lanes = pl.ds(pl.multiple_of(seat * wide, 128), wide)
     own_terms[...] = known_ref[...]
     own_terms[:, lanes] = own_terms[:, lanes] + term_ref[...]
     for index, device in plane_peers(C):
@@ -722,9 +745,28 @@
         ).wait()
         terms = terms + all_terms[index]
     sum_ref[...] = terms
-
-
-def project_back(dq, dk, dv, raw_q, raw_k, sums, gains, cosine, sine, terms, C, number):
+    for number in range(Z):
+        to, away, stay = deal(number)
+
+        @pl.when(to != seat)
+        def _():
+            away.wait_send()
+
+        @pl.when(to == seat)
+        def _():
+            stay.wait()
+
+    for number in range(Z):
+        origin = lax.div(number * 2 * C + seat, Z)
+        spot = dealt_ref.at[number]
+        device = line + lax.div(origin, C), lax.rem(origin, C)
+
+        @pl.when(origin != seat)
+        def _():
+            remote(spot, spot, deal_sent.at[number], deal_came.at[number], device).wait_recv()
+
+
+def project_back(dq, dk, dv, raw_q, raw_k, sums, gains, cosine, sine, terms, dealt, C, Z, number):
     total, wide = dq.shape
     blocks = total // ROWS
     return pl.pallas_call(
@@ -732,10 +774,14 @@
         out_shape=(
             jax.ShapeDtypeStruct((total, 3 * wide), BF16),
             jax.ShapeDtypeStruct(terms.shape, F32),
+            jax.ShapeDtypeStruct((Z, dealt.shape[0] // Z, dealt.shape[1]), BF16),
         ),
-        in_specs=[VM] * 10,
-        out_specs=(VM, VM),
+        in_specs=[VM] * 10 + [ANY],
+        out_specs=(VM, VM, ANY),
         scratch_shapes=[
+            pltpu.SemaphoreType.DMA((Z,)),
+            pltpu.SemaphoreType.DMA((Z,)),
+            pltpu.SemaphoreType.DMA((Z,)),
             pltpu.VMEM((8, wide), F32),
             pltpu.VMEM(terms.shape, F32),
             pltpu.VMEM((2 * C,) + terms.shape, F32),
@@ -749,7 +795,7 @@
         compiler_params=comm_params(number, 48),
         cost_estimate=cost_of(15),
         name="project_back",
-    )(dq, dk, dv, raw_q, raw_k, sums, gains, cosine, sine, terms)
+    )(dq, dk, dv, raw_q, raw_k, sums, gains, cosine, sine, terms, dealt)
 
 
 def attention_out_kernel(
@@ -832,17 +878,14 @@
             pltpu.SemaphoreType.DMA,
         ]
         + gather_sems(C),
-        compiler_params=comm_params(number, 40),
+        compiler_params=comm_params(number, 60),
         cost_estimate=cost_of(60),
         name="attention_out",
     )(attended, w, tokens, gain)
 
 
-def return_kernel(C, Z, groups, blocks, carried, x_ref, *refs):
-    outs, refs = refs[:groups], refs[groups:]
-    if carried:
-        y_out, refs = refs[0], refs[1:]
-    landing, sent, came, own_sem = refs[:4]
+def return_kernel(C, groups, blocks, x_ref, *refs):
+    outs, (landing, sent, came, own_sem) = refs[:groups], refs[groups:]
     A = 2 * C
     shard = outs[0].shape[0]
     part = outs[0].shape[1] // (blocks * A)
@@ -850,30 +893,7 @@
     dp, ctx, _ = places_of()
     own_at = place_in_plane(C, (dp, ctx))
     peers = plane_peers(C)
-    if not carried:
-        greet([device for _, device in peers])
-    else:
-        y_sent, y_came = refs[4:]
-        here = dp * C + ctx
-        target = own_at * Z + lax.div(dp, 2)
-        origin = lax.rem(here, Z) * A + lax.div(here, Z)
-        ahead = lax.div(target, C), lax.rem(target, C)
-        behind = lax.div(origin, C), lax.rem(origin, C)
-        y_ref = x_ref.at[:, pl.ds(wide, carried)]
-        carry = remote(y_ref, y_out, y_sent, y_came, ahead)
-
-        barrier = signal_barrier([device for _, device in peers])
-
-        @pl.when(target != here)
-        def _():
-            signal_barrier([ahead, behind])
-            pl.semaphore_wait(barrier, len(peers) + 2)
-            carry.start()
-
-        @pl.when(target == here)
-        def _():
-            pl.semaphore_wait(barrier, len(peers))
-
+    greet([device for _, device in peers])
     own = pltpu.make_async_copy(
         x_ref.at[pl.ds(own_at * shard, shard), pl.ds(0, wide)], landing.at[own_at], own_sem
     )
@@ -906,39 +926,22 @@
                 lanes = (group * blocks + block) * part
                 to = (block * A + at) * part
                 outs[group][:, to : to + part] = landing[at, :, lanes : lanes + part]
-    if carried:
-
-        @pl.when(target != here)
-        def _():
-            carry.wait()
-
-        @pl.when(target == here)
-        def _():
-            keep = pltpu.make_async_copy(y_ref, y_out, y_sent)
-            keep.start()
-            keep.wait()
-
-
-def return_rows(x, C, Z, groups, blocks, number, carried=0):
+
+
+def return_rows(x, wide, C, groups, blocks, number):
     A = 2 * C
     shard = x.shape[0] // A
-    wide = x.shape[1] - carried
-    shapes = (jax.ShapeDtypeStruct((shard, wide * A // groups), x.dtype),) * groups
-    scratch = [
-        pltpu.VMEM((A, shard, wide), x.dtype),
-        pltpu.SemaphoreType.DMA((A,)),
-        pltpu.SemaphoreType.DMA((A,)),
-        pltpu.SemaphoreType.DMA,
-    ]
-    if carried:
-        shapes += (jax.ShapeDtypeStruct((x.shape[0], carried), x.dtype),)
-        scratch += [pltpu.SemaphoreType.DMA, pltpu.SemaphoreType.DMA]
     return pl.pallas_call(
-        functools.partial(return_kernel, C, Z, groups, blocks, carried),
-        out_shape=shapes,
+        functools.partial(return_kernel, C, groups, blocks),
+        out_shape=(jax.ShapeDtypeStruct((shard, wide * A // groups), x.dtype),) * groups,
         in_specs=[ANY],
-        out_specs=(VM,) * len(shapes),
-        scratch_shapes=scratch,
+        out_specs=(VM,) * groups,
+        scratch_shapes=[
+            pltpu.VMEM((A, shard, wide), x.dtype),
+            pltpu.SemaphoreType.DMA((A,)),
+            pltpu.SemaphoreType.DMA((A,)),
+            pltpu.SemaphoreType.DMA,
+        ],
         compiler_params=comm_params(number, 24),
         cost_estimate=cost_of(20),
         name="return_rows",
@@ -1069,20 +1072,32 @@
             pl.BlockSpec((rows, ffn), lambda i: (i, 0)),
             pl.BlockSpec((ffn, rows), lambda i: (0, i)),
         ),
-        compiler_params=pltpu.CompilerParams(vmem_limit_bytes=48 * 2**20),
+        compiler_params=pltpu.CompilerParams(vmem_limit_bytes=60 * 2**20),
         cost_estimate=cost_of(20),
         name="mix",
     )(h, w_gate_up)
 
 
 def feed_forward_kernel(
-    C, mixed_ref, turned_ref, gu_ref, wd_ref, hidden_ref, cot_ref, gain_ref,
-    out_ref, f_out, b_out, down_ref, term_ref,
-    mixed_buf, proj, f_own, f_buf, turned_buf, gu_buf, b_buf, total,
-    mixed_sem, f_sem, turned_sem, gu_sem, b_sem, own_sem,
+    C, mixed_ref, turned_ref, gu_ref, first_wd, second_wd, hidden_in, cot_in, gain_ref,
+    out_hbm, b_out, down_hbm, term_ref,
+    wd_ref, hidden_ref, cot_ref, out_ref,
+    mixed_buf, proj, f_own, f_all, turned_buf, gu_buf, b_buf, total,
+    mixed_sem, turned_sem, gu_sem, b_sem, down_sem, load_sem,
     ctx_sent, ctx_came, core_sent, core_came,
     own, other, twin_part, landing, *sems,
 ):
+    split = first_wd.shape[1]
+    loads = [
+        pltpu.make_async_copy(first_wd, wd_ref.at[:, pl.ds(0, split)], load_sem.at[0]),
+        pltpu.make_async_copy(
+            second_wd, wd_ref.at[:, pl.ds(split, second_wd.shape[1])], load_sem.at[1]
+        ),
+        pltpu.make_async_copy(hidden_in, hidden_ref, load_sem.at[2]),
+        pltpu.make_async_copy(cot_in, cot_ref, load_sem.at[3]),
+    ]
+    for load in loads:
+        load.start()
     greet(plane_neighbours(C))
     count, width = hidden_ref.shape
     ffn = wd_ref.shape[0]
@@ -1120,7 +1135,11 @@
             lanes = at_tile(number, wide)
             target[here, lanes] = dot(mixed_buf[slot], wd_ref[:, lanes], 1, 0).astype(BF16)
 
+    for load in loads[:2]:
+        load.wait()
     scatter.run(compute)
+    for load in loads[2:]:
+        load.wait()
     gain = gain_ref[0:1, :]
     term_ref[...] = jnp.zeros_like(term_ref)
     chunks, chunk = tiles(count, 32)
@@ -1131,15 +1150,15 @@
         value = proj[here, :]
         factor = lax.rsqrt(jnp.mean(value * value, axis=-1, keepdims=True) + EPS)
         unit = value * factor
-        out_ref[here, :] = (hidden_ref[here, :] + unit * gain).astype(BF16)
+        out_ref[here, :] = hidden_ref[here, :] + unit * gain
         incoming = cot_ref[here, :].astype(F32)
         weighted = incoming * gain
         inner = jnp.mean(weighted * unit, axis=-1, keepdims=True)
         f_own[here, :] = (factor * (weighted - unit * inner)).astype(BF16)
         term_ref[0:1, :] += jnp.sum(incoming * unit, axis=0, keepdims=True)
 
-    gather = rows_gather(C, f_own, f_out, (ctx_sent, ctx_came, core_sent, core_came))
-    copy = pltpu.make_async_copy(f_own, f_out.at[0, pl.ds(scatter.ctx * count, count)], own_sem)
+    gather = rows_gather(C, f_own, f_all, (ctx_sent, ctx_came, core_sent, core_came))
+    output = pltpu.make_async_copy(out_ref, out_hbm, load_sem.at[4])
     blocks = [
         (side, mask, index)
         for index in range(C)
@@ -1155,16 +1174,17 @@
             pltpu.make_async_copy(gu_ref.at[rows], gu_buf.at[slot], gu_sem.at[slot]),
         )
 
-    def fetch_grad(number):
-        side, mask, _ = blocks[number]
-        return pltpu.make_async_copy(
-            f_out.at[side, scatter.block(mask)], f_buf.at[number % 2], f_sem.at[number % 2]
-        )
-
     def keep(number):
         side, mask, _ = blocks[number]
         return pltpu.make_async_copy(
             b_buf.at[number % 2], b_out.at[rows_of(side, mask)], b_sem.at[number % 2]
+        )
+
+    def sum_out(at):
+        lanes = pl.ds(at * wide, wide)
+        rows = pl.ds(0, ffn)
+        return pltpu.make_async_copy(
+            other.at[rows, lanes], down_hbm.at[:, lanes], down_sem.at[at]
         )
 
     def back(number, grads):
@@ -1185,16 +1205,23 @@
 
         keep(number).start()
 
-        @pl.loop(0, outs)
-        def _(at):
-            lanes = at_tile(at, wide)
-            value = dot(turned_buf[slot], grads[:, lanes], 1, 0)
-            if number == 0:
-                total[:, lanes] = value
-            elif number < len(blocks) - 1:
-                total[:, lanes] += value
-            else:
-                down_ref[:, lanes] = (total[:, lanes] + value).astype(BF16)
+        if number < len(blocks) - 1:
+
+            @pl.loop(0, outs)
+            def _(at):
+                lanes = at_tile(at, wide)
+                value = dot(turned_buf[slot], grads[:, lanes], 1, 0)
+                if number == 0:
+                    total[:, lanes] = value
+                else:
+                    total[:, lanes] += value
+
+        else:
+            for at in range(outs):
+                lanes = slice(at * wide, (at + 1) * wide)
+                value = dot(turned_buf[slot], grads[:, lanes], 1, 0)
+                other[0:ffn, lanes] = (total[:, lanes] + value).astype(BF16)
+                sum_out(at).start()
 
     for arriving in fetch_kept(0):
         arriving.start()
@@ -1202,7 +1229,7 @@
     for index in range(C):
         gather.step(index)
         if index == 0:
-            copy.start()
+            output.start()
         while done < len(blocks) and blocks[done][2] == index:
             side, mask, _ = blocks[done]
             if done + 1 < len(blocks):
@@ -1214,36 +1241,39 @@
                 if side:
                     for half in range(2):
                         gather.crossed(half, mask)
-                fetch_grad(done).start()
-                fetch_grad(done).wait()
-                back(done, f_buf.at[done % 2])
+                back(done, f_all.at[side, scatter.block(mask)])
             done += 1
     for number in (len(blocks) - 2, len(blocks) - 1):
         keep(number).wait()
-    copy.wait()
+    for at in range(outs):
+        sum_out(at).wait()
+    output.wait()
     gather.sent()
 
 
 def feed_forward(mixed, turned_units, gate_up, w_down, hidden, cotangent, gain, C, number):
     count, width = hidden.shape
-    total, ffn = 2 * C * count, w_down.shape[0]
+    total, ffn = 2 * C * count, w_down[0].shape[0]
     pair = pltpu.SemaphoreType.DMA((2,))
     return pl.pallas_call(
         functools.partial(feed_forward_kernel, C),
         out_shape=(
-            jax.ShapeDtypeStruct((count, width), BF16),
-            jax.ShapeDtypeStruct((2, C * count, width), BF16),
+            jax.ShapeDtypeStruct((count, width), F32),
             jax.ShapeDtypeStruct((total, 2 * ffn), BF16),
             jax.ShapeDtypeStruct((ffn, width), BF16),
             jax.ShapeDtypeStruct((8, width), F32),
         ),
-        in_specs=[ANY] * 3 + [VM] * 4,
-        out_specs=(VM, ANY, ANY, VM, VM),
+        in_specs=[ANY] * 7 + [VM],
+        out_specs=(ANY, ANY, ANY, VM),
         scratch_shapes=[
+            pltpu.VMEM((ffn, width), BF16),
+            pltpu.VMEM((count, width), F32),
+            pltpu.VMEM((count, width), BF16),
+            pltpu.VMEM((count, width), F32),
             pltpu.VMEM((2, count, ffn), BF16),
             pltpu.VMEM((count, width), F32),
             pltpu.VMEM((count, width), BF16),
-            pltpu.VMEM((2, count, width), BF16),
+            pltpu.VMEM((2, C * count, width), BF16),
             pltpu.VMEM((2, ffn, count), BF16),
             pltpu.VMEM((2, count, 2 * ffn), BF16),
             pltpu.VMEM((2, count, 2 * ffn), BF16),
@@ -1252,20 +1282,27 @@
             pair,
             pair,
             pair,
-            pair,
-            pltpu.SemaphoreType.DMA,
+            pltpu.SemaphoreType.DMA((tiles(width, 512)[0],)),
+            pltpu.SemaphoreType.DMA((5,)),
         ]
         + gather_sems(C)
         + scatter_scratch(C, count, width),
         compiler_params=comm_params(number, 60),
         cost_estimate=cost_of(80),
         name="feed_forward",
-    )(mixed, turned_units, gate_up, w_down, hidden, cotangent, gain)
+    )(mixed, turned_units, gate_up, *w_down, hidden, cotangent, gain)
 
 
 def back_scatter_kernel(
-    C, b_ref, w_ref, add_ref, out_ref, b_buf, b_sem, own, other, twin_part, landing, *sems
+    C, b_ref, w_in, add_in, out_hbm, out_ref, out_sem, w_ref, add_ref, load_sem, b_buf, b_sem,
+    own, other, twin_part, landing, *sems,
 ):
+    loads = [
+        pltpu.make_async_copy(w_in, w_ref, load_sem.at[0]),
+        pltpu.make_async_copy(add_in, add_ref, load_sem.at[1]),
+    ]
+    for load in loads:
+        load.start()
     greet(plane_neighbours(C))
     count, width = out_ref.shape
     seq = C * count
@@ -1274,6 +1311,11 @@
     def final(half, total):
         rows = pl.ds(half * half_rows, half_rows)
         out_ref[rows, :] = total + add_ref[rows, :].astype(F32)
+        leave(half).start()
+
+    def leave(half):
+        rows = pl.ds(half * half_rows, half_rows)
+        return pltpu.make_async_copy(out_ref.at[rows], out_hbm.at[rows], out_sem.at[half])
 
     scatter = Scatter(C, count, own, other, twin_part, landing, sems, final)
     sequence = [(side, mask) for mask in scatter.order() for side in (1, 0)]
@@ -1299,7 +1341,11 @@
             lanes = at_tile(number, wide)
             target[here, lanes] = dot(b_buf[slot], w_ref[lanes, :], 1, 1).astype(BF16)
 
+    for load in loads:
+        load.wait()
     scatter.run(compute)
+    for half in range(2):
+        leave(half).wait()
 
 
 def back_scatter(b, w, add, C, number):
@@ -1307,9 +1353,14 @@
     return pl.pallas_call(
         functools.partial(back_scatter_kernel, C),
         out_shape=jax.ShapeDtypeStruct((count, width), F32),
-        in_specs=[ANY, VM, VM],
-        out_specs=VM,
+        in_specs=[ANY, ANY, ANY],
+        out_specs=ANY,
         scratch_shapes=[
+            pltpu.VMEM((count, width), F32),
+            pltpu.SemaphoreType.DMA((2,)),
+            pltpu.VMEM(w.shape, w.dtype),
+            pltpu.VMEM(add.shape, add.dtype),
+            pltpu.SemaphoreType.DMA((2,)),
             pltpu.VMEM((2, count, b.shape[1]), BF16),
             pltpu.SemaphoreType.DMA((2,)),
         ]
@@ -1392,6 +1443,8 @@
     def exchange(x):
         return lax.all_to_all(x, AXES, 0, 0, tiled=True, axis_index_groups=planes)
 
+    split = width * 3 // 4
+    first_down = gather_z_aside(w_down[:, :split])
     part = down_shard
     dealt = part % 128 == 0
     gains = jnp.stack([gain_query, gain_key, gain_attn, gain_ffn])
@@ -1404,7 +1457,10 @@
     else:
         gate_up = jnp.stack([w.reshape(shard, Z, A, part) for w in (w_gate, w_up)], axis=1)
         gate_up = exchange(gate_up.transpose(3, 0, 1, 2, 4).reshape(A * shard, 2 * ffn_slice))
-    full_qkv, gate_up = lax.optimization_barrier((full_qkv, gate_up))
+    second_down = w_down[:, split:]
+    full_qkv, gate_up, first_down, second_down = lax.optimization_barrier(
+        (full_qkv, gate_up, first_down, second_down)
+    )
     full_gate_up = gather_z_aside(gate_up)
     all_gains = all_gains[:, :, :4, :shard].astype(F32).transpose(2, 0, 1, 3).reshape(4, width)
     head_gains = lax.dynamic_slice(all_gains, (0, plane_at * slice_width), (2, slice_width))
@@ -1433,11 +1489,11 @@
     )
 
     h_all = h_both.reshape(2 * seq_len, width)
-    full_gate_up, w_down, h_all = lax.optimization_barrier((full_gate_up, w_down, h_all))
-    full_down = gather_z_aside(w_down)
+    full_gate_up, second_down, h_all = lax.optimization_barrier((full_gate_up, second_down, h_all))
+    second_down = gather_z_aside(second_down)
     gate_up_low, mixed, turned_units = mix(h_all, full_gate_up)
-    output, f_both, b_all, term_down, term_gain_ffn = feed_forward(
-        mixed, turned_units, gate_up_low, full_down, hidden, cotangent,
+    output, b_all, term_down, term_gain_ffn = feed_forward(
+        mixed, turned_units, gate_up_low, (first_down, second_down), hidden, cotangent,
         jnp.pad(gain_f, ((0, 7), (0, 0))), C, 3,
     )
 
@@ -1463,17 +1519,18 @@
     known = jnp.concatenate(
         [jnp.zeros((2, width), F32), term_gain_attn[None], term_gain_ffn[:1], jnp.zeros((4, width), F32)]
     )
-    grad_raw, gain_terms = project_back(
-        grad_q, grad_k, grad_v, raw_q, raw_k, squares, head_gains, cosine, sine, known, C, 9
+    grad_raw, gain_terms, term_out = project_back(
+        grad_q, grad_k, grad_v, raw_q, raw_k, squares, head_gains, cosine, sine, known, term_out,
+        C, Z, 9,
     )
     term_qkv = dot(x_all, grad_raw, 0, 0, BF16)
     last = jnp.concatenate([term_qkv, term_out.reshape(width, slice_width)], axis=1)
-    last, grad_raw, grad_gate_up, gain_terms = lax.optimization_barrier(
-        (last, grad_raw, grad_gate_up, gain_terms)
+    last, grad_raw, grad_gate_up, gain_terms, output, grad_w_down = lax.optimization_barrier(
+        (last, grad_raw, grad_gate_up, gain_terms, output.astype(BF16), grad_w_down.astype(F32))
     )
     last = scatter_z_aside(last)
     if dealt:
-        grad_gate_up = return_rows(grad_gate_up, C, Z, 2, Z, 10)
+        grad_gate_up = return_rows(grad_gate_up, 2 * ffn_slice, C, 2, Z, 10)
     else:
         grad_gate_up = (
             exchange(grad_gate_up)
@@ -1490,7 +1547,8 @@
         gain_terms = gain_terms + swap(gain_terms, A << power)
     grad_input = back_scatter(grad_raw, full_qkv, grad_hidden, C, 6)
     last, grad_input = lax.optimization_barrier((last, grad_input))
-    *grad_qkv, grad_w_out = return_rows(last, C, Z, 3, 1, 11, slice_width)
+    grad_qkv = return_rows(last, 3 * slice_width, C, 3, 1, 11)
+    grad_w_out = last[:, 3 * slice_width :]
     gain_sums = lax.dynamic_slice(gain_terms, (0, own_at * shard), (4, shard))
 
     return (
@@ -1505,7 +1563,7 @@
         gain_sums[2],
         grad_gate_up[0],
         grad_gate_up[1],
-        grad_w_down.astype(F32),
+        grad_w_down,
         gain_sums[3],
     )
 

time: 780 us -> 759 us (0.973)
  waiting for transfers between devices: 82.7 us -> 33.4 us
  Pallas kernels: 583 us -> 618 us
  local copies, waits for them, and re-layouts: 26.9 us -> 18.2 us
    all_gather x2 -> x3, waiting for transfers between devices: 55.9 us -> 4.5 us  [gather_z_aside(): lax.all_gather(x, 'dp', axis=0, tiled=True, axis_index_groups=columns)]
    pallas_call x1, Pallas kernels: 88.3 us -> 134 us  [first_gather(): pl.pallas_call(functools.partial(first_kernel, C, Z, dealt), out_shape=tu...]
    unnamed x60 -> x51, local copies, waits for them, and re-layouts: 20 us -> 8.05 us
    pallas_call x1, Pallas kernels: 107 us -> 97.9 us  [feed_forward(): pl.pallas_call(functools.partial(feed_forward_kernel, C), out_shape=(jax....]
  transfers between devices with their start and end apart: 7 -> 8, of which waited for: 4 -> 4; matrix products, arithmetic and copies ran while one was open for 8% -> 9% of each run, Pallas kernels for 48% -> 68%
where the time goes in v4:
time: 759 us; the launch traced here: 750 us
  Pallas kernels  618 us (81%)
  matrix products  39.1 us (5%)
  waiting for transfers between devices  33.4 us (4%)
  other arithmetic  21.7 us (3%)
  local copies, waits for them, and re-layouts  18.2 us (2%)
  between operations  15 us (2%)
    pallas_call x1, Pallas kernels, first_gather(): pl.pallas_call(functools.partial(first_kernel, C, Z, dealt), out_shape=tu...  134 us
    pallas_call x1, Pallas kernels, feed_forward(): pl.pallas_call(functools.partial(feed_forward_kernel, C), out_shape=(jax....  97.9 us
    pallas_call x2, Pallas kernels, back_scatter(): pl.pallas_call(functools.partial(back_scatter_kernel, C), out_shape=jax.S...  91 us
    pallas_call x1, Pallas kernels, attention_out(): pl.pallas_call(functools.partial(attention_out_kernel, C), out_shape=(jax...  66.1 us
    pallas_call x1, Pallas kernels, project(): pl.pallas_call(functools.partial(project_kernel, C), out_shape=(raw, raw,...  57.3 us
    pallas_call x1, Pallas kernels, gather_rows(): pl.pallas_call(functools.partial(gather_kernel, C), out_shape=jax.ShapeDt...  40.3 us
    dot_general x4, matrix products, dot(): lax.dot_general(left, right, (((left_dim,), (right_dim,)), ((), ())), pre...  39.1 us
    pallas_call x2, Pallas kernels, return_rows(): pl.pallas_call(functools.partial(return_kernel, C, groups, blocks), out_s...  38.5 us
  transfers between devices with their start and end apart: 8, of which 4 were waited for; matrix products, arithmetic and copies ran while one was open for 9% of the time, Pallas kernels for 68%

profile of v4, /device:TPU:0, one launch (start us, length us, event | category | flops | bytes accessed | tf_op | source)
XLA Modules:
  0.0 750.3 jit_solution(15795033805860816159)
XLA Ops:
  7.2 2.1 slice.42
  9.4 1.7 slice.43
  11.0 1.3 fusion.12.refs_5_
  12.3 133.5 %first_gather.1 = (bf16[2,1024,2048]{2,1,0:T(8,128)(2,1)}, bf16[2048,768]{1,0:T(8,128)(2,1)}, bf16[4,64,2048]{2,1,0:T(8,128)(2,1)}, bf16[4,16,128]{2,1,0:T(8,128...) custom-call(bf16[256,2048]{1,0:T(8,128)(2,1)} %tokens_ref.1, bf16[64,2048]{1,0:T(8,128)(2,1)} %refs_1_.1, ...), custom_call_target="tpu_custom_call" | custom-call | flops 100000000 | bytes 1024 | tf_op jit(solution)/shard_map/first_gather/pallas_call | solution.py:521
  146.4 0.7 fusion.18
  147.7 0.9 convert_bitcast_fusion
  149.5 3.7 fusion.2
  153.9 57.3 %project.1 = (f32[2048,256]{1,0:T(8,128)}, f32[2048,256]{1,0:T(8,128)}, bf16[2048,256]{1,0:T(8,128)(2,1)S(1)}, bf16[2048,256]{1,0:T(8,128)(2,1)S(1)}, bf16[2048,...) custom-call(bf16[2048,2048]{1,0:T(8,128)(2,1)} %bitcast.41, ...), custom_call_target="tpu_custom_call" | custom-call | flops 18000000 | bytes 1024 | tf_op jit(solution)/shard_map/project/pallas_call | solution.py:646
  211.2 13.7 %attend.1.attended_ref = bf16[2048,256]{1,0:T(8,128)(2,1)S(1)} custom-call(bf16[2048,256]{1,0:T(8,128)(2,1)S(1)} %get-tuple-element.76.q_ref, bf16[2048,256]{1,0:T(8,128)(2,1)S(1)} %get-tuple-element.77.k_ref, bf16[2048,256]{1,0:T(8,128)(2,1)S(1)} %get-tuple-element.78.v_ref, s32[2048,1]{1,0:T(8,128)S(1)} %bitcast.37, s32[2,1,1024]{2,1,0:T(1,128)S(1)} %pad_add_fusion.1.place_ref), custom_call_target="tpu_custom_call" | custom-call | flops 2147483648 | bytes 4194304 | tf_op jit(solution)/shard_map/attend/pallas_call | solution.py:75
  225.0 1.0 copy-done.6
  226.0 66.1 %attention_out.1 = (bf16[256,2048]{1,0:T(8,128)(2,1)}, f32[256,2048]{1,0:T(8,128)}, f32[256,2048]{1,0:T(8,128)}, bf16[2,1024,2048]{2,1,0:T(8,128)(2,1)}) custom-call(bf16[2048,256]{1,0:T(8,128)(2,1)} %copy-done.6, bf16[2048,2048]{1,0:T(8,128)(2,1)} %bitcast.39, bf16[256,2048]{1,0:T(8,128)(2,1)} %tokens_ref.1, f32[8,2048]{1,0:T(8,128)} %pad.17.gain_ref), custom_call_target="tpu_custom_call" | custom-call | flops 60000000 | bytes 1024 | tf_op jit(solution)/shard_map/attention_out/pallas_call | solution.py:863
  292.1 2.2 all-gather.6.cloned.1.call-done.wgu_ref.w_in
  295.6 24.8 %mix.1 = (bf16[2048,2048]{1,0:T(8,128)(2,1)}, bf16[2048,1024]{1,0:T(8,128)(2,1)}, bf16[1024,2048]{1,0:T(8,128)(2,1)}) custom-call(bf16[2048,2048]{1,0:T(8,128)(2,1)} %bitcast.43, bf16[2048,2048]{1,0:T(8,128)(2,1)} %all-gather.6.cloned.1.call-done.wgu_ref.w_in), custom_call_target="tpu_custom_call" | custom-call | flops 20000000 | bytes 1024 | tf_op jit(solution)/shard_map/mix/pallas_call | solution.py:1058
  320.3 2.3 all-gather.8.cloned.1.call-done.second_wd
  322.7 97.9 %feed_forward.1 = (f32[256,2048]{1,0:T(8,128)}, bf16[2048,2048]{1,0:T(8,128)(2,1)}, bf16[1024,2048]{1,0:T(8,128)(2,1)}, f32[8,2048]{1,0:T(8,128)}) custom-call(bf16[2048,1024]{1,0:T(8,128)(2,1)} %get-tuple-element.86.mixed_ref, bf16[1024,2048]{1,0:T(8,128)(2,1)} %get-tuple-element.87.turned_ref, bf16[2048,2048]{1,0:T(8,128)(2,1)} %get-tuple-element.88.gu_ref, ...), custom_call_target="tpu_custom_call" | custom-call | flops 80000000 | bytes 1024 | tf_op jit(solution)/shard_map/feed_forward/pallas_call | solution.py:1258
  420.6 1.1 copy-done.7
  421.8 46.7 %back_scatter.2.add_in = f32[256,2048]{1,0:T(8,128)S(1)} custom-call(bf16[2048,2048]{1,0:T(8,128)(2,1)} %get-tuple-element.94.b_ref, bf16[2048,2048]{1,0:T(8,128)(2,1)} %all-gather.6.cloned.1.call-done.wgu_ref.w_in, bf16[256,2048]{1,0:T(8,128)(2,1)S(1)} %copy-done.7), custom_call_target="tpu_custom_call" | custom-call | flops 50000000 | bytes 1024 | tf_op jit(solution)/shard_map/back_scatter/pallas_call | solution.py:1353
  468.4 21.3 %fusion.19 = bf16[2048,2048]{1,0:T(8,128)(2,1)} fusion(bf16[2048,2048]{1,0:T(8,128)(2,1)} %bitcast.44, bf16[2048,2048]{1,0:T(8,128)(2,1)S(1)} %copy-done.19), kind=kOutput, calls=%fused_computation.53 | convolution fusion | flops 17179869184 | bytes 25165824 | tf_op jit(solution)/shard_map/dot_general | solution.py:24
  489.7 5.9 reduce-scatter.4.cloned.1.call-done
  496.1 2.0 multiply_reduce_fusion.2
  498.0 0.8 slice.49
  498.9 1.1 convert_element_type.47
  500.0 1.6 convert_element_type.48
  502.7 40.3 %gather_rows.1 = bf16[2,1024,2048]{2,1,0:T(8,128)(2,1)S(1)} custom-call(bf16[256,2048]{1,0:T(8,128)(2,1)S(1)} %multiply_convert_fusion.x_ref), custom_call_target="tpu_custom_call" | custom-call | flops 40000000 | bytes 1024 | tf_op jit(solution)/shard_map/gather_rows/pallas_call | solution.py:331
  543.2 3.8 fusion.g_ref
  547.0 22.7 %attend_back.1 = (f32[2048,256]{1,0:T(8,128)}, f32[2048,256]{1,0:T(8,128)}, f32[2048,256]{1,0:T(8,128)}) custom-call(bf16[2048,256]{1,0:T(8,128)(2,1)S(1)} %copy-done.15, bf16[2048,256]{1,0:T(8,128)(2,1)S(1)} %copy-done.17, bf16[2048,256]{1,0:T(8,128)(2,1)S(1)} %copy-done.13, bf16[2048,256]{1,0:T(8,128)(2,1)S(1)} %fusion.g_ref, s32[2048,1]{1,0:T(8,128)S(1)} %bitcast.38, ...), custom_call_target="tpu_custom_call" | custom-call | flops 5368709120 | bytes 10485760 | tf_op jit(solution)/shard_map/attend_back/pallas_call | solution.py:96
  569.7 3.7 fusion.20.deal_ref
  573.4 32.5 %project_back.1 = (bf16[2048,768]{1,0:T(8,128)(2,1)}, f32[8,2048]{1,0:T(8,128)S(1)}, bf16[4,64,2048]{2,1,0:T(8,128)(2,1)S(1)}) custom-call(f32[2048,256]{1,0:T(8,128)} %get-tuple-element.97.dq_ref, f32[2048,256]{1,0:T(8,128)} %get-tuple-element.98.dk_ref, f32[2048,256]{1,0:T(8,128)} %get-tuple-element.99.dv_ref, f32[2048,256]{1,0:T(8,128)} %get-tuple-element.100.rq_ref, ...), custom_call_target="tpu_custom_call" | custom-call | flops 15000000 | bytes 1024 | tf_op jit(solution)/shard_map/project_back/pallas_call | solution.py:772
  605.9 1.3 reshape.109
  607.2 10.3 %fusion.21 = bf16[2048,768]{1,0:T(8,128)(2,1)S(1)} fusion(bf16[2048,2048]{1,0:T(8,128)(2,1)} %bitcast.42, bf16[2048,768]{1,0:T(8,128)(2,1)} %get-tuple-element.117.b_ref), kind=kOutput, calls=%fused_computation.55 | convolution fusion | flops 6442450944 | bytes 14680064 | tf_op jit(solution)/shard_map/dot_general | solution.py:24
  617.5 2.6 pad_maximum_fusion
  620.1 22.9 %reduce-scatter.6.cloned.1.call-done.x_ref = bf16[512,2048]{1,0:T(8,128)(2,1)} async-done(((bf16[2048,2048]{1,0:T(8,128)(2,1)}), bf16[512,2048]{1,0:T(8,128)(2,1)}) %reduce-scatter.6.cloned.1.call-update) | async-done | bytes 2097168 | tf_op jit(solution)/shard_map/reduce_scatter | solution.py:1439
  643.0 1.2 collective-permute-start
  644.2 1.6 copy-done.8
  645.8 26.3 %return_rows.2 = (bf16[64,8192]{1,0:T(8,128)(2,1)S(1)}, bf16[64,8192]{1,0:T(8,128)(2,1)S(1)}) custom-call(bf16[512,2048]{1,0:T(8,128)(2,1)S(1)} %copy-done.8), custom_call_target="tpu_custom_call" | custom-call | flops 20000000 | bytes 1024 | tf_op jit(solution)/shard_map/return_rows/pallas_call | solution.py:934
  672.1 1.5 convert_element_type.49
  673.6 1.5 convert_element_type.50
  675.1 2.5 collective-permute-start.1
  677.6 44.4 %back_scatter.3 = f32[256,2048]{1,0:T(8,128)S(1)} custom-call(bf16[2048,768]{1,0:T(8,128)(2,1)} %get-tuple-element.117.b_ref, bf16[2048,768]{1,0:T(8,128)(2,1)} %get-tuple-element.73.w_ref.w_in, f32[256,2048]{1,0:T(8,128)S(1)} %back_scatter.2.add_in), custom_call_target="tpu_custom_call" | custom-call | flops 50000000 | bytes 1024 | tf_op jit(solution)/shard_map/back_scatter/pallas_call | solution.py:1353
  722.0 1.3 copy-done.4
  723.9 1.0 slice_convert_fusion
  724.9 1.2 copy-done.9
  726.1 12.1 %return_rows.3 = (bf16[64,2048]{1,0:T(8,128)(2,1)S(1)}, bf16[64,2048]{1,0:T(8,128)(2,1)S(1)}, bf16[64,2048]{1,0:T(8,128)(2,1)S(1)}) custom-call(bf16[512,1024]{1,0:T(8,128)(2,1)S(1)} %copy-done.9), custom_call_target="tpu_custom_call" | custom-call | flops 20000000 | bytes 1024 | tf_op jit(solution)/shard_map/return_rows/pallas_call | solution.py:934
  738.3 0.9 reshape.110
  739.2 0.8 convert_element_type.51
  740.0 0.8 convert_element_type.52
  740.8 0.8 convert_element_type.53
  741.7 1.3 copy.51
  (96 shorter events, 6.4 us)
Async XLA Ops:
  7.2 138.7 %all-gather.4.cloned.1.call-start = ((), (), s32[]{:S(2)}) async-start(), calls=%async_computation.3 | async-start | bytes 3932160 | tf_op jit(solution)/shard_map/all_gather | solution.py:1436
  9.3 285.0 %all-gather.6.cloned.1.call-start = ((), (), s32[]{:S(2)}) async-start(), calls=%async_computation.4 | async-start | bytes 10485760 | tf_op jit(solution)/shard_map/all_gather | solution.py:1436
  12.3 133.6 %copy-start.23 = (s32[8,2]{0,1:T(2,128)S(1)}, s32[8,2]{0,1:T(2,128)}, u32[]{:S(2)}) copy-start(s32[8,2]{0,1:T(2,128)} %param.28) | copy-start | bytes 196
  145.9 176.7 %all-gather.8.cloned.1.call-start = ((), (), s32[]{:S(2)}) async-start(), calls=%async_computation.5 | async-start | bytes 1310720 | tf_op jit(solution)/shard_map/all_gather | solution.py:1436
  147.7 63.6 %copy-start.10 = (s32[1,2048]{0,1:T(8,128)}, s32[1,2048]{0,1:T(8,128)S(1)}, u32[]{:S(2)}) copy-start(s32[1,2048]{0,1:T(8,128)S(1)} %copy.49) | copy-start | bytes 24580
  153.9 57.3 %copy-start = (f32[2048,128]{1,0:T(8,128)}, f32[2048,128]{1,0:T(8,128)S(1)}, u32[]{:S(2)}) copy-start(f32[2048,128]{1,0:T(8,128)S(1)} %get-tuple-element.147.cos_ref) | copy-start | bytes 3145732
  153.9 57.3 %copy-start.2 = (f32[2048,128]{1,0:T(8,128)}, f32[2048,128]{1,0:T(8,128)S(1)}, u32[]{:S(2)}) copy-start(f32[2048,128]{1,0:T(8,128)S(1)} %get-tuple-element.148.sin_ref) | copy-start | bytes 3145732
  211.2 13.8 %copy-start.12 = (bf16[2048,256]{1,0:T(8,128)(2,1)}, bf16[2048,256]{1,0:T(8,128)(2,1)S(1)}, u32[]{:S(2)}) copy-start(bf16[2048,256]{1,0:T(8,128)(2,1)S(1)} %get-tuple-element.78.v_ref) | copy-start | bytes 3145732
  211.2 13.8 %copy-start.14 = (bf16[2048,256]{1,0:T(8,128)(2,1)}, bf16[2048,256]{1,0:T(8,128)(2,1)S(1)}, u32[]{:S(2)}) copy-start(bf16[2048,256]{1,0:T(8,128)(2,1)S(1)} %get-tuple-element.76.q_ref) | copy-start | bytes 3145732
  211.2 13.8 %copy-start.16 = (bf16[2048,256]{1,0:T(8,128)(2,1)}, bf16[2048,256]{1,0:T(8,128)(2,1)S(1)}, u32[]{:S(2)}) copy-start(bf16[2048,256]{1,0:T(8,128)(2,1)S(1)} %get-tuple-element.77.k_ref) | copy-start | bytes 3145732
  225.0 1.0 copy-start.6
  294.3 201.3 %reduce-scatter.4.cloned.1.call-start = ((), (), s32[]{:S(2)}) async-start(), calls=%async_computation.6 | async-start | bytes 5242880 | tf_op jit(solution)/shard_map/reduce_scatter | solution.py:1439
  420.5 1.2 copy-start.7
  420.6 222.4 %reduce-scatter.6.cloned.1.call-start = ((), (), s32[]{:S(2)}) async-start(), calls=%async_computation.7 | async-start | bytes 10485760 | tf_op jit(solution)/shard_map/reduce_scatter | solution.py:1439
  421.7 46.7 %copy-start.19 = (bf16[2048,2048]{1,0:T(8,128)(2,1)S(1)}, bf16[2048,2048]{1,0:T(8,128)(2,1)}, u32[]{:S(2)}) copy-start(bf16[2048,2048]{1,0:T(8,128)(2,1)} %get-tuple-element.94.b_ref) | copy-start | bytes 25165828
  495.6 4.4 copy-start.22
  495.6 228.3 %reduce-scatter.8.cloned.1.call-start = ((), (), s32[]{:S(2)}) async-start(), calls=%async_computation.8 | async-start | bytes 5242880 | tf_op jit(solution)/shard_map/reduce_scatter | solution.py:1439
  496.1 2.8 copy-start.21
  498.9 2.7 copy-start.18
  543.1 3.8 copy-start.11
  543.1 3.8 copy-start.13
  543.1 3.8 copy-start.15
  543.1 3.8 copy-start.17
  569.7 3.8 copy-start.1
  569.7 3.8 copy-start.3
  607.2 10.3 %copy-start.20 = (bf16[2048,256]{1,0:T(8,128)(2,1)S(1)}, bf16[2048,256]{1,0:T(8,128)(2,1)}, u32[]{:S(2)}) copy-start(bf16[2048,256]{1,0:T(8,128)(2,1)} %reshape.109) | copy-start | bytes 3145732
  643.0 32.1 %collective-permute-start = (f32[4,2048]{1,0:T(4,128)S(1)}, f32[4,2048]{1,0:T(4,128)S(1)}, u32[]{:S(2)}, u32[]{:S(2)}) collective-permute-start(f32[4,2048]{1,0:T(4,128)S(1)} %slice.50), channel_id=1, source_target_pairs={{0,8},{1,9},{2,10},{3,11},{4,12},{5,13},{6,14},{7,15},{8,0},{9,1},... | collective-permute-start | bytes 98312 | tf_op jit(solution)/shard_map/ppermute | solution.py:1430
  644.2 1.6 copy-start.8
  675.1 48.2 %collective-permute-start.1 = (f32[4,2048]{1,0:T(4,128)S(1)}, f32[4,2048]{1,0:T(4,128)S(1)}, u32[]{:S(2)}, u32[]{:S(2)}) collective-permute-start(f32[4,2048]{1,0:T(4,128)S(1)} %slice_add_fusion), channel_id=1, source_target_pairs={{0,16},{1,17},{2,18},{3,19},{4,20},{5,21},{6,22},{7,23},{8,24},{9,... | collective-permute-start | bytes 98312 | tf_op jit(solution)/shard_map/ppermute | solution.py:1430
  722.0 1.3 copy-start.4
  723.3 18.4 %copy-start.5 = (f32[256,2048]{1,0:T(8,128)S(1)}, f32[256,2048]{1,0:T(8,128)}, u32[]{:S(2)}) copy-start(f32[256,2048]{1,0:T(8,128)} %copy-done.4) | copy-start | bytes 6291460
  724.9 1.2 copy-start.9
Sparse Core Ops, SparseCore 0:
  10.2 110.9 all-gather.3
  146.0 148.2 all-gather.5
  296.5 26.1 all-gather.7
  420.7 74.8 reduce-scatter.3
  497.9 144.9 reduce-scatter.5
  645.2 78.1 reduce-scatter.7

commit v5 on v4

--- a/solution.py
+++ b/solution.py
@@ -885,10 +885,10 @@
 
 
 def return_kernel(C, groups, blocks, x_ref, *refs):
-    outs, (landing, sent, came, own_sem) = refs[:groups], refs[groups:]
+    out, landing, sent, came, own_sem = refs
     A = 2 * C
-    shard = outs[0].shape[0]
-    part = outs[0].shape[1] // (blocks * A)
+    shard = out.shape[0] // groups
+    part = out.shape[1] // (blocks * A)
     wide = groups * blocks * part
     dp, ctx, _ = places_of()
     own_at = place_in_plane(C, (dp, ctx))
@@ -925,7 +925,8 @@
             for at in range(A):
                 lanes = (group * blocks + block) * part
                 to = (block * A + at) * part
-                outs[group][:, to : to + part] = landing[at, :, lanes : lanes + part]
+                rows = slice(group * shard, (group + 1) * shard)
+                out[rows, to : to + part] = landing[at, :, lanes : lanes + part]
 
 
 def return_rows(x, wide, C, groups, blocks, number):
@@ -933,9 +934,9 @@
     shard = x.shape[0] // A
     return pl.pallas_call(
         functools.partial(return_kernel, C, groups, blocks),
-        out_shape=(jax.ShapeDtypeStruct((shard, wide * A // groups), x.dtype),) * groups,
+        out_shape=jax.ShapeDtypeStruct((groups * shard, wide * A // groups), x.dtype),
         in_specs=[ANY],
-        out_specs=(VM,) * groups,
+        out_specs=VM,
         scratch_shapes=[
             pltpu.VMEM((A, shard, wide), x.dtype),
             pltpu.SemaphoreType.DMA((A,)),
@@ -1293,14 +1294,14 @@
     )(mixed, turned_units, gate_up, *w_down, hidden, cotangent, gain)
 
 
-def back_scatter_kernel(
-    C, b_ref, w_in, add_in, out_hbm, out_ref, out_sem, w_ref, add_ref, load_sem, b_buf, b_sem,
-    own, other, twin_part, landing, *sems,
-):
-    loads = [
-        pltpu.make_async_copy(w_in, w_ref, load_sem.at[0]),
-        pltpu.make_async_copy(add_in, add_ref, load_sem.at[1]),
-    ]
+def back_scatter_kernel(C, added, b_ref, w_in, *refs):
+    if added:
+        add_in, add_ref, refs = refs[0], refs[1], refs[2:]
+    out_hbm, out_ref, out_sem, w_ref, load_sem, b_buf, b_sem = refs[:7]
+    own, other, twin_part, landing, *sems = refs[7:]
+    loads = [pltpu.make_async_copy(w_in, w_ref, load_sem.at[0])]
+    if added:
+        loads.append(pltpu.make_async_copy(add_in, add_ref, load_sem.at[1]))
     for load in loads:
         load.start()
     greet(plane_neighbours(C))
@@ -1310,7 +1311,9 @@
 
     def final(half, total):
         rows = pl.ds(half * half_rows, half_rows)
-        out_ref[rows, :] = total + add_ref[rows, :].astype(F32)
+        if added:
+            total = total + add_ref[rows, :].astype(F32)
+        out_ref[rows, :] = total
         leave(half).start()
 
     def leave(half):
@@ -1349,26 +1352,35 @@
 
 
 def back_scatter(b, w, add, C, number):
-    count, width = add.shape
+    width = w.shape[0]
+    count = b.shape[0] // (2 * C)
+    added = add is not None
+    scratch = [
+        pltpu.VMEM((count, width), F32),
+        pltpu.SemaphoreType.DMA((2,)),
+        pltpu.VMEM(w.shape, w.dtype),
+        pltpu.SemaphoreType.DMA((2,)),
+        pltpu.VMEM((2, count, b.shape[1]), BF16),
+        pltpu.SemaphoreType.DMA((2,)),
+    ] + scatter_scratch(C, count, width)
+
+    def kernel(*refs):
+        if added:
+            b_ref, w_in, add_in, out_hbm, *rest = refs
+            back_scatter_kernel(C, True, b_ref, w_in, add_in, rest[-1], out_hbm, *rest[:-1])
+        else:
+            back_scatter_kernel(C, False, *refs)
+
     return pl.pallas_call(
-        functools.partial(back_scatter_kernel, C),
+        kernel,
         out_shape=jax.ShapeDtypeStruct((count, width), F32),
-        in_specs=[ANY, ANY, ANY],
+        in_specs=[ANY] * (3 if added else 2),
         out_specs=ANY,
-        scratch_shapes=[
-            pltpu.VMEM((count, width), F32),
-            pltpu.SemaphoreType.DMA((2,)),
-            pltpu.VMEM(w.shape, w.dtype),
-            pltpu.VMEM(add.shape, add.dtype),
-            pltpu.SemaphoreType.DMA((2,)),
-            pltpu.VMEM((2, count, b.shape[1]), BF16),
-            pltpu.SemaphoreType.DMA((2,)),
-        ]
-        + scatter_scratch(C, count, width),
+        scratch_shapes=scratch + ([pltpu.VMEM(add.shape, add.dtype)] if added else []),
         compiler_params=comm_params(number, 48),
         cost_estimate=cost_of(50),
         name="back_scatter",
-    )(b, w, add)
+    )(*((b, w, add) if added else (b, w)))
 
 
 def rope_tables(places):
@@ -1457,10 +1469,10 @@
     else:
         gate_up = jnp.stack([w.reshape(shard, Z, A, part) for w in (w_gate, w_up)], axis=1)
         gate_up = exchange(gate_up.transpose(3, 0, 1, 2, 4).reshape(A * shard, 2 * ffn_slice))
+    full_qkv, gate_up, first_down, w_down = lax.optimization_barrier(
+        (full_qkv, gate_up, first_down, w_down)
+    )
     second_down = w_down[:, split:]
-    full_qkv, gate_up, first_down, second_down = lax.optimization_barrier(
-        (full_qkv, gate_up, first_down, second_down)
-    )
     full_gate_up = gather_z_aside(gate_up)
     all_gains = all_gains[:, :, :4, :shard].astype(F32).transpose(2, 0, 1, 3).reshape(4, width)
     head_gains = lax.dynamic_slice(all_gains, (0, plane_at * slice_width), (2, slice_width))
@@ -1531,6 +1543,7 @@
     last = scatter_z_aside(last)
     if dealt:
         grad_gate_up = return_rows(grad_gate_up, 2 * ffn_slice, C, 2, Z, 10)
+        grad_gate_up = grad_gate_up.reshape(2, shard, ffn_width)
     else:
         grad_gate_up = (
             exchange(grad_gate_up)
@@ -1545,9 +1558,9 @@
     )
     for power in range(1, Z.bit_length() - 1):
         gain_terms = gain_terms + swap(gain_terms, A << power)
-    grad_input = back_scatter(grad_raw, full_qkv, grad_hidden, C, 6)
+    grad_input = back_scatter(grad_raw, full_qkv, None, C, 6) + grad_hidden
     last, grad_input = lax.optimization_barrier((last, grad_input))
-    grad_qkv = return_rows(last, 3 * slice_width, C, 3, 1, 11)
+    grad_qkv = return_rows(last, 3 * slice_width, C, 3, 1, 11).reshape(3, shard, width)
     grad_w_out = last[:, 3 * slice_width :]
     gain_sums = lax.dynamic_slice(gain_terms, (0, own_at * shard), (4, shard))
 

time: 759 us -> 757 us (level)
  no operation moved by 1% of the time
where the time goes in v5:
time: 757 us; the launch traced here: 749 us
  Pallas kernels  617 us (82%)
  matrix products  39.1 us (5%)
  waiting for transfers between devices  33.5 us (4%)
  other arithmetic  21.4 us (3%)
  local copies, waits for them, and re-layouts  17.8 us (2%)
  between operations  15 us (2%)
    pallas_call x1, Pallas kernels, first_gather(): pl.pallas_call(functools.partial(first_kernel, C, Z, dealt), out_shape=tu...  134 us
    pallas_call x1, Pallas kernels, feed_forward(): pl.pallas_call(functools.partial(feed_forward_kernel, C), out_shape=(jax....  97.8 us
    pallas_call x2, Pallas kernels, back_scatter(): pl.pallas_call(kernel, out_shape=jax.ShapeDtypeStruct((count, width), F32...  90.4 us
    pallas_call x1, Pallas kernels, attention_out(): pl.pallas_call(functools.partial(attention_out_kernel, C), out_shape=(jax...  66.1 us
    pallas_call x1, Pallas kernels, project(): pl.pallas_call(functools.partial(project_kernel, C), out_shape=(raw, raw,...  56.2 us
    pallas_call x1, Pallas kernels, gather_rows(): pl.pallas_call(functools.partial(gather_kernel, C), out_shape=jax.ShapeDt...  40.3 us
    dot_general x4, matrix products, dot(): lax.dot_general(left, right, (((left_dim,), (right_dim,)), ((), ())), pre...  39.1 us
    pallas_call x2, Pallas kernels, return_rows(): pl.pallas_call(functools.partial(return_kernel, C, groups, blocks), out_s...  38.5 us
  transfers between devices with their start and end apart: 8, of which 4 were waited for; matrix products, arithmetic and copies ran while one was open for 9% of the time, Pallas kernels for 68%

profile of v5, /device:TPU:0, one launch (start us, length us, event | category | flops | bytes accessed | tf_op | source)
XLA Modules:
  0.0 748.6 jit_solution(14747421586654110262)
XLA Ops:
  7.2 2.1 slice.62
  9.4 1.3 fusion.12.refs_5_
  10.7 134.2 %first_gather.1 = (bf16[2,1024,2048]{2,1,0:T(8,128)(2,1)}, bf16[2048,768]{1,0:T(8,128)(2,1)}, bf16[4,64,2048]{2,1,0:T(8,128)(2,1)}, bf16[4,16,128]{2,1,0:T(8,128...) custom-call(bf16[256,2048]{1,0:T(8,128)(2,1)} %tokens_ref.1, bf16[64,2048]{1,0:T(8,128)(2,1)} %refs_1_.1, ...), custom_call_target="tpu_custom_call" | custom-call | flops 100000000 | bytes 1024 | tf_op jit(solution)/shard_map/first_gather/pallas_call | solution.py:521
  145.4 0.7 fusion.18
  146.7 0.9 convert_bitcast_fusion
  147.9 0.6 pad.17.gain_ref
  148.5 3.7 fusion.2
  152.2 0.6 pad_maximum_fusion.1
  152.9 1.9 slice.66
  154.8 56.2 %project.1 = (f32[2048,256]{1,0:T(8,128)}, f32[2048,256]{1,0:T(8,128)}, bf16[2048,256]{1,0:T(8,128)(2,1)S(1)}, bf16[2048,256]{1,0:T(8,128)(2,1)S(1)}, bf16[2048,...) custom-call(bf16[2048,2048]{1,0:T(8,128)(2,1)} %bitcast.41, ...), custom_call_target="tpu_custom_call" | custom-call | flops 18000000 | bytes 1024 | tf_op jit(solution)/shard_map/project/pallas_call | solution.py:646
  211.1 13.7 %attend.1.attended_ref = bf16[2048,256]{1,0:T(8,128)(2,1)S(1)} custom-call(bf16[2048,256]{1,0:T(8,128)(2,1)S(1)} %get-tuple-element.71.q_ref, bf16[2048,256]{1,0:T(8,128)(2,1)S(1)} %get-tuple-element.72.k_ref, bf16[2048,256]{1,0:T(8,128)(2,1)S(1)} %get-tuple-element.73.v_ref, s32[2048,1]{1,0:T(8,128)S(1)} %bitcast.37, s32[2,1,1024]{2,1,0:T(1,128)S(1)} %pad_add_fusion.1.place_ref), custom_call_target="tpu_custom_call" | custom-call | flops 2147483648 | bytes 4194304 | tf_op jit(solution)/shard_map/attend/pallas_call | solution.py:75
  224.9 1.0 copy-done.4
  225.9 66.1 %attention_out.1 = (bf16[256,2048]{1,0:T(8,128)(2,1)}, f32[256,2048]{1,0:T(8,128)}, f32[256,2048]{1,0:T(8,128)}, bf16[2,1024,2048]{2,1,0:T(8,128)(2,1)}) custom-call(bf16[2048,256]{1,0:T(8,128)(2,1)} %copy-done.4, bf16[2048,2048]{1,0:T(8,128)(2,1)} %bitcast.39, bf16[256,2048]{1,0:T(8,128)(2,1)} %tokens_ref.1, f32[8,2048]{1,0:T(8,128)} %pad.17.gain_ref), custom_call_target="tpu_custom_call" | custom-call | flops 60000000 | bytes 1024 | tf_op jit(solution)/shard_map/attention_out/pallas_call | solution.py:863
  292.0 2.3 all-gather.6.cloned.1.call-done.wgu_ref.refs_1_
  294.9 0.6 pad.18.gain_ref
  295.6 24.8 %mix.1 = (bf16[2048,2048]{1,0:T(8,128)(2,1)}, bf16[2048,1024]{1,0:T(8,128)(2,1)}, bf16[1024,2048]{1,0:T(8,128)(2,1)}) custom-call(bf16[2048,2048]{1,0:T(8,128)(2,1)} %bitcast.43, bf16[2048,2048]{1,0:T(8,128)(2,1)} %all-gather.6.cloned.1.call-done.wgu_ref.refs_1_), custom_call_target="tpu_custom_call" | custom-call | flops 20000000 | bytes 1024 | tf_op jit(solution)/shard_map/mix/pallas_call | solution.py:1059
  320.4 2.3 all-gather.8.cloned.1.call-done.second_wd
  322.7 97.8 %feed_forward.1 = (f32[256,2048]{1,0:T(8,128)}, bf16[2048,2048]{1,0:T(8,128)(2,1)}, bf16[1024,2048]{1,0:T(8,128)(2,1)}, f32[8,2048]{1,0:T(8,128)}) custom-call(bf16[2048,1024]{1,0:T(8,128)(2,1)} %get-tuple-element.81.mixed_ref, bf16[1024,2048]{1,0:T(8,128)(2,1)} %get-tuple-element.82.turned_ref, bf16[2048,2048]{1,0:T(8,128)(2,1)} %get-tuple-element.83.gu_ref, ...), custom_call_target="tpu_custom_call" | custom-call | flops 80000000 | bytes 1024 | tf_op jit(solution)/shard_map/feed_forward/pallas_call | solution.py:1259
  420.6 1.1 copy-done.5
  421.7 46.7 %back_scatter.2 = f32[256,2048]{1,0:T(8,128)S(1)} custom-call(bf16[2048,2048]{1,0:T(8,128)(2,1)} %get-tuple-element.89.refs_0_, bf16[2048,2048]{1,0:T(8,128)(2,1)} %all-gather.6.cloned.1.call-done.wgu_ref.refs_1_, bf16[256,2048]{1,0:T(8,128)(2,1)S(1)} %copy-done.5), custom_call_target="tpu_custom_call" | custom-call | flops 50000000 | bytes 1024 | tf_op jit(solution)/shard_map/back_scatter/pallas_call | solution.py:1374
  468.4 21.3 %fusion.19 = bf16[2048,2048]{1,0:T(8,128)(2,1)} fusion(bf16[2048,2048]{1,0:T(8,128)(2,1)} %bitcast.44, bf16[2048,2048]{1,0:T(8,128)(2,1)S(1)} %copy-done.18), kind=kOutput, calls=%fused_computation.58 | convolution fusion | flops 17179869184 | bytes 25165824 | tf_op jit(solution)/shard_map/dot_general | solution.py:24
  489.7 5.9 reduce-scatter.4.cloned.1.call-done
  496.0 2.0 multiply_reduce_fusion.2
  498.0 0.8 slice.69
  498.9 1.1 convert_element_type.47
  500.0 1.6 convert_element_type.48
  502.6 40.3 %gather_rows.1 = bf16[2,1024,2048]{2,1,0:T(8,128)(2,1)S(1)} custom-call(bf16[256,2048]{1,0:T(8,128)(2,1)S(1)} %multiply_convert_fusion.x_ref), custom_call_target="tpu_custom_call" | custom-call | flops 40000000 | bytes 1024 | tf_op jit(solution)/shard_map/gather_rows/pallas_call | solution.py:331
  543.0 3.8 fusion.g_ref
  546.8 22.7 %attend_back.1 = (f32[2048,256]{1,0:T(8,128)}, f32[2048,256]{1,0:T(8,128)}, f32[2048,256]{1,0:T(8,128)}) custom-call(bf16[2048,256]{1,0:T(8,128)(2,1)S(1)} %copy-done.14, bf16[2048,256]{1,0:T(8,128)(2,1)S(1)} %copy-done.16, bf16[2048,256]{1,0:T(8,128)(2,1)S(1)} %copy-done.12, bf16[2048,256]{1,0:T(8,128)(2,1)S(1)} %fusion.g_ref, s32[2048,1]{1,0:T(8,128)S(1)} %bitcast.38, ...), custom_call_target="tpu_custom_call" | custom-call | flops 5368709120 | bytes 10485760 | tf_op jit(solution)/shard_map/attend_back/pallas_call | solution.py:96
  569.5 3.8 fusion.20.deal_ref
  573.3 32.5 %project_back.1 = (bf16[2048,768]{1,0:T(8,128)(2,1)}, f32[8,2048]{1,0:T(8,128)S(1)}, bf16[4,64,2048]{2,1,0:T(8,128)(2,1)S(1)}) custom-call(f32[2048,256]{1,0:T(8,128)} %get-tuple-element.92.dq_ref, f32[2048,256]{1,0:T(8,128)} %get-tuple-element.93.dk_ref, f32[2048,256]{1,0:T(8,128)} %get-tuple-element.94.dv_ref, f32[2048,256]{1,0:T(8,128)} %get-tuple-element.95.rq_ref, ...), custom_call_target="tpu_custom_call" | custom-call | flops 15000000 | bytes 1024 | tf_op jit(solution)/shard_map/project_back/pallas_call | solution.py:772
  605.7 1.3 reshape.121
  607.1 10.3 %fusion.21 = bf16[2048,768]{1,0:T(8,128)(2,1)S(1)} fusion(bf16[2048,2048]{1,0:T(8,128)(2,1)} %bitcast.42, bf16[2048,768]{1,0:T(8,128)(2,1)} %get-tuple-element.110.refs_0_), kind=kOutput, calls=%fused_computation.60 | convolution fusion | flops 6442450944 | bytes 14680064 | tf_op jit(solution)/shard_map/dot_general | solution.py:24
  617.4 2.6 pad_maximum_fusion
  619.9 23.0 %reduce-scatter.6.cloned.1.call-done.x_ref = bf16[512,2048]{1,0:T(8,128)(2,1)} async-done(((bf16[2048,2048]{1,0:T(8,128)(2,1)}), bf16[512,2048]{1,0:T(8,128)(2,1)}) %reduce-scatter.6.cloned.1.call-update) | async-done | bytes 2097168 | tf_op jit(solution)/shard_map/reduce_scatter | solution.py:1451
  642.9 1.2 collective-permute-start
  644.2 1.6 copy-done.7
  645.8 26.3 %return_rows.2 = bf16[128,8192]{1,0:T(8,128)(2,1)S(1)} custom-call(bf16[512,2048]{1,0:T(8,128)(2,1)S(1)} %copy-done.7), custom_call_target="tpu_custom_call" | custom-call | flops 20000000 | bytes 1024 | tf_op jit(solution)/shard_map/return_rows/pallas_call | solution.py:935
  672.1 2.4 slice_convert_fusion
  674.6 2.5 collective-permute-start.1
  677.1 1.9 copy-done.6
  678.9 43.7 %back_scatter.3 = f32[256,2048]{1,0:T(8,128)S(1)} custom-call(bf16[2048,768]{1,0:T(8,128)(2,1)S(1)} %copy-done.6, bf16[2048,768]{1,0:T(8,128)(2,1)} %get-tuple-element.68.w_ref.refs_1_), custom_call_target="tpu_custom_call" | custom-call | flops 50000000 | bytes 1024 | tf_op jit(solution)/shard_map/back_scatter/pallas_call | solution.py:1374
  722.6 1.7 add.92
  724.9 1.0 slice_convert_fusion.2
  725.9 1.2 copy-done.8
  727.1 12.2 %return_rows.3 = bf16[192,2048]{1,0:T(8,128)(2,1)S(1)} custom-call(bf16[512,1024]{1,0:T(8,128)(2,1)S(1)} %copy-done.8), custom_call_target="tpu_custom_call" | custom-call | flops 20000000 | bytes 1024 | tf_op jit(solution)/shard_map/return_rows/pallas_call | solution.py:935
  739.3 0.9 reshape.122
  740.2 1.2 slice_convert_fusion.3
  (91 shorter events, 4.4 us)
Async XLA Ops:
  7.2 137.7 %all-gather.4.cloned.1.call-start = ((), (), s32[]{:S(2)}) async-start(), calls=%async_computation.3 | async-start | bytes 3932160 | tf_op jit(solution)/shard_map/all_gather | solution.py:1448
  9.3 285.0 %all-gather.6.cloned.1.call-start = ((), (), s32[]{:S(2)}) async-start(), calls=%async_computation.4 | async-start | bytes 10485760 | tf_op jit(solution)/shard_map/all_gather | solution.py:1448
  10.7 134.3 %copy-start.22 = (s32[8,2]{0,1:T(2,128)S(1)}, s32[8,2]{0,1:T(2,128)}, u32[]{:S(2)}) copy-start(s32[8,2]{0,1:T(2,128)} %param.28) | copy-start | bytes 196
  144.9 177.8 %all-gather.8.cloned.1.call-start = ((), (), s32[]{:S(2)}) async-start(), calls=%async_computation.5 | async-start | bytes 1310720 | tf_op jit(solution)/shard_map/all_gather | solution.py:1448
  146.6 64.5 %copy-start.9 = (s32[1,2048]{0,1:T(8,128)}, s32[1,2048]{0,1:T(8,128)S(1)}, u32[]{:S(2)}) copy-start(s32[1,2048]{0,1:T(8,128)S(1)} %copy.49) | copy-start | bytes 24580
  152.9 58.2 %copy-start = (f32[2048,128]{1,0:T(8,128)}, f32[2048,128]{1,0:T(8,128)S(1)}, u32[]{:S(2)}) copy-start(f32[2048,128]{1,0:T(8,128)S(1)} %get-tuple-element.142.cos_ref) | copy-start | bytes 3145732
  152.9 58.2 %copy-start.2 = (f32[2048,128]{1,0:T(8,128)}, f32[2048,128]{1,0:T(8,128)S(1)}, u32[]{:S(2)}) copy-start(f32[2048,128]{1,0:T(8,128)S(1)} %get-tuple-element.143.sin_ref) | copy-start | bytes 3145732
  211.1 13.8 %copy-start.11 = (bf16[2048,256]{1,0:T(8,128)(2,1)}, bf16[2048,256]{1,0:T(8,128)(2,1)S(1)}, u32[]{:S(2)}) copy-start(bf16[2048,256]{1,0:T(8,128)(2,1)S(1)} %get-tuple-element.73.v_ref) | copy-start | bytes 3145732
  211.1 13.8 %copy-start.13 = (bf16[2048,256]{1,0:T(8,128)(2,1)}, bf16[2048,256]{1,0:T(8,128)(2,1)S(1)}, u32[]{:S(2)}) copy-start(bf16[2048,256]{1,0:T(8,128)(2,1)S(1)} %get-tuple-element.71.q_ref) | copy-start | bytes 3145732
  211.1 13.8 %copy-start.15 = (bf16[2048,256]{1,0:T(8,128)(2,1)}, bf16[2048,256]{1,0:T(8,128)(2,1)S(1)}, u32[]{:S(2)}) copy-start(bf16[2048,256]{1,0:T(8,128)(2,1)S(1)} %get-tuple-element.72.k_ref) | copy-start | bytes 3145732
  224.9 1.0 copy-start.4
  294.3 201.2 %reduce-scatter.4.cloned.1.call-start = ((), (), s32[]{:S(2)}) async-start(), calls=%async_computation.6 | async-start | bytes 5242880 | tf_op jit(solution)/shard_map/reduce_scatter | solution.py:1451
  420.5 1.2 copy-start.5
  420.5 222.4 %reduce-scatter.6.cloned.1.call-start = ((), (), s32[]{:S(2)}) async-start(), calls=%async_computation.7 | async-start | bytes 10485760 | tf_op jit(solution)/shard_map/reduce_scatter | solution.py:1451
  421.7 46.7 %copy-start.18 = (bf16[2048,2048]{1,0:T(8,128)(2,1)S(1)}, bf16[2048,2048]{1,0:T(8,128)(2,1)}, u32[]{:S(2)}) copy-start(bf16[2048,2048]{1,0:T(8,128)(2,1)} %get-tuple-element.89.refs_0_) | copy-start | bytes 25165828
  495.6 4.4 copy-start.21
  495.6 229.3 %reduce-scatter.8.cloned.1.call-start = ((), (), s32[]{:S(2)}) async-start(), calls=%async_computation.8 | async-start | bytes 5242880 | tf_op jit(solution)/shard_map/reduce_scatter | solution.py:1451
  496.0 2.8 copy-start.20
  498.9 2.7 copy-start.17
  542.9 3.8 copy-start.10
  542.9 3.8 copy-start.12
  543.0 3.8 copy-start.14
  543.0 3.8 copy-start.16
  569.5 3.8 copy-start.1
  569.5 3.8 copy-start.3
  607.1 10.3 %copy-start.19 = (bf16[2048,256]{1,0:T(8,128)(2,1)S(1)}, bf16[2048,256]{1,0:T(8,128)(2,1)}, u32[]{:S(2)}) copy-start(bf16[2048,256]{1,0:T(8,128)(2,1)} %reshape.121) | copy-start | bytes 3145732
  642.9 31.6 %collective-permute-start = (f32[4,2048]{1,0:T(4,128)S(1)}, f32[4,2048]{1,0:T(4,128)S(1)}, u32[]{:S(2)}, u32[]{:S(2)}) collective-permute-start(f32[4,2048]{1,0:T(4,128)S(1)} %slice.72), channel_id=1, source_target_pairs={{0,8},{1,9},{2,10},{3,11},{4,12},{5,13},{6,14},{7,15},{8,0},{9,1},... | collective-permute-start | bytes 98312 | tf_op jit(solution)/shard_map/ppermute | solution.py:1442
  644.2 1.6 copy-start.7
  674.6 49.7 %collective-permute-start.1 = (f32[4,2048]{1,0:T(4,128)S(1)}, f32[4,2048]{1,0:T(4,128)S(1)}, u32[]{:S(2)}, u32[]{:S(2)}) collective-permute-start(f32[4,2048]{1,0:T(4,128)S(1)} %slice_add_fusion), channel_id=1, source_target_pairs={{0,16},{1,17},{2,18},{3,19},{4,20},{5,21},{6,22},{7,23},{8,24},{9,... | collective-permute-start | bytes 98312 | tf_op jit(solution)/shard_map/ppermute | solution.py:1442
  677.1 1.9 copy-start.6
  725.9 1.2 copy-start.8
Sparse Core Ops, SparseCore 0:
  10.2 125.3 all-gather.3
  145.0 149.2 all-gather.5
  296.5 26.1 all-gather.7
  420.7 74.8 reduce-scatter.3
  497.9 144.9 reduce-scatter.5
  645.2 78.1 reduce-scatter.7

commit v6 on v5

--- a/solution.py
+++ b/solution.py
@@ -885,9 +885,9 @@
 
 
 def return_kernel(C, groups, blocks, x_ref, *refs):
-    out, landing, sent, came, own_sem = refs
+    out, landing, sent, came, own_sem, *refs = refs
     A = 2 * C
-    shard = out.shape[0] // groups
+    shard = landing.shape[1]
     part = out.shape[1] // (blocks * A)
     wide = groups * blocks * part
     dp, ctx, _ = places_of()
@@ -898,6 +898,10 @@
         x_ref.at[pl.ds(own_at * shard, shard), pl.ds(0, wide)], landing.at[own_at], own_sem
     )
     own.start()
+    if refs:
+        kept, kept_sem = refs
+        stay = pltpu.make_async_copy(x_ref.at[:, pl.ds(wide, kept.shape[1])], kept, kept_sem)
+        stay.start()
 
     def copy_to(index, device):
         rows = pl.ds(place_in_plane(C, device) * shard, shard)
@@ -927,22 +931,34 @@
                 to = (block * A + at) * part
                 rows = slice(group * shard, (group + 1) * shard)
                 out[rows, to : to + part] = landing[at, :, lanes : lanes + part]
+    if refs:
+        stay.wait()
+        size = kept.shape[1]
+        for at in range(A):
+            rows, lanes = slice(at * shard, (at + 1) * shard), slice(at * size, (at + 1) * size)
+            out[groups * shard : (groups + 1) * shard, lanes] = kept[rows, :]
 
 
 def return_rows(x, wide, C, groups, blocks, number):
     A = 2 * C
     shard = x.shape[0] // A
+    more = x.shape[1] - wide
+    scratch = [
+        pltpu.VMEM((A, shard, wide), x.dtype),
+        pltpu.SemaphoreType.DMA((A,)),
+        pltpu.SemaphoreType.DMA((A,)),
+        pltpu.SemaphoreType.DMA,
+    ]
+    if more:
+        scratch += [pltpu.VMEM((x.shape[0], more), x.dtype), pltpu.SemaphoreType.DMA]
     return pl.pallas_call(
         functools.partial(return_kernel, C, groups, blocks),
-        out_shape=jax.ShapeDtypeStruct((groups * shard, wide * A // groups), x.dtype),
+        out_shape=jax.ShapeDtypeStruct(
+            ((groups + (more > 0)) * shard, wide * A // groups), x.dtype
+        ),
         in_specs=[ANY],
         out_specs=VM,
-        scratch_shapes=[
-            pltpu.VMEM((A, shard, wide), x.dtype),
-            pltpu.SemaphoreType.DMA((A,)),
-            pltpu.SemaphoreType.DMA((A,)),
-            pltpu.SemaphoreType.DMA,
-        ],
+        scratch_shapes=scratch,
         compiler_params=comm_params(number, 24),
         cost_estimate=cost_of(20),
         name="return_rows",
@@ -1536,7 +1552,9 @@
         C, Z, 9,
     )
     term_qkv = dot(x_all, grad_raw, 0, 0, BF16)
-    last = jnp.concatenate([term_qkv, term_out.reshape(width, slice_width)], axis=1)
+    by_blocks = term_out.reshape(Z, shard, A, slice_width).transpose(0, 2, 1, 3)
+    by_blocks = by_blocks.reshape(width, slice_width)
+    last = jnp.concatenate([term_qkv, by_blocks], axis=1)
     last, grad_raw, grad_gate_up, gain_terms, output, grad_w_down = lax.optimization_barrier(
         (last, grad_raw, grad_gate_up, gain_terms, output.astype(BF16), grad_w_down.astype(F32))
     )
@@ -1560,8 +1578,7 @@
         gain_terms = gain_terms + swap(gain_terms, A << power)
     grad_input = back_scatter(grad_raw, full_qkv, None, C, 6) + grad_hidden
     last, grad_input = lax.optimization_barrier((last, grad_input))
-    grad_qkv = return_rows(last, 3 * slice_width, C, 3, 1, 11).reshape(3, shard, width)
-    grad_w_out = last[:, 3 * slice_width :]
+    grad_qkv = return_rows(last, 3 * slice_width, C, 3, 1, 11).reshape(4, shard, width)
     gain_sums = lax.dynamic_slice(gain_terms, (0, own_at * shard), (4, shard))
 
     return (
@@ -1570,7 +1587,7 @@
         grad_qkv[0].astype(F32),
         grad_qkv[1].astype(F32),
         grad_qkv[2].astype(F32),
-        grad_w_out.reshape(shard, width).astype(F32),
+        grad_qkv[3].astype(F32),
         gain_sums[0],
         gain_sums[1],
         gain_sums[2],

time: 757 us -> 755 us (level)
  no operation moved by 1% of the time
where the time goes in v6:
time: 755 us; the launch traced here: 747 us
  Pallas kernels  617 us (82%)
  matrix products  39.2 us (5%)
  waiting for transfers between devices  34.6 us (5%)
  other arithmetic  20.7 us (3%)
  local copies, waits for them, and re-layouts  15.7 us (2%)
  between operations  15 us (2%)
    pallas_call x1, Pallas kernels, first_gather(): pl.pallas_call(functools.partial(first_kernel, C, Z, dealt), out_shape=tu...  134 us
    pallas_call x1, Pallas kernels, feed_forward(): pl.pallas_call(functools.partial(feed_forward_kernel, C), out_shape=(jax....  97.9 us
    pallas_call x2, Pallas kernels, back_scatter(): pl.pallas_call(kernel, out_shape=jax.ShapeDtypeStruct((count, width), F32...  90.4 us
    pallas_call x1, Pallas kernels, attention_out(): pl.pallas_call(functools.partial(attention_out_kernel, C), out_shape=(jax...  66.1 us
    pallas_call x1, Pallas kernels, project(): pl.pallas_call(functools.partial(project_kernel, C), out_shape=(raw, raw,...  56.2 us
    pallas_call x1, Pallas kernels, gather_rows(): pl.pallas_call(functools.partial(gather_kernel, C), out_shape=jax.ShapeDt...  40.3 us
    dot_general x4, matrix products, dot(): lax.dot_general(left, right, (((left_dim,), (right_dim,)), ((), ())), pre...  39.2 us
    pallas_call x2, Pallas kernels, return_rows(): pl.pallas_call(functools.partial(return_kernel, C, groups, blocks), out_s...  38.5 us
  transfers between devices with their start and end apart: 8, of which 4 were waited for; matrix products, arithmetic and copies ran while one was open for 9% of the time, Pallas kernels for 68%

profile of v6, /device:TPU:0, one launch (start us, length us, event | category | flops | bytes accessed | tf_op | source)
XLA Modules:
  0.0 747.1 jit_solution(14491903483588502720)
XLA Ops:
  7.2 2.1 slice.63
  9.4 1.3 fusion.12.refs_5_
  10.7 134.2 %first_gather.1 = (bf16[2,1024,2048]{2,1,0:T(8,128)(2,1)}, bf16[2048,768]{1,0:T(8,128)(2,1)}, bf16[4,64,2048]{2,1,0:T(8,128)(2,1)}, bf16[4,16,128]{2,1,0:T(8,128...) custom-call(bf16[256,2048]{1,0:T(8,128)(2,1)} %tokens_ref.1, bf16[64,2048]{1,0:T(8,128)(2,1)} %refs_1_.1, ...), custom_call_target="tpu_custom_call" | custom-call | flops 100000000 | bytes 1024 | tf_op jit(solution)/shard_map/first_gather/pallas_call | solution.py:521
  145.4 0.7 fusion.18
  146.7 0.9 convert_bitcast_fusion
  147.9 0.6 pad.17.gain_ref
  148.5 3.7 fusion.2
  152.2 0.6 pad_maximum_fusion.1
  152.9 1.9 slice.67
  154.8 56.2 %project.1 = (f32[2048,256]{1,0:T(8,128)}, f32[2048,256]{1,0:T(8,128)}, bf16[2048,256]{1,0:T(8,128)(2,1)S(1)}, bf16[2048,256]{1,0:T(8,128)(2,1)S(1)}, bf16[2048,...) custom-call(bf16[2048,2048]{1,0:T(8,128)(2,1)} %bitcast.49, ...), custom_call_target="tpu_custom_call" | custom-call | flops 18000000 | bytes 1024 | tf_op jit(solution)/shard_map/project/pallas_call | solution.py:646
  211.1 13.7 %attend.1.attended_ref = bf16[2048,256]{1,0:T(8,128)(2,1)S(1)} custom-call(bf16[2048,256]{1,0:T(8,128)(2,1)S(1)} %get-tuple-element.71.q_ref, bf16[2048,256]{1,0:T(8,128)(2,1)S(1)} %get-tuple-element.72.k_ref, bf16[2048,256]{1,0:T(8,128)(2,1)S(1)} %get-tuple-element.73.v_ref, s32[2048,1]{1,0:T(8,128)S(1)} %bitcast.44, s32[2,1,1024]{2,1,0:T(1,128)S(1)} %pad_add_fusion.1.place_ref), custom_call_target="tpu_custom_call" | custom-call | flops 2147483648 | bytes 4194304 | tf_op jit(solution)/shard_map/attend/pallas_call | solution.py:75
  224.9 1.0 copy-done.4
  225.9 66.1 %attention_out.1 = (bf16[256,2048]{1,0:T(8,128)(2,1)}, f32[256,2048]{1,0:T(8,128)}, f32[256,2048]{1,0:T(8,128)}, bf16[2,1024,2048]{2,1,0:T(8,128)(2,1)}) custom-call(bf16[2048,256]{1,0:T(8,128)(2,1)} %copy-done.4, bf16[2048,2048]{1,0:T(8,128)(2,1)} %bitcast.47, bf16[256,2048]{1,0:T(8,128)(2,1)} %tokens_ref.1, f32[8,2048]{1,0:T(8,128)} %pad.17.gain_ref), custom_call_target="tpu_custom_call" | custom-call | flops 60000000 | bytes 1024 | tf_op jit(solution)/shard_map/attention_out/pallas_call | solution.py:863
  292.0 2.3 all-gather.6.cloned.1.call-done.wgu_ref.refs_1_
  294.9 0.6 pad.18.gain_ref
  295.6 24.8 %mix.1 = (bf16[2048,2048]{1,0:T(8,128)(2,1)}, bf16[2048,1024]{1,0:T(8,128)(2,1)}, bf16[1024,2048]{1,0:T(8,128)(2,1)}) custom-call(bf16[2048,2048]{1,0:T(8,128)(2,1)} %bitcast.51, bf16[2048,2048]{1,0:T(8,128)(2,1)} %all-gather.6.cloned.1.call-done.wgu_ref.refs_1_), custom_call_target="tpu_custom_call" | custom-call | flops 20000000 | bytes 1024 | tf_op jit(solution)/shard_map/mix/pallas_call | solution.py:1075
  320.4 2.3 all-gather.8.cloned.1.call-done.second_wd
  322.7 97.9 %feed_forward.1 = (f32[256,2048]{1,0:T(8,128)}, bf16[2048,2048]{1,0:T(8,128)(2,1)}, bf16[1024,2048]{1,0:T(8,128)(2,1)}, f32[8,2048]{1,0:T(8,128)}) custom-call(bf16[2048,1024]{1,0:T(8,128)(2,1)} %get-tuple-element.81.mixed_ref, bf16[1024,2048]{1,0:T(8,128)(2,1)} %get-tuple-element.82.turned_ref, bf16[2048,2048]{1,0:T(8,128)(2,1)} %get-tuple-element.83.gu_ref, ...), custom_call_target="tpu_custom_call" | custom-call | flops 80000000 | bytes 1024 | tf_op jit(solution)/shard_map/feed_forward/pallas_call | solution.py:1275
  420.6 1.1 copy-done.5
  421.8 46.7 %back_scatter.2 = f32[256,2048]{1,0:T(8,128)S(1)} custom-call(bf16[2048,2048]{1,0:T(8,128)(2,1)} %get-tuple-element.89.refs_0_, bf16[2048,2048]{1,0:T(8,128)(2,1)} %all-gather.6.cloned.1.call-done.wgu_ref.refs_1_, bf16[256,2048]{1,0:T(8,128)(2,1)S(1)} %copy-done.5), custom_call_target="tpu_custom_call" | custom-call | flops 50000000 | bytes 1024 | tf_op jit(solution)/shard_map/back_scatter/pallas_call | solution.py:1390
  468.4 21.3 %fusion.19 = bf16[2048,2048]{1,0:T(8,128)(2,1)} fusion(bf16[2048,2048]{1,0:T(8,128)(2,1)} %bitcast.52, bf16[2048,2048]{1,0:T(8,128)(2,1)S(1)} %copy-done.18), kind=kOutput, calls=%fused_computation.59 | convolution fusion | flops 17179869184 | bytes 25165824 | tf_op jit(solution)/shard_map/dot_general | solution.py:24
  489.7 5.9 reduce-scatter.4.cloned.1.call-done
  496.1 2.0 multiply_reduce_fusion.2
  498.0 0.8 slice.70
  498.9 1.1 convert_element_type.44
  500.0 1.6 convert_element_type.45
  501.6 0.6 multiply_reduce_fusion
  502.2 0.5 multiply_convert_fusion.x_ref
  502.7 40.3 %gather_rows.1 = bf16[2,1024,2048]{2,1,0:T(8,128)(2,1)S(1)} custom-call(bf16[256,2048]{1,0:T(8,128)(2,1)S(1)} %multiply_convert_fusion.x_ref), custom_call_target="tpu_custom_call" | custom-call | flops 40000000 | bytes 1024 | tf_op jit(solution)/shard_map/gather_rows/pallas_call | solution.py:331
  543.1 3.8 fusion.g_ref
  546.9 22.7 %attend_back.1 = (f32[2048,256]{1,0:T(8,128)}, f32[2048,256]{1,0:T(8,128)}, f32[2048,256]{1,0:T(8,128)}) custom-call(bf16[2048,256]{1,0:T(8,128)(2,1)S(1)} %copy-done.14, bf16[2048,256]{1,0:T(8,128)(2,1)S(1)} %copy-done.16, bf16[2048,256]{1,0:T(8,128)(2,1)S(1)} %copy-done.12, bf16[2048,256]{1,0:T(8,128)(2,1)S(1)} %fusion.g_ref, s32[2048,1]{1,0:T(8,128)S(1)} %bitcast.45, ...), custom_call_target="tpu_custom_call" | custom-call | flops 5368709120 | bytes 10485760 | tf_op jit(solution)/shard_map/attend_back/pallas_call | solution.py:96
  569.6 3.7 fusion.20.deal_ref
  573.4 32.5 %project_back.1 = (bf16[2048,768]{1,0:T(8,128)(2,1)}, f32[8,2048]{1,0:T(8,128)S(1)}, bf16[4,64,2048]{2,1,0:T(8,128)(2,1)S(1)}) custom-call(f32[2048,256]{1,0:T(8,128)} %get-tuple-element.92.dq_ref, f32[2048,256]{1,0:T(8,128)} %get-tuple-element.93.dk_ref, f32[2048,256]{1,0:T(8,128)} %get-tuple-element.94.dv_ref, f32[2048,256]{1,0:T(8,128)} %get-tuple-element.95.rq_ref, ...), custom_call_target="tpu_custom_call" | custom-call | flops 15000000 | bytes 1024 | tf_op jit(solution)/shard_map/project_back/pallas_call | solution.py:772
  606.0 10.3 %fusion.21 = bf16[2048,768]{1,0:T(8,128)(2,1)S(1)} fusion(bf16[2048,2048]{1,0:T(8,128)(2,1)} %bitcast.50, bf16[2048,768]{1,0:T(8,128)(2,1)} %get-tuple-element.110.refs_0_), kind=kOutput, calls=%fused_computation.61 | convolution fusion | flops 6442450944 | bytes 14680064 | tf_op jit(solution)/shard_map/dot_general | solution.py:24
  616.3 2.6 pad_maximum_fusion
  618.9 24.0 %reduce-scatter.6.cloned.1.call-done.x_ref = bf16[512,2048]{1,0:T(8,128)(2,1)} async-done(((bf16[2048,2048]{1,0:T(8,128)(2,1)}), bf16[512,2048]{1,0:T(8,128)(2,1)}) %reduce-scatter.6.cloned.1.call-update) | async-done | bytes 2097168 | tf_op jit(solution)/shard_map/reduce_scatter | solution.py:1467
  643.0 1.2 collective-permute-start
  644.2 1.6 copy-done.7
  645.8 26.3 %return_rows.2 = bf16[128,8192]{1,0:T(8,128)(2,1)S(1)} custom-call(bf16[512,2048]{1,0:T(8,128)(2,1)S(1)} %copy-done.7), custom_call_target="tpu_custom_call" | custom-call | flops 20000000 | bytes 1024 | tf_op jit(solution)/shard_map/return_rows/pallas_call | solution.py:954
  672.2 2.4 slice_convert_fusion
  674.6 2.5 collective-permute-start.1
  677.1 1.9 copy-done.6
  679.0 43.7 %back_scatter.3 = f32[256,2048]{1,0:T(8,128)S(1)} custom-call(bf16[2048,768]{1,0:T(8,128)(2,1)S(1)} %copy-done.6, bf16[2048,768]{1,0:T(8,128)(2,1)} %get-tuple-element.68.w_ref.refs_1_), custom_call_target="tpu_custom_call" | custom-call | flops 50000000 | bytes 1024 | tf_op jit(solution)/shard_map/back_scatter/pallas_call | solution.py:1390
  722.7 1.7 add.92
  724.4 0.5 slice_bitcast_fusion
  725.0 1.2 copy-done.10
  726.2 12.2 %return_rows.3 = bf16[256,2048]{1,0:T(8,128)(2,1)S(1)} custom-call(bf16[512,1024]{1,0:T(8,128)(2,1)S(1)} %copy-done.10), custom_call_target="tpu_custom_call" | custom-call | flops 20000000 | bytes 1024 | tf_op jit(solution)/shard_map/return_rows/pallas_call | solution.py:954
  738.4 1.4 slice_convert_fusion.2
  (87 shorter events, 2.9 us)
Async XLA Ops:
  7.2 137.7 %all-gather.4.cloned.1.call-start = ((), (), s32[]{:S(2)}) async-start(), calls=%async_computation.3 | async-start | bytes 3932160 | tf_op jit(solution)/shard_map/all_gather | solution.py:1464
  9.3 285.0 %all-gather.6.cloned.1.call-start = ((), (), s32[]{:S(2)}) async-start(), calls=%async_computation.4 | async-start | bytes 10485760 | tf_op jit(solution)/shard_map/all_gather | solution.py:1464
  10.7 134.3 %copy-start.21 = (s32[8,2]{0,1:T(2,128)S(1)}, s32[8,2]{0,1:T(2,128)}, u32[]{:S(2)}) copy-start(s32[8,2]{0,1:T(2,128)} %param.28) | copy-start | bytes 196
  144.9 177.8 %all-gather.8.cloned.1.call-start = ((), (), s32[]{:S(2)}) async-start(), calls=%async_computation.5 | async-start | bytes 1310720 | tf_op jit(solution)/shard_map/all_gather | solution.py:1464
  146.6 64.5 %copy-start.8 = (s32[1,2048]{0,1:T(8,128)}, s32[1,2048]{0,1:T(8,128)S(1)}, u32[]{:S(2)}) copy-start(s32[1,2048]{0,1:T(8,128)S(1)} %copy.53) | copy-start | bytes 24580
  152.9 58.2 %copy-start = (f32[2048,128]{1,0:T(8,128)}, f32[2048,128]{1,0:T(8,128)S(1)}, u32[]{:S(2)}) copy-start(f32[2048,128]{1,0:T(8,128)S(1)} %get-tuple-element.143.cos_ref) | copy-start | bytes 3145732
  152.9 58.2 %copy-start.2 = (f32[2048,128]{1,0:T(8,128)}, f32[2048,128]{1,0:T(8,128)S(1)}, u32[]{:S(2)}) copy-start(f32[2048,128]{1,0:T(8,128)S(1)} %get-tuple-element.144.sin_ref) | copy-start | bytes 3145732
  211.1 13.8 %copy-start.11 = (bf16[2048,256]{1,0:T(8,128)(2,1)}, bf16[2048,256]{1,0:T(8,128)(2,1)S(1)}, u32[]{:S(2)}) copy-start(bf16[2048,256]{1,0:T(8,128)(2,1)S(1)} %get-tuple-element.73.v_ref) | copy-start | bytes 3145732
  211.1 13.8 %copy-start.13 = (bf16[2048,256]{1,0:T(8,128)(2,1)}, bf16[2048,256]{1,0:T(8,128)(2,1)S(1)}, u32[]{:S(2)}) copy-start(bf16[2048,256]{1,0:T(8,128)(2,1)S(1)} %get-tuple-element.71.q_ref) | copy-start | bytes 3145732
  211.1 13.8 %copy-start.15 = (bf16[2048,256]{1,0:T(8,128)(2,1)}, bf16[2048,256]{1,0:T(8,128)(2,1)S(1)}, u32[]{:S(2)}) copy-start(bf16[2048,256]{1,0:T(8,128)(2,1)S(1)} %get-tuple-element.72.k_ref) | copy-start | bytes 3145732
  224.9 1.0 copy-start.4
  294.3 201.3 %reduce-scatter.4.cloned.1.call-start = ((), (), s32[]{:S(2)}) async-start(), calls=%async_computation.6 | async-start | bytes 5242880 | tf_op jit(solution)/shard_map/reduce_scatter | solution.py:1467
  420.5 1.2 copy-start.5
  420.6 222.4 %reduce-scatter.6.cloned.1.call-start = ((), (), s32[]{:S(2)}) async-start(), calls=%async_computation.7 | async-start | bytes 10485760 | tf_op jit(solution)/shard_map/reduce_scatter | solution.py:1467
  421.8 46.7 %copy-start.18 = (bf16[2048,2048]{1,0:T(8,128)(2,1)S(1)}, bf16[2048,2048]{1,0:T(8,128)(2,1)}, u32[]{:S(2)}) copy-start(bf16[2048,2048]{1,0:T(8,128)(2,1)} %get-tuple-element.89.refs_0_) | copy-start | bytes 25165828
  495.6 4.4 copy-start.20
  495.6 229.3 %reduce-scatter.8.cloned.1.call-start = ((), (), s32[]{:S(2)}) async-start(), calls=%async_computation.8 | async-start | bytes 5242880 | tf_op jit(solution)/shard_map/reduce_scatter | solution.py:1467
  496.1 2.8 copy-start.19
  498.9 2.7 copy-start.17
  543.1 3.8 copy-start.9
  543.1 3.8 copy-start.12
  543.1 3.8 copy-start.14
  543.1 3.8 copy-start.16
  569.6 3.8 copy-start.1
  569.6 3.8 copy-start.3
  643.0 31.6 %collective-permute-start = (f32[4,2048]{1,0:T(4,128)S(1)}, f32[4,2048]{1,0:T(4,128)S(1)}, u32[]{:S(2)}, u32[]{:S(2)}) collective-permute-start(f32[4,2048]{1,0:T(4,128)S(1)} %slice.73), channel_id=1, source_target_pairs={{0,8},{1,9},{2,10},{3,11},{4,12},{5,13},{6,14},{7,15},{8,0},{9,1},... | collective-permute-start | bytes 98312 | tf_op jit(solution)/shard_map/ppermute | solution.py:1458
  644.2 1.6 copy-start.7
  674.6 49.7 %collective-permute-start.1 = (f32[4,2048]{1,0:T(4,128)S(1)}, f32[4,2048]{1,0:T(4,128)S(1)}, u32[]{:S(2)}, u32[]{:S(2)}) collective-permute-start(f32[4,2048]{1,0:T(4,128)S(1)} %slice_add_fusion), channel_id=1, source_target_pairs={{0,16},{1,17},{2,18},{3,19},{4,20},{5,21},{6,22},{7,23},{8,24},{9,... | collective-permute-start | bytes 98312 | tf_op jit(solution)/shard_map/ppermute | solution.py:1458
  677.1 1.9 copy-start.6
  725.0 1.2 copy-start.10
Sparse Core Ops, SparseCore 0:
  10.2 125.3 all-gather.3
  145.0 149.2 all-gather.5
  296.5 26.1 all-gather.7
  420.7 74.8 reduce-scatter.3
  497.9 144.9 reduce-scatter.5
  645.2 78.1 reduce-scatter.7
